TPU v7x, 32 devices: a whole 2x2x4 slice. The times are simulated.
32 devices in a mesh: section: 4 (over x, core), seq: 2 (over y), expert: 4 (over z).
Axes of the slice: x: 2, y: 2, z: 4, core: 2. Of those that a mesh axis runs over, the one named last changes fastest.
Arguments:
- queries: bfloat16 [16, 192, 4096], P(('section', 'expert'), 'seq'), may hold values from -112 to 112
- dec_state: bfloat16 [16, 192, 4096], P(('section', 'expert'), 'seq'), may hold values from -6 to 6
- enc_kv: bfloat16 [2, 16, 320, 1024], P(None, ('section', 'expert'), 'seq'), may hold values from -15 to 15
- band_start: int32 [16, 2], P(('section', 'expert'), 'seq'), may hold values from 0 to 192, as said below
- norm_gain: float32 [4096], replicated, may hold values from 0.5 to 1.5
- route_ids: int32 [16, 192, 1], P(('section', 'expert'), 'seq'), may hold values from 0 to 3; in each aligned block of 96 rows (0 to 95, 96 to 191, ..., all dimensions but the last counted through in order) at most 24 rows name the same one
- keep: int32 [16, 192], P(('section', 'expert'), 'seq'), may hold values 0 or 1
- route_prob: float32 [16, 192], P(('section', 'expert'), 'seq'), may hold values from 0.25 to 1
- w_in: bfloat16 [4, 5120, 4096], P('seq', ('section', 'expert')), may hold values from -0.09375 to 0.09375
- w_out: bfloat16 [4, 5120, 4096], P('seq', ('section', 'expert')), may hold values from -0.078125 to 0.078125
Outputs:
- mixed: bfloat16 [16, 192, 4096], P(('section', 'expert'), 'seq')
Inputs may be any that keep to these rules, and one draw needn't show every extreme that they name: `band_start`: block q's band lies within encoder frames (q - 1) * 160 to (q + 2) * 160 - 1. `route_ids`: among the tokens of one device no expert is named more than 24 times.
All inputs are finite; a program needn't handle non-finite values. No bound on the sum of `keep` on one device may be relied on, other than what follows from the above.
Results may differ from a plain program's by a relative error of at most 0.011.
Values may be sent and summed in bfloat16 or wider, within the bound.
No kernel may reach another device: no remote copies, remote signals or barrier semaphores. Data moves between devices by JAX's collectives and lax.ppermute only.
A program may use at most 128 MiB of HBM per device.

v0:
```python
import functools
import math

import jax
import jax.numpy as jnp
from jax import lax
from jax.experimental import pallas as pl
from jax.experimental.pallas import tpu as pltpu
from jax.sharding import PartitionSpec as P

D = 4096
HEADS = 32
KV_HEADS = 8
DH = 128
WIN = 128
CORES = 2
VMEM_LIMIT = 16 * 1024 * 1024
EXPERT_VMEM = 8 * 1024 * 1024
SPAN = 1024


def attend_kernel(shards, blocks, rel_ref, q_ref, res_ref, gain_ref, *refs):
    kv_refs = refs[:shards]
    disp_refs = refs[shards : shards + blocks]
    state_ref = refs[shards + blocks]
    out_refs = refs[shards + blocks + 1 :]
    tok_count = q_ref.shape[0]
    groups = HEADS // KV_HEADS
    frames = kv_refs[0].shape[1]
    row = lax.broadcasted_iota(jnp.int32, (WIN, frames), 0)
    col = lax.broadcasted_iota(jnp.int32, (WIN, frames), 1)
    band = [None, None]
    for j in range(shards):
        pick = (col == row + rel_ref[j]).astype(jnp.bfloat16)
        for side in range(2):
            part = jnp.dot(pick, kv_refs[j][side], preferred_element_type=jnp.float32)
            band[side] = part if band[side] is None else band[side] + part
    keys_b = band[0].astype(jnp.bfloat16)
    values_b = band[1].astype(jnp.bfloat16)
    squares = jnp.zeros((tok_count, DH), jnp.float32)
    for g in range(KV_HEADS):
        key = keys_b[:, g * DH : (g + 1) * DH]
        value = values_b[:, g * DH : (g + 1) * DH]
        heads = [slice(h * DH, (h + 1) * DH) for h in range(g * groups, (g + 1) * groups)]
        grouped = jnp.concatenate([q_ref[:, cols] for cols in heads], axis=0)
        scores = lax.dot_general(
            grouped, key, (((1,), (1,)), ((), ())), preferred_element_type=jnp.float32
        ) * (1.0 / math.sqrt(DH))
        weights = jnp.exp(scores - jnp.max(scores, axis=-1, keepdims=True))
        total = jnp.sum(weights, axis=-1, keepdims=True)
        context = jnp.dot(
            weights.astype(jnp.bfloat16), value, preferred_element_type=jnp.float32
        ) / total
        for i, cols in enumerate(heads):
            state = res_ref[:, cols].astype(jnp.float32) + context[i * tok_count : (i + 1) * tok_count]
            state_ref[:, cols] = state
            squares = squares + state * state
    squares = jnp.sum(squares, axis=-1, keepdims=True)
    scale = lax.rsqrt(squares / D + 1e-06)
    normed = (state_ref[...] * scale * gain_ref[...]).astype(jnp.bfloat16)
    for disp_ref, out_ref in zip(disp_refs, out_refs):
        out_ref[...] = jnp.dot(
            disp_ref[...], normed, preferred_element_type=jnp.float32
        ).astype(jnp.bfloat16)


def attend(rel, query_rows, residual, gain, shards, dispatch):
    tok_count = query_rows.shape[0]
    vmem = pl.BlockSpec(memory_space=pltpu.VMEM)
    outs = [jax.ShapeDtypeStruct((tok_count, D), jnp.float32)]
    outs += [jax.ShapeDtypeStruct((d.shape[0], D), jnp.bfloat16) for d in dispatch]
    return pl.pallas_call(
        functools.partial(attend_kernel, len(shards), len(dispatch)),
        out_shape=outs,
        in_specs=[pl.BlockSpec(memory_space=pltpu.SMEM)]
        + [vmem] * (3 + len(shards) + len(dispatch)),
        out_specs=[vmem] * len(outs),
        compiler_params=pltpu.CompilerParams(vmem_limit_bytes=VMEM_LIMIT),
        cost_estimate=pl.CostEstimate(
            flops=6 * tok_count * D * WIN, bytes_accessed=6_000_000, transcendentals=HEADS * WIN * tok_count
        ),
        name="attend",
    )(rel, query_rows, residual, gain, *shards, *dispatch)


def expert_kernel(count, *refs):
    x_refs = refs[:count]
    in_ref, out_w_ref = refs[count], refs[count + 1]
    out_refs = refs[count + 2 :]
    joined = all(ref.shape[0] % 16 == 0 for ref in x_refs)
    groups = [x_refs] if joined else [[ref] for ref in x_refs]
    targets = [out_refs] if joined else [[ref] for ref in out_refs]
    for sources, outs in zip(groups, targets):
        rows_b = jnp.concatenate([ref[...] for ref in sources], axis=0)
        hidden = lax.dot_general(
            rows_b, in_ref[...], (((1,), (1,)), ((), ())), preferred_element_type=jnp.float32
        )
        hidden = jnp.maximum(hidden, 0.0).astype(jnp.bfloat16)
        for at in range(0, D, SPAN):
            cols = slice(at, at + SPAN)
            part = jnp.dot(
                hidden, out_w_ref[:, cols], preferred_element_type=jnp.float32
            ).astype(jnp.bfloat16)
            begin = 0
            for out_ref in outs:
                out_ref[:, cols] = part[begin : begin + out_ref.shape[0]]
                begin += out_ref.shape[0]


def pick_kernel(core_ref, in_ref, out_w_ref, pair_in_ref, pair_out_ref, sems):
    other = 1 - core_ref[0]
    copies = [
        pltpu.make_async_copy(in_ref.at[other], pair_in_ref, sems.at[0]),
        pltpu.make_async_copy(out_w_ref.at[other], pair_out_ref, sems.at[1]),
    ]
    for copy in copies:
        copy.start()
    for copy in copies:
        copy.wait()


def pool_kernel(core_ref, in_ref, out_w_ref, pair_in_ref, pair_out_ref, unit_in_ref, unit_out_ref, sems):
    core = core_ref[0]
    units = pair_in_ref.shape[0]
    copies = []
    sources = [
        (in_ref.at[core], pair_in_ref, unit_in_ref),
        (out_w_ref.at[core], pair_out_ref, unit_out_ref),
    ]
    for mine, other, target in sources:
        for at, source in enumerate((mine, other)):
            copies.append(
                pltpu.make_async_copy(
                    source, target.at[pl.ds(at * units, units)], sems.at[len(copies)]
                )
            )
    for copy in copies:
        copy.start()
    for copy in copies:
        copy.wait()


def staged(kernel, core, arrays, rows, copies, name):
    anywhere = pl.BlockSpec(memory_space=pl.ANY)
    vmem = pl.BlockSpec(memory_space=pltpu.VMEM)
    return pl.pallas_call(
        kernel,
        out_shape=[rows_like(rows), rows_like(rows)],
        in_specs=[pl.BlockSpec(memory_space=pltpu.SMEM)] + [anywhere] * len(arrays),
        out_specs=[vmem, vmem],
        scratch_shapes=[pltpu.SemaphoreType.DMA((copies,))],
        compiler_params=pltpu.CompilerParams(vmem_limit_bytes=EXPERT_VMEM),
        cost_estimate=pl.CostEstimate(
            flops=0, bytes_accessed=4 * rows * D * 2, transcendentals=0
        ),
        name=name,
    )(core, *arrays)


def expert_sums(parts, unit_in, unit_out):
    rows = [x.shape[0] for x in parts]
    units = unit_in.shape[0]
    vmem = pl.BlockSpec(memory_space=pltpu.VMEM)
    return pl.pallas_call(
        functools.partial(expert_kernel, len(parts)),
        out_shape=[jax.ShapeDtypeStruct((r, D), jnp.bfloat16) for r in rows],
        in_specs=[vmem] * (len(parts) + 2),
        out_specs=[vmem] * len(parts),
        compiler_params=pltpu.CompilerParams(vmem_limit_bytes=EXPERT_VMEM),
        cost_estimate=pl.CostEstimate(
            flops=4 * sum(rows) * units * D,
            bytes_accessed=4 * D * (units + sum(rows)),
            transcendentals=0,
        ),
        name="expert",
    )(*parts, unit_in, unit_out)


def local(kernel, outs, *args, name):
    vmem = pl.BlockSpec(memory_space=pltpu.VMEM)
    moved = sum(x.size * x.dtype.itemsize for x in (*args, *outs))
    return pl.pallas_call(
        kernel,
        out_shape=outs,
        in_specs=[vmem] * len(args),
        out_specs=[vmem] * len(outs),
        compiler_params=pltpu.CompilerParams(vmem_limit_bytes=EXPERT_VMEM),
        cost_estimate=pl.CostEstimate(
            flops=moved // 2, bytes_accessed=moved, transcendentals=0
        ),
        name=name,
    )(*args)


def rows_like(rows):
    return jax.ShapeDtypeStruct((rows, D), jnp.bfloat16)


def join_slots(stayed, crossed):
    capacity = stayed[0].shape[0]
    if capacity % 8:
        return [
            jnp.concatenate([rows, crossed[i * capacity : (i + 1) * capacity]], axis=0)
            for i, rows in enumerate(stayed)
        ]

    def kernel(*refs):
        count = len(stayed)
        other = refs[count][...].astype(jnp.float32)
        for i in range(count):
            pair = [refs[i][...].astype(jnp.float32), other[i * capacity : (i + 1) * capacity]]
            refs[count + 1 + i][...] = jnp.concatenate(pair, axis=0).astype(jnp.bfloat16)

    outs = [rows_like(2 * capacity) for _ in stayed]
    return local(kernel, outs, *stayed, crossed, name="join_slots")


def split_rows(fore_rows, rear_rows, cut):
    size = fore_rows.shape[0]

    def kernel(fore_ref, rear_ref, *out_refs):
        out_refs = list(out_refs)
        if cut > 0:
            out_refs.pop(0)[...] = fore_ref[:cut, :]
        if cut < size:
            out_refs.pop(0)[...] = rear_ref[cut:, :]

    outs = [rows_like(rows) for rows in (cut, size - cut) if rows > 0]
    return local(kernel, outs, fore_rows, rear_rows, name="split_rows")


def add_sums(ahead_part, behind_part, ahead, behind, cut):
    size = ahead_part.shape[0]

    def filled(rows, before):
        rows = rows.astype(jnp.float32)
        edges = [jnp.zeros((before, D), jnp.float32)] if before else []
        edges.append(rows)
        after = size - before - rows.shape[0]
        if after:
            edges.append(jnp.zeros((after, D), jnp.float32))
        return jnp.concatenate(edges, axis=0) if len(edges) > 1 else rows

    totals = [x for x in (ahead, behind) if x is not None]

    def kernel(*refs):
        refs = list(refs)
        sums = [refs.pop(0)[...].astype(jnp.float32), refs.pop(0)[...].astype(jnp.float32)]
        if ahead is not None:
            sums[0] = sums[0] + filled(refs.pop(0)[...], 0)
        if behind is not None:
            sums[1] = sums[1] + filled(refs.pop(0)[...], size - behind.shape[0])
        for out_ref, total in zip(refs, sums):
            out_ref[...] = total.astype(jnp.bfloat16)

    outs = [rows_like(size), rows_like(size)]
    return local(kernel, outs, ahead_part, behind_part, *totals, name="add_sums")


def finish_sums(own, ahead, behind):
    def kernel(own_ref, ahead_ref, behind_ref, out_ref):
        total = own_ref[...].astype(jnp.float32) + ahead_ref[...].astype(jnp.float32)
        out_ref[...] = (total + behind_ref[...].astype(jnp.float32)).astype(jnp.bfloat16)

    return local(kernel, [rows_like(own.shape[0])], own, ahead, behind, name="finish_sums")[0]


def combine_kernel(blocks, state_ref, scale_ref, *refs):
    total = None
    for j in range(blocks):
        part = lax.dot_general(
            refs[j][...],
            refs[blocks + j][...],
            (((1,), (0,)), ((), ())),
            preferred_element_type=jnp.float32,
        )
        total = part if total is None else total + part
    refs[2 * blocks][...] = (state_ref[...] + scale_ref[...] * total).astype(jnp.bfloat16)


def combine(state, scale, undo, returned):
    tok_count = state.shape[0]
    blocks = len(undo)
    vmem = pl.BlockSpec(memory_space=pltpu.VMEM)
    return pl.pallas_call(
        functools.partial(combine_kernel, blocks),
        out_shape=jax.ShapeDtypeStruct((tok_count, D), jnp.bfloat16),
        in_specs=[vmem] * (2 + 2 * blocks),
        out_specs=vmem,
        compiler_params=pltpu.CompilerParams(vmem_limit_bytes=EXPERT_VMEM),
        cost_estimate=pl.CostEstimate(
            flops=2 * tok_count * tok_count * D, bytes_accessed=4_000_000, transcendentals=0
        ),
        name="combine",
    )(state, scale, *undo, *returned)


def body(
    queries, dec_state, enc_kv, band_start, norm_gain, route_ids, keep, route_prob, w_in, w_out
):
    sections = lax.axis_size("section")
    seqs = lax.axis_size("seq")
    depth = lax.axis_size("expert")
    chips = sections // CORES
    assert chips == 2 and w_in.shape[0] == CORES
    s = lax.axis_index("section")
    q = lax.axis_index("seq")
    core = s % CORES

    def route(source_of):
        pairs = []
        for a in range(sections):
            for b in range(seqs):
                origin = source_of(b)
                if origin is not None:
                    pairs.append((((a - 1) % sections) * seqs + origin, a * seqs + b))
        return pairs

    frames = enc_kv.shape[2]
    block = enc_kv[:, 0]
    if seqs == 2:
        shards = [
            lax.ppermute(block, ("section", "seq"), route(lambda b: b)),
            lax.ppermute(block, ("section", "seq"), route(lambda b: 1 - b)),
        ]
        origins = [q, 1 - q]
    else:
        shards = [
            lax.ppermute(block, ("section", "seq"), route(lambda b: b)),
            lax.ppermute(block, ("section", "seq"), route(lambda b: b - 1 if b > 0 else None)),
            lax.ppermute(
                block, ("section", "seq"), route(lambda b: b + 1 if b < seqs - 1 else None)
            ),
        ]
        origins = [q, q - 1, q + 1]
    rel = jnp.stack([band_start[0, 0] - origin * frames for origin in origins]).astype(jnp.int32)

    def core_pairs():
        return [(a, a ^ 1) for a in range(sections)]

    core_at = core.astype(jnp.int32)[None]
    share = w_in.shape[1]
    pair_units = staged(pick_kernel, core_at, [w_in, w_out], share, 2, "pick_units")
    rel, pair_units = lax.optimization_barrier((rel, pair_units))
    pair_units = [lax.ppermute(rows, "section", core_pairs()) for rows in pair_units]

    experts_of = route_ids[0, :, 0]
    tok_count = experts_of.shape[0]
    expert_count = seqs * CORES
    capacity = max(2, tok_count // expert_count)
    one_hot = (experts_of[:, None] == jnp.arange(expert_count, dtype=jnp.int32)[None, :]).astype(
        jnp.int32
    )
    slot_of = jnp.sum((jnp.cumsum(one_hot, axis=0) - one_hot) * one_hot, axis=1)
    kept = keep[0] == 1
    turns = [(dq, dc) for dq in range(seqs) for dc in range(CORES)]
    slots = jnp.arange(capacity, dtype=jnp.int32)
    dispatch, undo = [], []
    block_slots = jnp.arange(CORES * capacity, dtype=jnp.int32)
    for dq, dc in turns:
        named = ((q + dq) % seqs) * CORES + (core ^ dc)
        code = jnp.where(kept & (experts_of == named), slot_of, -1)
        dispatch.append((slots[:, None] == code[None, :]).astype(jnp.bfloat16))
        code = jnp.where(code >= 0, code + dc * capacity, -1)
        undo.append((code[:, None] == block_slots[None, :]).astype(jnp.bfloat16))
    scale = (keep[0].astype(jnp.float32) * route_prob[0])[:, None]

    crossing = jnp.concatenate(
        [rows for (dq, dc), rows in zip(turns, dispatch) if dc == 1], axis=0
    )
    staying = [rows for (dq, dc), rows in zip(turns, dispatch) if dc == 0]
    rel, crossing, staying, undo, scale = lax.optimization_barrier(
        (rel, crossing, staying, undo, scale)
    )
    state, crossed, *stayed = attend(
        rel, queries[0], dec_state[0], norm_gain[None, :], shards, [crossing] + staying
    )

    def core_swap(rows):
        return lax.ppermute(rows, "section", core_pairs())

    def seq_move(rows, step):
        return lax.ppermute(rows, "seq", [(b, (b + step) % seqs) for b in range(seqs)])

    slot_blocks = join_slots(stayed, core_swap(crossed))
    moved = [seq_move(slot_blocks[dq], dq) for dq in range(1, seqs)]
    parts = [slot_blocks[0], moved[0] if seqs == 2 else jnp.concatenate(moved, axis=0)]

    unit_in, unit_out = staged(
        pool_kernel, core_at, [w_in, w_out, *pair_units], CORES * share, 4, "pool_units"
    )
    parts[1], unit_in, unit_out = lax.optimization_barrier((parts[1], unit_in, unit_out))

    cycle = [(0, z) for z in range(depth)] + [(1, z) for z in reversed(range(depth))]
    count = len(cycle)

    def hop(rows, step):
        pairs = []
        for c in range(CORES):
            ids = [(x * CORES + c) * depth + z for x, z in cycle]
            pairs += [(ids[i], ids[(i + step) % count]) for i in range(count)]
        return lax.ppermute(rows, ("section", "expert"), pairs)

    half = count // 2
    sizes = [rows.shape[0] for rows in parts]
    cut = [min(sizes[0], (sizes[0] // 2 + 15) // 16 * 16), sizes[1] // 2 // 16 * 16]
    fore = [[rows] for rows in parts]
    rear = [[rows] for rows in parts]
    sums = {}

    def after(key, rows):
        if key in sums:
            rows, sums[key] = lax.optimization_barrier((rows, sums[key]))
        return rows

    for k in range(1, half):
        for p in range(2):
            rows = after(k - 2, lax.optimization_barrier((fore[p][-1], rear[p][-1])))
            fore[p].append(hop(rows[0], 1))
            rear[p].append(hop(rows[1], -1))
        rows = [fore[0][k], fore[1][k], rear[0][k], rear[1][k]]
        sums[k] = expert_sums(rows, unit_in, unit_out)
    for p in (1, 0):
        rows = split_rows(*after(half - 2, (fore[p][-1], rear[p][-1])), cut[p])
        if cut[p] > 0:
            fore[p].append(hop(rows[0], 1))
        if cut[p] < sizes[p]:
            rear[p].append(hop(rows[-1], -1))
    ahead_part, behind_part = [{}, {}], [{}, {}]
    for p in (1, 0):
        rows = fore[p][half:] + rear[p][half:]
        if p == 1:
            rows = after(half - 1, rows)
        got = list(expert_sums(rows, unit_in, unit_out))
        if cut[p] > 0:
            ahead_part[p][half] = got.pop(0)
        if cut[p] < sizes[p]:
            behind_part[p][half] = got.pop(0)
    for k in range(1, half):
        for p in range(2):
            behind_part[p][k] = sums[k][p]
            ahead_part[p][k] = sums[k][2 + p]

    ahead, behind = [None, None], [None, None]
    for p in (1, 0):
        if half in ahead_part[p]:
            ahead[p] = hop(ahead_part[p][half], 1)
        if half in behind_part[p]:
            behind[p] = hop(behind_part[p][half], -1)
    for k in range(half - 1, 0, -1):
        for p in (1, 0):
            if k == half - 1 and p == 1:
                ahead[p], parts = lax.optimization_barrier((ahead[p], parts))
                sums["own"] = expert_sums(parts, unit_in, unit_out)
            totals = add_sums(
                ahead_part[p][k], behind_part[p][k], ahead[p], behind[p], cut[p]
            )
            if k == 1:
                totals = after("own", totals)
            ahead[p], behind[p] = hop(totals[0], 1), hop(totals[1], -1)
    done = [finish_sums(sums["own"][p], ahead[p], behind[p]) for p in range(2)]

    width = CORES * capacity
    if seqs == 2:
        far = [done[1]]
    else:
        far = [done[1][i * width : (i + 1) * width] for i in range(seqs - 1)]
    returned = []
    for dq, rows in enumerate([done[0]] + far):
        rows = seq_move(rows, -dq) if dq else rows
        returned += [rows, core_swap(rows)]
    return combine(state, scale, undo, returned)[None]


def solution(mesh):
    return jax.shard_map(
        body,
        mesh=mesh,
        in_specs=(
            P(("section", "expert"), "seq", None),
            P(("section", "expert"), "seq", None),
            P(None, ("section", "expert"), "seq", None),
            P(("section", "expert"), "seq"),
            P(),
            P(("section", "expert"), "seq", None),
            P(("section", "expert"), "seq"),
            P(("section", "expert"), "seq"),
            P("seq", ("section", "expert"), None),
            P("seq", ("section", "expert"), None),
        ),
        out_specs=P(("section", "expert"), "seq", None),
        check_vma=False,
    )
```

profile of v0, /device:TPU:1, one launch (start us, length us, event | category | flops | bytes accessed | tf_op | source)
XLA Modules:
  0.0 166.9 jit_solution(15663670308598949097)
XLA Ops:
  0.0 2.6 %collective-permute-start = (bf16[2,160,1024]{2,1,0:T(8,128)(2,1)}, bf16[2,160,1024]{2,1,0:T(8,128)(2,1)}, u32[]{:S(2)}, u32[]{:S(2)}) collective-permute-start(bf16[2,160,1024]{2,1,0:T(8,128)(2,1)} %bitcast.89), channel_id=1, source_target_pairs={{24,0},{28,4},{0,8},{4,12},{8,16},{12,20},{16,24},{20,28},{25,1},{... | collective-permute-start | bytes 1966088 | tf_op jit(solution)/shard_map/ppermute | solution.py:323
  4.3 2.5 %copy-done = bf16[2,320,4096]{2,1,0:T(8,128)(2,1)S(1)} copy-done((bf16[2,320,4096]{2,1,0:T(8,128)(2,1)S(1)}, bf16[2,320,4096]{2,1,0:T(8,128)(2,1)}, u32[]{:S(2)}) %copy-start) | copy-done | bytes 5242904
  9.3 2.7 %pick_units.1 = (bf16[320,4096]{1,0:T(8,128)(2,1)}, bf16[320,4096]{1,0:T(8,128)(2,1)}) custom-call(s32[1]{0:T(128)} %bitcast.3.core_ref, bf16[2,320,4096]{2,1,0:T(8,128)(2,1)S(1)} %copy-done, bf16[2,320,4096]{2,1,0:T(8,128)(2,1)S(1)} %copy-done.2), custom_call_target="tpu_custom_call" | custom-call | bytes 10485760 | tf_op jit(solution)/shard_map/pick_units/pallas_call | solution.py:146
  13.6 6.4 %collective-permute-done.1.refs_1_ = bf16[2,160,1024]{2,1,0:T(8,128)(2,1)} collective-permute-done((bf16[2,160,1024]{2,1,0:T(8,128)(2,1)}, bf16[2,160,1024]{2,1,0:T(8,128)(2,1)}, u32[]{:S(2)}, u32[]{:S(2)}) %collective-permute-start.1) | collective-permute-done | bytes 655392 | tf_op jit(solution)/shard_map/ppermute | solution.py:324
  21.1 3.2 %attend.1 = (f32[96,4096]{1,0:T(8,128)S(1)}, bf16[48,4096]{1,0:T(8,128)(2,1)S(1)}, bf16[24,4096]{1,0:T(8,128)(2,1)S(1)}, bf16[24,4096]{1,0:T(8,128)(2,1)S(1)}) custom-call(s32[2]{0:T(128)S(1)} %pad_add_fusion.rel_ref, bf16[96,4096]{1,0:T(8,128)(2,1)S(1)} %bitcast.84, bf16[96,4096]{1,0:T(8,128)(2,1)S(1)} %bitcast.85, f32[1,4096]{1,0:T(1,128)S(1)} %bitcast.86, ...), custom_call_target="tpu_custom_call" | custom-call | flops 301989888 | bytes 6000000 | tf_op jit(solution)/shard_map/attend/pallas_call | solution.py:72
  40.2 6.3 %collective-permute-done.6.refs_1_ = bf16[48,4096]{1,0:T(8,128)(2,1)S(1)} collective-permute-done((bf16[48,4096]{1,0:T(8,128)(2,1)S(1)}, bf16[48,4096]{1,0:T(8,128)(2,1)S(1)}, u32[]{:S(2)}, u32[]{:S(2)}) %collective-permute-start.6) | collective-permute-done | bytes 393248 | tf_op jit(solution)/shard_map/ppermute | solution.py:402
  49.0 6.0 %collective-permute-done.12.refs_0_ = bf16[48,4096]{1,0:T(8,128)(2,1)S(1)} collective-permute-done((bf16[48,4096]{1,0:T(8,128)(2,1)S(1)}, bf16[48,4096]{1,0:T(8,128)(2,1)S(1)}, u32[]{:S(2)}, u32[]{:S(2)}) %collective-permute-start.12) | collective-permute-done | bytes 393248 | tf_op jit(solution)/shard_map/ppermute | solution.py:402
  55.9 4.0 %expert.6 = (bf16[48,4096]{1,0:T(8,128)(2,1)S(1)}, bf16[48,4096]{1,0:T(8,128)(2,1)S(1)}, bf16[48,4096]{1,0:T(8,128)(2,1)S(1)}, bf16[48,4096]{1,0:T(8,128)(2,1)S(1)}) custom-call(bf16[48,4096]{1,0:T(8,128)(2,1)S(1)} %collective-permute-done.10.refs_0_, bf16[48,4096]{1,0:T(8,128)(2,1)S(1)} %collective-permute-done.6.refs_1_, ...), custom_call_target="tpu_custom_call" | custom-call | flops 2013265920 | bytes 13631488 | tf_op jit(solution)/shard_map/expert/pallas_call | solution.py:164
  59.9 3.4 %collective-permute-done.8.refs_1_ = bf16[48,4096]{1,0:T(8,128)(2,1)S(1)} collective-permute-done((bf16[48,4096]{1,0:T(8,128)(2,1)S(1)}, bf16[48,4096]{1,0:T(8,128)(2,1)S(1)}, u32[]{:S(2)}, u32[]{:S(2)}) %collective-permute-start.8) | collective-permute-done | bytes 393248 | tf_op jit(solution)/shard_map/ppermute | solution.py:402
  67.3 4.0 %expert.7 = (bf16[48,4096]{1,0:T(8,128)(2,1)S(1)}, bf16[48,4096]{1,0:T(8,128)(2,1)S(1)}, bf16[48,4096]{1,0:T(8,128)(2,1)S(1)}, bf16[48,4096]{1,0:T(8,128)(2,1)S(1)}) custom-call(bf16[48,4096]{1,0:T(8,128)(2,1)S(1)} %collective-permute-done.12.refs_0_, bf16[48,4096]{1,0:T(8,128)(2,1)S(1)} %collective-permute-done.8.refs_1_, ...), custom_call_target="tpu_custom_call" | custom-call | flops 2013265920 | bytes 13631488 | tf_op jit(solution)/shard_map/expert/pallas_call | solution.py:164
  75.4 5.8 %collective-permute-done.14.refs_0_.fore_ref = bf16[48,4096]{1,0:T(8,128)(2,1)S(1)} collective-permute-done((bf16[48,4096]{1,0:T(8,128)(2,1)S(1)}, bf16[48,4096]{1,0:T(8,128)(2,1)S(1)}, u32[]{:S(2)}, u32[]{:S(2)}) %collective-permute-start.14) | collective-permute-done | bytes 393248 | tf_op jit(solution)/shard_map/ppermute | solution.py:402
  82.2 4.0 %expert.8 = (bf16[48,4096]{1,0:T(8,128)(2,1)S(1)}, bf16[48,4096]{1,0:T(8,128)(2,1)S(1)}, bf16[48,4096]{1,0:T(8,128)(2,1)S(1)}, bf16[48,4096]{1,0:T(8,128)(2,1)S(1)}) custom-call(bf16[48,4096]{1,0:T(8,128)(2,1)S(1)} %collective-permute-done.14.refs_0_.fore_ref, bf16[48,4096]{1,0:T(8,128)(2,1)S(1)} %collective-permute-done.16.fore_ref.refs_1_, ...), custom_call_target="tpu_custom_call" | custom-call | flops 2013265920 | bytes 13631488 | tf_op jit(solution)/shard_map/expert/pallas_call | solution.py:164
  87.9 2.9 %expert.10 = (bf16[16,4096]{1,0:T(8,128)(2,1)S(1)}, bf16[32,4096]{1,0:T(8,128)(2,1)S(1)}) custom-call(bf16[16,4096]{1,0:T(8,128)(2,1)S(1)} %collective-permute-done.18.refs_0_, bf16[32,4096]{1,0:T(8,128)(2,1)S(1)} %collective-permute-done.19.refs_1_, bf16[640,4096]{1,0:T(8,128)(2,1)S(1)} %get-tuple-element.152.refs_4_.refs_2_, ...), custom_call_target="tpu_custom_call" | custom-call | flops 503316480 | bytes 11272192 | tf_op jit(solution)/shard_map/expert/pallas_call | solution.py:164
  93.9 3.9 %collective-permute-done.28.refs_2_ = bf16[16,4096]{1,0:T(8,128)(2,1)S(1)} collective-permute-done((bf16[16,4096]{1,0:T(8,128)(2,1)S(1)}, bf16[16,4096]{1,0:T(8,128)(2,1)S(1)}, u32[]{:S(2)}, u32[]{:S(2)}) %collective-permute-start.28) | collective-permute-done | bytes 131104 | tf_op jit(solution)/shard_map/ppermute | solution.py:402
  99.4 2.9 %expert.9 = (bf16[32,4096]{1,0:T(8,128)(2,1)S(1)}, bf16[16,4096]{1,0:T(8,128)(2,1)S(1)}) custom-call(bf16[32,4096]{1,0:T(8,128)(2,1)S(1)} %collective-permute-done.20.refs_0_, bf16[16,4096]{1,0:T(8,128)(2,1)S(1)} %collective-permute-done.21.refs_1_, bf16[640,4096]{1,0:T(8,128)(2,1)S(1)} %get-tuple-element.152.refs_4_.refs_2_, ...), custom_call_target="tpu_custom_call" | custom-call | flops 503316480 | bytes 11272192 | tf_op jit(solution)/shard_map/expert/pallas_call | solution.py:164
  103.8 4.9 %collective-permute-done.23.refs_3_ = bf16[16,4096]{1,0:T(8,128)(2,1)S(1)} collective-permute-done((bf16[16,4096]{1,0:T(8,128)(2,1)S(1)}, bf16[16,4096]{1,0:T(8,128)(2,1)S(1)}, u32[]{:S(2)}, u32[]{:S(2)}) %collective-permute-start.23) | collective-permute-done | bytes 131104 | tf_op jit(solution)/shard_map/ppermute | solution.py:402
  114.2 3.1 %expert.11 = (bf16[48,4096]{1,0:T(8,128)(2,1)S(1)}, bf16[48,4096]{1,0:T(8,128)(2,1)S(1)}) custom-call(bf16[48,4096]{1,0:T(8,128)(2,1)S(1)} %get-tuple-element.217.refs_0_, bf16[48,4096]{1,0:T(8,128)(2,1)S(1)} %collective-permute-done.3.refs_1_, bf16[640,4096]{1,0:T(8,128)(2,1)S(1)} %get-tuple-element.152.refs_4_.refs_2_, ...), custom_call_target="tpu_custom_call" | custom-call | flops 1006632960 | bytes 12058624 | tf_op jit(solution)/shard_map/expert/pallas_call | solution.py:164
  117.3 4.0 %collective-permute-done.24.refs_2_ = bf16[48,4096]{1,0:T(8,128)(2,1)S(1)} collective-permute-done((bf16[48,4096]{1,0:T(8,128)(2,1)S(1)}, bf16[48,4096]{1,0:T(8,128)(2,1)S(1)}, u32[]{:S(2)}, u32[]{:S(2)}) %collective-permute-start.24) | collective-permute-done | bytes 393248 | tf_op jit(solution)/shard_map/ppermute | solution.py:402
  123.0 3.9 %collective-permute-done.32.refs_2_ = bf16[48,4096]{1,0:T(8,128)(2,1)S(1)} collective-permute-done((bf16[48,4096]{1,0:T(8,128)(2,1)S(1)}, bf16[48,4096]{1,0:T(8,128)(2,1)S(1)}, u32[]{:S(2)}, u32[]{:S(2)}) %collective-permute-start.32) | collective-permute-done | bytes 393248 | tf_op jit(solution)/shard_map/ppermute | solution.py:402
  128.6 6.7 %collective-permute-done.26.refs_2_ = bf16[48,4096]{1,0:T(8,128)(2,1)S(1)} collective-permute-done((bf16[48,4096]{1,0:T(8,128)(2,1)S(1)}, bf16[48,4096]{1,0:T(8,128)(2,1)S(1)}, u32[]{:S(2)}, u32[]{:S(2)}) %collective-permute-start.26) | collective-permute-done | bytes 393248 | tf_op jit(solution)/shard_map/ppermute | solution.py:402
  137.0 6.7 %collective-permute-done.37.ahead_ref = bf16[48,4096]{1,0:T(8,128)(2,1)S(1)} collective-permute-done((bf16[48,4096]{1,0:T(8,128)(2,1)S(1)}, bf16[48,4096]{1,0:T(8,128)(2,1)S(1)}, u32[]{:S(2)}, u32[]{:S(2)}) %collective-permute-start.37) | collective-permute-done | bytes 393248 | tf_op jit(solution)/shard_map/ppermute | solution.py:402
  145.2 7.0 %collective-permute-done.34.ahead_ref = bf16[48,4096]{1,0:T(8,128)(2,1)S(1)} collective-permute-done((bf16[48,4096]{1,0:T(8,128)(2,1)S(1)}, bf16[48,4096]{1,0:T(8,128)(2,1)S(1)}, u32[]{:S(2)}, u32[]{:S(2)}) %collective-permute-start.34) | collective-permute-done | bytes 393248 | tf_op jit(solution)/shard_map/ppermute | solution.py:402
  152.3 8.7 %collective-permute-start.36 = (bf16[48,4096]{1,0:T(8,128)(2,1)S(1)}, bf16[48,4096]{1,0:T(8,128)(2,1)S(1)}, u32[]{:S(2)}, u32[]{:S(2)}) collective-permute-start(bf16[48,4096]{1,0:T(8,128)(2,1)S(1)} %finish_sums.2.refs_4_), channel_id=1, source_target_pairs={{0,8},{8,0},{16,24},{24,16},{1,9},{9,1},{17,25},{25,17},{2,10},{10... | collective-permute-start | bytes 1179656 | tf_op jit(solution)/shard_map/ppermute | solution.py:380
  161.0 2.7 %collective-permute-start.40 = (bf16[48,4096]{1,0:T(8,128)(2,1)S(1)}, bf16[48,4096]{1,0:T(8,128)(2,1)S(1)}, u32[]{:S(2)}, u32[]{:S(2)}) collective-permute-start(bf16[48,4096]{1,0:T(8,128)(2,1)S(1)} %collective-permute-done.39.refs_6_), channel_id=1, source_target_pairs={{0,8},{8,0},{16,24},{24,16},{1,9},{9,1},{17,25},{25,17},{2,10},{10... | collective-permute-start | bytes 1179656 | tf_op jit(solution)/shard_map/ppermute | solution.py:380
  (116 shorter events, 57.7 us)
Async XLA Ops:
  0.0 13.6 %collective-permute-start = (bf16[2,160,1024]{2,1,0:T(8,128)(2,1)}, bf16[2,160,1024]{2,1,0:T(8,128)(2,1)}, u32[]{:S(2)}, u32[]{:S(2)}) collective-permute-start(bf16[2,160,1024]{2,1,0:T(8,128)(2,1)} %bitcast.89), channel_id=1, source_target_pairs={{24,0},{28,4},{0,8},{4,12},{8,16},{12,20},{16,24},{20,28},{25,1},{... | collective-permute-start | bytes 1966088 | tf_op jit(solution)/shard_map/ppermute | solution.py:323
  2.6 17.3 %collective-permute-start.1 = (bf16[2,160,1024]{2,1,0:T(8,128)(2,1)}, bf16[2,160,1024]{2,1,0:T(8,128)(2,1)}, u32[]{:S(2)}, u32[]{:S(2)}) collective-permute-start(bf16[2,160,1024]{2,1,0:T(8,128)(2,1)} %bitcast.90), channel_id=1, source_target_pairs={{28,0},{24,4},{4,8},{0,12},{12,16},{8,20},{20,24},{16,28},{29,1},{... | collective-permute-start | bytes 1966088 | tf_op jit(solution)/shard_map/ppermute | solution.py:324
  12.0 16.9 %collective-permute-start.4 = (bf16[320,4096]{1,0:T(8,128)(2,1)}, bf16[320,4096]{1,0:T(8,128)(2,1)S(1)}, u32[]{:S(2)}, u32[]{:S(2)}) collective-permute-start(bf16[320,4096]{1,0:T(8,128)(2,1)} %get-tuple-element.134), channel_id=1, source_target_pairs={{0,8},{8,0},{16,24},{24,16},{1,9},{9,1},{17,25},{25,17},{2,10},{10... | collective-permute-start | bytes 7864328 | tf_op jit(solution)/shard_map/ppermute | solution.py:345
  12.8 16.2 %collective-permute-start.5 = (bf16[320,4096]{1,0:T(8,128)(2,1)}, bf16[320,4096]{1,0:T(8,128)(2,1)}, u32[]{:S(2)}, u32[]{:S(2)}) collective-permute-start(bf16[320,4096]{1,0:T(8,128)(2,1)} %get-tuple-element.135), channel_id=1, source_target_pairs={{0,8},{8,0},{16,24},{24,16},{1,9},{9,1},{17,25},{25,17},{2,10},{10... | collective-permute-start | bytes 7864328 | tf_op jit(solution)/shard_map/ppermute | solution.py:345
  38.7 16.2 %collective-permute-start.12 = (bf16[48,4096]{1,0:T(8,128)(2,1)S(1)}, bf16[48,4096]{1,0:T(8,128)(2,1)S(1)}, u32[]{:S(2)}, u32[]{:S(2)}) collective-permute-start(bf16[48,4096]{1,0:T(8,128)(2,1)S(1)} %collective-permute-done.10.refs_0_), channel_id=1, source_target_pairs={{0,1},{1,2},{2,3},{3,19},{19,18},{18,17},{17,16},{16,0},{8,9},{9,1... | collective-permute-start | bytes 1179656 | tf_op jit(solution)/shard_map/ppermute | solution.py:402
  40.0 15.9 %collective-permute-start.13 = (bf16[48,4096]{1,0:T(8,128)(2,1)S(1)}, bf16[48,4096]{1,0:T(8,128)(2,1)S(1)}, u32[]{:S(2)}, u32[]{:S(2)}) collective-permute-start(bf16[48,4096]{1,0:T(8,128)(2,1)S(1)} %collective-permute-done.11.refs_2_), channel_id=1, source_target_pairs={{0,16},{1,0},{2,1},{3,2},{19,3},{18,19},{17,18},{16,17},{8,24},{9,... | collective-permute-start | bytes 1179656 | tf_op jit(solution)/shard_map/ppermute | solution.py:402
  47.5 15.8 %collective-permute-start.8 = (bf16[48,4096]{1,0:T(8,128)(2,1)S(1)}, bf16[48,4096]{1,0:T(8,128)(2,1)S(1)}, u32[]{:S(2)}, u32[]{:S(2)}) collective-permute-start(bf16[48,4096]{1,0:T(8,128)(2,1)S(1)} %collective-permute-done.6.refs_1_), channel_id=1, source_target_pairs={{0,1},{1,2},{2,3},{3,19},{19,18},{18,17},{17,16},{16,0},{8,9},{9,1... | collective-permute-start | bytes 1179656 | tf_op jit(solution)/shard_map/ppermute | solution.py:402
  48.8 15.6 %collective-permute-start.9 = (bf16[48,4096]{1,0:T(8,128)(2,1)S(1)}, bf16[48,4096]{1,0:T(8,128)(2,1)S(1)}, u32[]{:S(2)}, u32[]{:S(2)}) collective-permute-start(bf16[48,4096]{1,0:T(8,128)(2,1)S(1)} %collective-permute-done.7.refs_3_), channel_id=1, source_target_pairs={{0,16},{1,0},{2,1},{3,2},{19,3},{18,19},{17,18},{16,17},{8,24},{9,... | collective-permute-start | bytes 1179656 | tf_op jit(solution)/shard_map/ppermute | solution.py:402
  65.8 15.4 %collective-permute-start.14 = (bf16[48,4096]{1,0:T(8,128)(2,1)S(1)}, bf16[48,4096]{1,0:T(8,128)(2,1)S(1)}, u32[]{:S(2)}, u32[]{:S(2)}) collective-permute-start(bf16[48,4096]{1,0:T(8,128)(2,1)S(1)} %collective-permute-done.12.refs_0_), channel_id=1, source_target_pairs={{0,1},{1,2},{2,3},{3,19},{19,18},{18,17},{17,16},{16,0},{8,9},{9,1... | collective-permute-start | bytes 1179656 | tf_op jit(solution)/shard_map/ppermute | solution.py:402
  67.1 15.1 %collective-permute-start.15 = (bf16[48,4096]{1,0:T(8,128)(2,1)S(1)}, bf16[48,4096]{1,0:T(8,128)(2,1)S(1)}, u32[]{:S(2)}, u32[]{:S(2)}) collective-permute-start(bf16[48,4096]{1,0:T(8,128)(2,1)S(1)} %collective-permute-done.13.refs_2_), channel_id=1, source_target_pairs={{0,16},{1,0},{2,1},{3,2},{19,3},{18,19},{17,18},{16,17},{8,24},{9,... | collective-permute-start | bytes 1179656 | tf_op jit(solution)/shard_map/ppermute | solution.py:402
  73.8 14.0 %collective-permute-start.19 = (bf16[32,4096]{1,0:T(8,128)(2,1)S(1)}, bf16[32,4096]{1,0:T(8,128)(2,1)S(1)}, u32[]{:S(2)}, u32[]{:S(2)}) collective-permute-start(bf16[32,4096]{1,0:T(8,128)(2,1)S(1)} %get-tuple-element.181), channel_id=1, source_target_pairs={{0,16},{1,0},{2,1},{3,2},{19,3},{18,19},{17,18},{16,17},{8,24},{9,... | collective-permute-start | bytes 786440 | tf_op jit(solution)/shard_map/ppermute | solution.py:402
  74.1 12.2 %collective-permute-start.18 = (bf16[16,4096]{1,0:T(8,128)(2,1)S(1)}, bf16[16,4096]{1,0:T(8,128)(2,1)S(1)}, u32[]{:S(2)}, u32[]{:S(2)}) collective-permute-start(bf16[16,4096]{1,0:T(8,128)(2,1)S(1)} %get-tuple-element.180), channel_id=1, source_target_pairs={{0,1},{1,2},{2,3},{3,19},{19,18},{18,17},{17,16},{16,0},{8,9},{9,1... | collective-permute-start | bytes 393224 | tf_op jit(solution)/shard_map/ppermute | solution.py:402
  97.8 14.7 %collective-permute-start.30 = (bf16[48,4096]{1,0:T(8,128)(2,1)S(1)}, bf16[48,4096]{1,0:T(8,128)(2,1)S(1)}, u32[]{:S(2)}, u32[]{:S(2)}) collective-permute-start(bf16[48,4096]{1,0:T(8,128)(2,1)S(1)} %get-tuple-element.211), channel_id=1, source_target_pairs={{0,1},{1,2},{2,3},{3,19},{19,18},{18,17},{17,16},{16,0},{8,9},{9,1... | collective-permute-start | bytes 1179656 | tf_op jit(solution)/shard_map/ppermute | solution.py:402
  99.2 13.4 %collective-permute-start.31 = (bf16[48,4096]{1,0:T(8,128)(2,1)S(1)}, bf16[48,4096]{1,0:T(8,128)(2,1)S(1)}, u32[]{:S(2)}, u32[]{:S(2)}) collective-permute-start(bf16[48,4096]{1,0:T(8,128)(2,1)S(1)} %get-tuple-element.212), channel_id=1, source_target_pairs={{0,16},{1,0},{2,1},{3,2},{19,3},{18,19},{17,18},{16,17},{8,24},{9,... | collective-permute-start | bytes 1179656 | tf_op jit(solution)/shard_map/ppermute | solution.py:402
  112.7 14.2 %collective-permute-start.32 = (bf16[48,4096]{1,0:T(8,128)(2,1)S(1)}, bf16[48,4096]{1,0:T(8,128)(2,1)S(1)}, u32[]{:S(2)}, u32[]{:S(2)}) collective-permute-start(bf16[48,4096]{1,0:T(8,128)(2,1)S(1)} %get-tuple-element.213), channel_id=1, source_target_pairs={{0,1},{1,2},{2,3},{3,19},{19,18},{18,17},{17,16},{16,0},{8,9},{9,1... | collective-permute-start | bytes 1179656 | tf_op jit(solution)/shard_map/ppermute | solution.py:402
  114.2 12.7 %collective-permute-start.33 = (bf16[48,4096]{1,0:T(8,128)(2,1)S(1)}, bf16[48,4096]{1,0:T(8,128)(2,1)S(1)}, u32[]{:S(2)}, u32[]{:S(2)}) collective-permute-start(bf16[48,4096]{1,0:T(8,128)(2,1)S(1)} %get-tuple-element.214), channel_id=1, source_target_pairs={{0,16},{1,0},{2,1},{3,2},{19,3},{18,19},{17,18},{16,17},{8,24},{9,... | collective-permute-start | bytes 1179656 | tf_op jit(solution)/shard_map/ppermute | solution.py:402
  121.5 13.8 %collective-permute-start.26 = (bf16[48,4096]{1,0:T(8,128)(2,1)S(1)}, bf16[48,4096]{1,0:T(8,128)(2,1)S(1)}, u32[]{:S(2)}, u32[]{:S(2)}) collective-permute-start(bf16[48,4096]{1,0:T(8,128)(2,1)S(1)} %get-tuple-element.196), channel_id=1, source_target_pairs={{0,1},{1,2},{2,3},{3,19},{19,18},{18,17},{17,16},{16,0},{8,9},{9,1... | collective-permute-start | bytes 1179656 | tf_op jit(solution)/shard_map/ppermute | solution.py:402
  122.8 12.5 %collective-permute-start.27 = (bf16[48,4096]{1,0:T(8,128)(2,1)S(1)}, bf16[48,4096]{1,0:T(8,128)(2,1)S(1)}, u32[]{:S(2)}, u32[]{:S(2)}) collective-permute-start(bf16[48,4096]{1,0:T(8,128)(2,1)S(1)} %get-tuple-element.197), channel_id=1, source_target_pairs={{0,16},{1,0},{2,1},{3,2},{19,3},{18,19},{17,18},{16,17},{8,24},{9,... | collective-permute-start | bytes 1179656 | tf_op jit(solution)/shard_map/ppermute | solution.py:402
  127.1 16.7 %collective-permute-start.37 = (bf16[48,4096]{1,0:T(8,128)(2,1)S(1)}, bf16[48,4096]{1,0:T(8,128)(2,1)S(1)}, u32[]{:S(2)}, u32[]{:S(2)}) collective-permute-start(bf16[48,4096]{1,0:T(8,128)(2,1)S(1)} %get-tuple-element.227), channel_id=1, source_target_pairs={{0,1},{1,2},{2,3},{3,19},{19,18},{18,17},{17,16},{16,0},{8,9},{9,1... | collective-permute-start | bytes 1179656 | tf_op jit(solution)/shard_map/ppermute | solution.py:402
  128.5 15.3 %collective-permute-start.38 = (bf16[48,4096]{1,0:T(8,128)(2,1)S(1)}, bf16[48,4096]{1,0:T(8,128)(2,1)S(1)}, u32[]{:S(2)}, u32[]{:S(2)}) collective-permute-start(bf16[48,4096]{1,0:T(8,128)(2,1)S(1)} %get-tuple-element.228), channel_id=1, source_target_pairs={{0,16},{1,0},{2,1},{3,2},{19,3},{18,19},{17,18},{16,17},{8,24},{9,... | collective-permute-start | bytes 1179656 | tf_op jit(solution)/shard_map/ppermute | solution.py:402
  135.5 16.7 %collective-permute-start.34 = (bf16[48,4096]{1,0:T(8,128)(2,1)S(1)}, bf16[48,4096]{1,0:T(8,128)(2,1)S(1)}, u32[]{:S(2)}, u32[]{:S(2)}) collective-permute-start(bf16[48,4096]{1,0:T(8,128)(2,1)S(1)} %get-tuple-element.224), channel_id=1, source_target_pairs={{0,1},{1,2},{2,3},{3,19},{19,18},{18,17},{17,16},{16,0},{8,9},{9,1... | collective-permute-start | bytes 1179656 | tf_op jit(solution)/shard_map/ppermute | solution.py:402
  136.9 15.3 %collective-permute-start.35 = (bf16[48,4096]{1,0:T(8,128)(2,1)S(1)}, bf16[48,4096]{1,0:T(8,128)(2,1)S(1)}, u32[]{:S(2)}, u32[]{:S(2)}) collective-permute-start(bf16[48,4096]{1,0:T(8,128)(2,1)S(1)} %get-tuple-element.225), channel_id=1, source_target_pairs={{0,16},{1,0},{2,1},{3,2},{19,3},{18,19},{17,18},{16,17},{8,24},{9,... | collective-permute-start | bytes 1179656 | tf_op jit(solution)/shard_map/ppermute | solution.py:402
  143.9 17.1 %collective-permute-start.39 = (bf16[48,4096]{1,0:T(8,128)(2,1)S(1)}, bf16[48,4096]{1,0:T(8,128)(2,1)S(1)}, u32[]{:S(2)}, u32[]{:S(2)}) collective-permute-start(bf16[48,4096]{1,0:T(8,128)(2,1)S(1)} %finish_sums.3), channel_id=1, source_target_pairs={{0,4},{4,0},{1,5},{5,1},{2,6},{6,2},{3,7},{7,3},{8,12},{12,8},{9,1... | collective-permute-start | bytes 1179656 | tf_op jit(solution)/shard_map/ppermute | solution.py:383
  152.3 11.5 %collective-permute-start.36 = (bf16[48,4096]{1,0:T(8,128)(2,1)S(1)}, bf16[48,4096]{1,0:T(8,128)(2,1)S(1)}, u32[]{:S(2)}, u32[]{:S(2)}) collective-permute-start(bf16[48,4096]{1,0:T(8,128)(2,1)S(1)} %finish_sums.2.refs_4_), channel_id=1, source_target_pairs={{0,8},{8,0},{16,24},{24,16},{1,9},{9,1},{17,25},{25,17},{2,10},{10... | collective-permute-start | bytes 1179656 | tf_op jit(solution)/shard_map/ppermute | solution.py:380
  (29 other events, 225.9 us)
where the time goes:
time: 168 us; the launch traced here: 167 us
  waiting for transfers between devices  79.2 us (47%)
  starting transfers between devices  42.5 us (25%)
  Pallas kernels  32.3 us (19%)
  local copies, waits for them, and re-layouts  11.2 us (7%)
    ppermute x32, waiting for transfers between devices, hop(): return lax.ppermute(rows, ('section', 'expert'), pairs)  69.3 us
    ppermute x32, starting transfers between devices, hop(): return lax.ppermute(rows, ('section', 'expert'), pairs)  24 us
    pallas_call x6, Pallas kernels, expert_sums(): pl.pallas_call(functools.partial(expert_kernel, len(parts)), out_shape=[j...  21 us
    ppermute x3, starting transfers between devices, core_swap(): return lax.ppermute(rows, 'section', core_pairs())  11.4 us
    unnamed x24, local copies, waits for them, and re-layouts  11.1 us
    ppermute x1, waiting for transfers between devices, body(): lax.ppermute(block, ('section', 'seq'), route(lambda b: 1 - b))  6.36 us
    pallas_call x2, Pallas kernels, staged(): pl.pallas_call(kernel, out_shape=[rows_like(rows), rows_like(rows)], in_s...  5.02 us
  transfers between devices with their start and end apart: 41, of which 24 were waited for; matrix products, arithmetic and copies ran while one was open for 0% of the time, Pallas kernels for 17%

commit v1 on v0

--- a/solution.py
+++ b/solution.py
@@ -87,23 +87,28 @@
     x_refs = refs[:count]
     in_ref, out_w_ref = refs[count], refs[count + 1]
     out_refs = refs[count + 2 :]
-    joined = all(ref.shape[0] % 16 == 0 for ref in x_refs)
+    joined = all(ref.shape[0] % 8 == 0 for ref in x_refs)
     groups = [x_refs] if joined else [[ref] for ref in x_refs]
     targets = [out_refs] if joined else [[ref] for ref in out_refs]
     for sources, outs in zip(groups, targets):
-        rows_b = jnp.concatenate([ref[...] for ref in sources], axis=0)
+        if len(sources) == 1:
+            rows_b = sources[0][...]
+        elif all(ref.shape[0] % 16 == 0 for ref in sources):
+            rows_b = jnp.concatenate([ref[...] for ref in sources], axis=0)
+        else:
+            rows_b = [ref[...].astype(jnp.float32) for ref in sources]
+            rows_b = jnp.concatenate(rows_b, axis=0).astype(jnp.bfloat16)
         hidden = lax.dot_general(
             rows_b, in_ref[...], (((1,), (1,)), ((), ())), preferred_element_type=jnp.float32
         )
         hidden = jnp.maximum(hidden, 0.0).astype(jnp.bfloat16)
         for at in range(0, D, SPAN):
             cols = slice(at, at + SPAN)
-            part = jnp.dot(
-                hidden, out_w_ref[:, cols], preferred_element_type=jnp.float32
-            ).astype(jnp.bfloat16)
+            part = jnp.dot(hidden, out_w_ref[:, cols], preferred_element_type=jnp.float32)
             begin = 0
             for out_ref in outs:
-                out_ref[:, cols] = part[begin : begin + out_ref.shape[0]]
+                rows = part[begin : begin + out_ref.shape[0]]
+                out_ref[:, cols] = rows.astype(jnp.bfloat16)
                 begin += out_ref.shape[0]
 
 
@@ -167,11 +172,7 @@
         in_specs=[vmem] * (len(parts) + 2),
         out_specs=[vmem] * len(parts),
         compiler_params=pltpu.CompilerParams(vmem_limit_bytes=EXPERT_VMEM),
-        cost_estimate=pl.CostEstimate(
-            flops=4 * sum(rows) * units * D,
-            bytes_accessed=4 * D * (units + sum(rows)),
-            transcendentals=0,
-        ),
+        cost_estimate=pl.CostEstimate(flops=1, bytes_accessed=1, transcendentals=0),
         name="expert",
     )(*parts, unit_in, unit_out)
 
@@ -221,9 +222,11 @@
     def kernel(fore_ref, rear_ref, *out_refs):
         out_refs = list(out_refs)
         if cut > 0:
-            out_refs.pop(0)[...] = fore_ref[:cut, :]
+            rows = fore_ref[...].astype(jnp.float32)[:cut]
+            out_refs.pop(0)[...] = rows.astype(jnp.bfloat16)
         if cut < size:
-            out_refs.pop(0)[...] = rear_ref[cut:, :]
+            rows = rear_ref[...].astype(jnp.float32)[cut:]
+            out_refs.pop(0)[...] = rows.astype(jnp.bfloat16)
 
     outs = [rows_like(rows) for rows in (cut, size - cut) if rows > 0]
     return local(kernel, outs, fore_rows, rear_rows, name="split_rows")
@@ -403,62 +406,73 @@
 
     half = count // 2
     sizes = [rows.shape[0] for rows in parts]
-    cut = [min(sizes[0], (sizes[0] // 2 + 15) // 16 * 16), sizes[1] // 2 // 16 * 16]
+    cut = [
+        rows // 2 if rows // 2 % 8 == 0 else rows * (1 - p) for p, rows in enumerate(sizes)
+    ]
     fore = [[rows] for rows in parts]
     rear = [[rows] for rows in parts]
     sums = {}
 
-    def after(key, rows):
-        if key in sums:
-            rows, sums[key] = lax.optimization_barrier((rows, sums[key]))
+    def after(keys, rows):
+        for key in keys:
+            if key in sums:
+                rows, sums[key] = lax.optimization_barrier((rows, sums[key]))
         return rows
 
     for k in range(1, half):
         for p in range(2):
-            rows = after(k - 2, lax.optimization_barrier((fore[p][-1], rear[p][-1])))
+            rows = lax.optimization_barrier((fore[p][-1], rear[p][-1]))
+            if p == 1:
+                rows = after([(0, k - 1), (1, k - 2)], rows)
             fore[p].append(hop(rows[0], 1))
             rear[p].append(hop(rows[1], -1))
-        rows = [fore[0][k], fore[1][k], rear[0][k], rear[1][k]]
-        sums[k] = expert_sums(rows, unit_in, unit_out)
-    for p in (1, 0):
-        rows = split_rows(*after(half - 2, (fore[p][-1], rear[p][-1])), cut[p])
+            if k < half - 1:
+                sums[p, k] = expert_sums([fore[p][k], rear[p][k]], unit_in, unit_out)
+    rows = (fore[0][-1], rear[0][-1])
+    lead = split_rows(*rows, cut[0])
+    rows, lead = lax.optimization_barrier((rows, lead))
+    sums[0, half - 1] = expert_sums(rows, unit_in, unit_out)
+    rows = (fore[1][-1], rear[1][-1])
+    follow = split_rows(*after([(0, half - 1), (1, half - 2)], rows), cut[1])
+    rows, follow = lax.optimization_barrier((rows, follow))
+    sums[1, half - 1] = expert_sums(rows, unit_in, unit_out)
+    ahead_part, behind_part = [{}, {}], [{}, {}]
+    for p, rows in enumerate((lead, follow)):
+        got = []
         if cut[p] > 0:
-            fore[p].append(hop(rows[0], 1))
+            got.append(hop(rows[0], 1))
         if cut[p] < sizes[p]:
-            rear[p].append(hop(rows[-1], -1))
-    ahead_part, behind_part = [{}, {}], [{}, {}]
-    for p in (1, 0):
-        rows = fore[p][half:] + rear[p][half:]
-        if p == 1:
-            rows = after(half - 1, rows)
-        got = list(expert_sums(rows, unit_in, unit_out))
+            got.append(hop(rows[-1], -1))
+        if p == 0:
+            got = after([(1, half - 1)], got)
+        sums[p, half] = expert_sums(got, unit_in, unit_out)
+    for p, k in list(sums):
+        got = list(sums[p, k])
+        if k < half:
+            behind_part[p][k], ahead_part[p][k] = got
+            continue
         if cut[p] > 0:
             ahead_part[p][half] = got.pop(0)
         if cut[p] < sizes[p]:
             behind_part[p][half] = got.pop(0)
-    for k in range(1, half):
-        for p in range(2):
-            behind_part[p][k] = sums[k][p]
-            ahead_part[p][k] = sums[k][2 + p]
 
     ahead, behind = [None, None], [None, None]
-    for p in (1, 0):
+    for p in range(2):
         if half in ahead_part[p]:
             ahead[p] = hop(ahead_part[p][half], 1)
         if half in behind_part[p]:
             behind[p] = hop(behind_part[p][half], -1)
+    (ahead[0], behind[0]), parts = lax.optimization_barrier(((ahead[0], behind[0]), parts))
+    own = expert_sums(parts, unit_in, unit_out)
     for k in range(half - 1, 0, -1):
         for p in (1, 0):
-            if k == half - 1 and p == 1:
-                ahead[p], parts = lax.optimization_barrier((ahead[p], parts))
-                sums["own"] = expert_sums(parts, unit_in, unit_out)
             totals = add_sums(
                 ahead_part[p][k], behind_part[p][k], ahead[p], behind[p], cut[p]
             )
-            if k == 1:
-                totals = after("own", totals)
+            if k == 1 and p == 1:
+                totals, own = lax.optimization_barrier((totals, own))
             ahead[p], behind[p] = hop(totals[0], 1), hop(totals[1], -1)
-    done = [finish_sums(sums["own"][p], ahead[p], behind[p]) for p in range(2)]
+    done = [finish_sums(own[p], ahead[p], behind[p]) for p in range(2)]
 
     width = CORES * capacity
     if seqs == 2:

time: 168 us -> 165 us (0.982)
  waiting for transfers between devices: 79.2 us -> 69.7 us
  Pallas kernels: 32.3 us -> 38.9 us
    ppermute x32, waiting for transfers between devices: 69.3 us -> 59.8 us  [hop(): return lax.ppermute(rows, ('section', 'expert'), pairs)]
    pallas_call x6 -> x9, Pallas kernels: 21 us -> 27.5 us  [expert_sums(): pl.pallas_call(functools.partial(expert_kernel, len(parts)), out_shape=[j...]
  transfers between devices with their start and end apart: 41 -> 41, of which waited for: 24 -> 29; matrix products, arithmetic and copies ran while one was open for 0% -> 0% of each run, Pallas kernels for 17% -> 23%
where the time goes in v1:
time: 165 us; the launch traced here: 164 us
  waiting for transfers between devices  69.7 us (42%)
  starting transfers between devices  42.4 us (26%)
  Pallas kernels  38.9 us (24%)
  local copies, waits for them, and re-layouts  11.2 us (7%)
    ppermute x32, waiting for transfers between devices, hop(): return lax.ppermute(rows, ('section', 'expert'), pairs)  59.8 us
    pallas_call x9, Pallas kernels, expert_sums(): pl.pallas_call(functools.partial(expert_kernel, len(parts)), out_shape=[j...  27.5 us
    ppermute x32, starting transfers between devices, hop(): return lax.ppermute(rows, ('section', 'expert'), pairs)  23.9 us
    ppermute x3, starting transfers between devices, core_swap(): return lax.ppermute(rows, 'section', core_pairs())  11.6 us
    unnamed x24, local copies, waits for them, and re-layouts  11.1 us
    ppermute x1, waiting for transfers between devices, body(): lax.ppermute(block, ('section', 'seq'), route(lambda b: 1 - b))  6.35 us
    pallas_call x2, Pallas kernels, staged(): pl.pallas_call(kernel, out_shape=[rows_like(rows), rows_like(rows)], in_s...  5.02 us
  transfers between devices with their start and end apart: 41, of which 29 were waited for; matrix products, arithmetic and copies ran while one was open for 0% of the time, Pallas kernels for 23%

profile of v1, /device:TPU:1, one launch (start us, length us, event | category | flops | bytes accessed | tf_op | source)
XLA Modules:
  0.0 164.0 jit_solution(8447809318421474268)
XLA Ops:
  0.0 2.6 %collective-permute-start = (bf16[2,160,1024]{2,1,0:T(8,128)(2,1)}, bf16[2,160,1024]{2,1,0:T(8,128)(2,1)}, u32[]{:S(2)}, u32[]{:S(2)}) collective-permute-start(bf16[2,160,1024]{2,1,0:T(8,128)(2,1)} %bitcast.89), channel_id=1, source_target_pairs={{24,0},{28,4},{0,8},{4,12},{8,16},{12,20},{16,24},{20,28},{25,1},{... | collective-permute-start | bytes 1966088 | tf_op jit(solution)/shard_map/ppermute | solution.py:326
  9.3 2.7 %pick_units.1 = (bf16[320,4096]{1,0:T(8,128)(2,1)}, bf16[320,4096]{1,0:T(8,128)(2,1)}) custom-call(s32[1]{0:T(128)} %bitcast.3.core_ref, bf16[2,320,4096]{2,1,0:T(8,128)(2,1)S(1)} %copy-done, bf16[2,320,4096]{2,1,0:T(8,128)(2,1)S(1)} %copy-done.2), custom_call_target="tpu_custom_call" | custom-call | bytes 10485760 | tf_op jit(solution)/shard_map/pick_units/pallas_call | solution.py:151
  13.6 6.4 %collective-permute-done.1.refs_1_ = bf16[2,160,1024]{2,1,0:T(8,128)(2,1)} collective-permute-done((bf16[2,160,1024]{2,1,0:T(8,128)(2,1)}, bf16[2,160,1024]{2,1,0:T(8,128)(2,1)}, u32[]{:S(2)}, u32[]{:S(2)}) %collective-permute-start.1) | collective-permute-done | bytes 655392 | tf_op jit(solution)/shard_map/ppermute | solution.py:327
  21.1 3.2 %attend.1 = (f32[96,4096]{1,0:T(8,128)S(1)}, bf16[48,4096]{1,0:T(8,128)(2,1)S(1)}, bf16[24,4096]{1,0:T(8,128)(2,1)S(1)}, bf16[24,4096]{1,0:T(8,128)(2,1)S(1)}) custom-call(s32[2]{0:T(128)S(1)} %pad_add_fusion.rel_ref, bf16[96,4096]{1,0:T(8,128)(2,1)S(1)} %bitcast.84, bf16[96,4096]{1,0:T(8,128)(2,1)S(1)} %bitcast.85, f32[1,4096]{1,0:T(1,128)S(1)} %bitcast.86, ...), custom_call_target="tpu_custom_call" | custom-call | flops 301989888 | bytes 6000000 | tf_op jit(solution)/shard_map/attend/pallas_call | solution.py:72
  40.2 3.1 %expert.9 = (bf16[48,4096]{1,0:T(8,128)(2,1)S(1)}, bf16[48,4096]{1,0:T(8,128)(2,1)S(1)}) custom-call(bf16[48,4096]{1,0:T(8,128)(2,1)S(1)} %collective-permute-done.8.refs_0_, bf16[48,4096]{1,0:T(8,128)(2,1)S(1)} %collective-permute-done.9.refs_1_, bf16[640,4096]{1,0:T(8,128)(2,1)S(1)} %get-tuple-element.145.refs_2_, ...), custom_call_target="tpu_custom_call" | custom-call | flops 1 | bytes 1 | tf_op jit(solution)/shard_map/expert/pallas_call | solution.py:169
  43.3 3.2 %collective-permute-done.6.refs_0_ = bf16[48,4096]{1,0:T(8,128)(2,1)S(1)} collective-permute-done((bf16[48,4096]{1,0:T(8,128)(2,1)S(1)}, bf16[48,4096]{1,0:T(8,128)(2,1)S(1)}, u32[]{:S(2)}, u32[]{:S(2)}) %collective-permute-start.6) | collective-permute-done | bytes 393248 | tf_op jit(solution)/shard_map/ppermute | solution.py:405
  49.0 6.0 %collective-permute-done.12.refs_0_ = bf16[48,4096]{1,0:T(8,128)(2,1)S(1)} collective-permute-done((bf16[48,4096]{1,0:T(8,128)(2,1)S(1)}, bf16[48,4096]{1,0:T(8,128)(2,1)S(1)}, u32[]{:S(2)}, u32[]{:S(2)}) %collective-permute-start.12) | collective-permute-done | bytes 393248 | tf_op jit(solution)/shard_map/ppermute | solution.py:405
  57.4 3.1 %expert.10 = (bf16[48,4096]{1,0:T(8,128)(2,1)S(1)}, bf16[48,4096]{1,0:T(8,128)(2,1)S(1)}) custom-call(bf16[48,4096]{1,0:T(8,128)(2,1)S(1)} %collective-permute-done.12.refs_0_, bf16[48,4096]{1,0:T(8,128)(2,1)S(1)} %collective-permute-done.13.refs_1_, bf16[640,4096]{1,0:T(8,128)(2,1)S(1)} %get-tuple-element.145.refs_2_, ...), custom_call_target="tpu_custom_call" | custom-call | flops 1 | bytes 1 | tf_op jit(solution)/shard_map/expert/pallas_call | solution.py:169
  60.5 3.1 %expert.11 = (bf16[48,4096]{1,0:T(8,128)(2,1)S(1)}, bf16[48,4096]{1,0:T(8,128)(2,1)S(1)}) custom-call(bf16[48,4096]{1,0:T(8,128)(2,1)S(1)} %collective-permute-done.6.refs_0_, bf16[48,4096]{1,0:T(8,128)(2,1)S(1)} %collective-permute-done.7.refs_1_, bf16[640,4096]{1,0:T(8,128)(2,1)S(1)} %get-tuple-element.145.refs_2_, ...), custom_call_target="tpu_custom_call" | custom-call | flops 1 | bytes 1 | tf_op jit(solution)/shard_map/expert/pallas_call | solution.py:169
  65.8 6.0 %collective-permute-done.16.fore_ref.refs_0_ = bf16[48,4096]{1,0:T(8,128)(2,1)S(1)} collective-permute-done((bf16[48,4096]{1,0:T(8,128)(2,1)S(1)}, bf16[48,4096]{1,0:T(8,128)(2,1)S(1)}, u32[]{:S(2)}, u32[]{:S(2)}) %collective-permute-start.16) | collective-permute-done | bytes 393248 | tf_op jit(solution)/shard_map/ppermute | solution.py:405
  72.8 3.1 %expert.12 = (bf16[48,4096]{1,0:T(8,128)(2,1)S(1)}, bf16[48,4096]{1,0:T(8,128)(2,1)S(1)}) custom-call(bf16[48,4096]{1,0:T(8,128)(2,1)S(1)} %collective-permute-done.16.fore_ref.refs_0_, bf16[48,4096]{1,0:T(8,128)(2,1)S(1)} %collective-permute-done.17.rear_ref.refs_1_, bf16[640,4096]{1,0:T(8,128)(2,1)S(1)} %get-tuple-element.145.refs_2_, ...), custom_call_target="tpu_custom_call" | custom-call | flops 1 | bytes 1 | tf_op jit(solution)/shard_map/expert/pallas_call | solution.py:169
  75.9 3.1 %expert.13 = (bf16[48,4096]{1,0:T(8,128)(2,1)S(1)}, bf16[48,4096]{1,0:T(8,128)(2,1)S(1)}) custom-call(bf16[48,4096]{1,0:T(8,128)(2,1)S(1)} %collective-permute-done.10.refs_0_, bf16[48,4096]{1,0:T(8,128)(2,1)S(1)} %collective-permute-done.11.refs_1_, bf16[640,4096]{1,0:T(8,128)(2,1)S(1)} %get-tuple-element.145.refs_2_, ...), custom_call_target="tpu_custom_call" | custom-call | flops 1 | bytes 1 | tf_op jit(solution)/shard_map/expert/pallas_call | solution.py:169
  87.4 2.9 %expert.15 = (bf16[24,4096]{1,0:T(8,128)(2,1)S(1)}, bf16[24,4096]{1,0:T(8,128)(2,1)S(1)}) custom-call(bf16[24,4096]{1,0:T(8,128)(2,1)S(1)} %collective-permute-done.20.refs_0_, bf16[24,4096]{1,0:T(8,128)(2,1)S(1)} %collective-permute-done.21.refs_1_, bf16[640,4096]{1,0:T(8,128)(2,1)S(1)} %get-tuple-element.145.refs_2_, ...), custom_call_target="tpu_custom_call" | custom-call | flops 1 | bytes 1 | tf_op jit(solution)/shard_map/expert/pallas_call | solution.py:169
  91.9 3.1 %expert.14 = (bf16[48,4096]{1,0:T(8,128)(2,1)S(1)}, bf16[48,4096]{1,0:T(8,128)(2,1)S(1)}) custom-call(bf16[48,4096]{1,0:T(8,128)(2,1)S(1)} %collective-permute-done.14.fore_ref.refs_0_, bf16[48,4096]{1,0:T(8,128)(2,1)S(1)} %collective-permute-done.15.rear_ref.refs_1_, bf16[640,4096]{1,0:T(8,128)(2,1)S(1)} %get-tuple-element.145.refs_2_, ...), custom_call_target="tpu_custom_call" | custom-call | flops 1 | bytes 1 | tf_op jit(solution)/shard_map/expert/pallas_call | solution.py:169
  97.8 2.9 %expert.16 = (bf16[24,4096]{1,0:T(8,128)(2,1)S(1)}, bf16[24,4096]{1,0:T(8,128)(2,1)S(1)}) custom-call(bf16[24,4096]{1,0:T(8,128)(2,1)S(1)} %collective-permute-done.18.refs_0_, bf16[24,4096]{1,0:T(8,128)(2,1)S(1)} %collective-permute-done.19.refs_1_, bf16[640,4096]{1,0:T(8,128)(2,1)S(1)} %get-tuple-element.145.refs_2_, ...), custom_call_target="tpu_custom_call" | custom-call | flops 1 | bytes 1 | tf_op jit(solution)/shard_map/expert/pallas_call | solution.py:169
  102.3 4.0 %collective-permute-done.28.refs_2_ = bf16[24,4096]{1,0:T(8,128)(2,1)S(1)} collective-permute-done((bf16[24,4096]{1,0:T(8,128)(2,1)S(1)}, bf16[24,4096]{1,0:T(8,128)(2,1)S(1)}, u32[]{:S(2)}, u32[]{:S(2)}) %collective-permute-start.28) | collective-permute-done | bytes 196640 | tf_op jit(solution)/shard_map/ppermute | solution.py:405
  111.4 3.1 %expert.17 = (bf16[48,4096]{1,0:T(8,128)(2,1)S(1)}, bf16[48,4096]{1,0:T(8,128)(2,1)S(1)}) custom-call(bf16[48,4096]{1,0:T(8,128)(2,1)S(1)} %get-tuple-element.205.refs_0_, bf16[48,4096]{1,0:T(8,128)(2,1)S(1)} %collective-permute-done.3.refs_1_, bf16[640,4096]{1,0:T(8,128)(2,1)S(1)} %get-tuple-element.145.refs_2_, ...), custom_call_target="tpu_custom_call" | custom-call | flops 1 | bytes 1 | tf_op jit(solution)/shard_map/expert/pallas_call | solution.py:169
  114.5 3.3 %collective-permute-done.30.refs_2_ = bf16[48,4096]{1,0:T(8,128)(2,1)S(1)} collective-permute-done((bf16[48,4096]{1,0:T(8,128)(2,1)S(1)}, bf16[48,4096]{1,0:T(8,128)(2,1)S(1)}, u32[]{:S(2)}, u32[]{:S(2)}) %collective-permute-start.30) | collective-permute-done | bytes 393248 | tf_op jit(solution)/shard_map/ppermute | solution.py:405
  120.2 3.1 %collective-permute-done.26.refs_2_ = bf16[48,4096]{1,0:T(8,128)(2,1)S(1)} collective-permute-done((bf16[48,4096]{1,0:T(8,128)(2,1)S(1)}, bf16[48,4096]{1,0:T(8,128)(2,1)S(1)}, u32[]{:S(2)}, u32[]{:S(2)}) %collective-permute-start.26) | collective-permute-done | bytes 393248 | tf_op jit(solution)/shard_map/ppermute | solution.py:405
  125.6 6.0 %collective-permute-done.32.refs_2_ = bf16[48,4096]{1,0:T(8,128)(2,1)S(1)} collective-permute-done((bf16[48,4096]{1,0:T(8,128)(2,1)S(1)}, bf16[48,4096]{1,0:T(8,128)(2,1)S(1)}, u32[]{:S(2)}, u32[]{:S(2)}) %collective-permute-start.32) | collective-permute-done | bytes 393248 | tf_op jit(solution)/shard_map/ppermute | solution.py:405
  134.1 6.0 %collective-permute-done.37.ahead_ref = bf16[48,4096]{1,0:T(8,128)(2,1)S(1)} collective-permute-done((bf16[48,4096]{1,0:T(8,128)(2,1)S(1)}, bf16[48,4096]{1,0:T(8,128)(2,1)S(1)}, u32[]{:S(2)}, u32[]{:S(2)}) %collective-permute-start.37) | collective-permute-done | bytes 393248 | tf_op jit(solution)/shard_map/ppermute | solution.py:405
  142.2 6.3 %collective-permute-done.34.ahead_ref = bf16[48,4096]{1,0:T(8,128)(2,1)S(1)} collective-permute-done((bf16[48,4096]{1,0:T(8,128)(2,1)S(1)}, bf16[48,4096]{1,0:T(8,128)(2,1)S(1)}, u32[]{:S(2)}, u32[]{:S(2)}) %collective-permute-start.34) | collective-permute-done | bytes 393248 | tf_op jit(solution)/shard_map/ppermute | solution.py:405
  149.4 7.9 %collective-permute-start.36 = (bf16[48,4096]{1,0:T(8,128)(2,1)S(1)}, bf16[48,4096]{1,0:T(8,128)(2,1)S(1)}, u32[]{:S(2)}, u32[]{:S(2)}) collective-permute-start(bf16[48,4096]{1,0:T(8,128)(2,1)S(1)} %finish_sums.2.refs_4_), channel_id=1, source_target_pairs={{0,8},{8,0},{16,24},{24,16},{1,9},{9,1},{17,25},{25,17},{2,10},{10... | collective-permute-start | bytes 1179656 | tf_op jit(solution)/shard_map/ppermute | solution.py:383
  157.3 3.6 %collective-permute-start.40 = (bf16[48,4096]{1,0:T(8,128)(2,1)S(1)}, bf16[48,4096]{1,0:T(8,128)(2,1)S(1)}, u32[]{:S(2)}, u32[]{:S(2)}) collective-permute-start(bf16[48,4096]{1,0:T(8,128)(2,1)S(1)} %collective-permute-done.39.refs_6_), channel_id=1, source_target_pairs={{0,8},{8,0},{16,24},{24,16},{1,9},{9,1},{17,25},{25,17},{2,10},{10... | collective-permute-start | bytes 1179656 | tf_op jit(solution)/shard_map/ppermute | solution.py:383
  (119 shorter events, 65.1 us)
Async XLA Ops:
  0.0 13.6 %collective-permute-start = (bf16[2,160,1024]{2,1,0:T(8,128)(2,1)}, bf16[2,160,1024]{2,1,0:T(8,128)(2,1)}, u32[]{:S(2)}, u32[]{:S(2)}) collective-permute-start(bf16[2,160,1024]{2,1,0:T(8,128)(2,1)} %bitcast.89), channel_id=1, source_target_pairs={{24,0},{28,4},{0,8},{4,12},{8,16},{12,20},{16,24},{20,28},{25,1},{... | collective-permute-start | bytes 1966088 | tf_op jit(solution)/shard_map/ppermute | solution.py:326
  2.6 17.3 %collective-permute-start.1 = (bf16[2,160,1024]{2,1,0:T(8,128)(2,1)}, bf16[2,160,1024]{2,1,0:T(8,128)(2,1)}, u32[]{:S(2)}, u32[]{:S(2)}) collective-permute-start(bf16[2,160,1024]{2,1,0:T(8,128)(2,1)} %bitcast.90), channel_id=1, source_target_pairs={{28,0},{24,4},{4,8},{0,12},{12,16},{8,20},{20,24},{16,28},{29,1},{... | collective-permute-start | bytes 1966088 | tf_op jit(solution)/shard_map/ppermute | solution.py:327
  12.0 16.9 %collective-permute-start.4 = (bf16[320,4096]{1,0:T(8,128)(2,1)}, bf16[320,4096]{1,0:T(8,128)(2,1)S(1)}, u32[]{:S(2)}, u32[]{:S(2)}) collective-permute-start(bf16[320,4096]{1,0:T(8,128)(2,1)} %get-tuple-element.133), channel_id=1, source_target_pairs={{0,8},{8,0},{16,24},{24,16},{1,9},{9,1},{17,25},{25,17},{2,10},{10... | collective-permute-start | bytes 7864328 | tf_op jit(solution)/shard_map/ppermute | solution.py:348
  12.8 16.2 %collective-permute-start.5 = (bf16[320,4096]{1,0:T(8,128)(2,1)}, bf16[320,4096]{1,0:T(8,128)(2,1)}, u32[]{:S(2)}, u32[]{:S(2)}) collective-permute-start(bf16[320,4096]{1,0:T(8,128)(2,1)} %get-tuple-element.134), channel_id=1, source_target_pairs={{0,8},{8,0},{16,24},{24,16},{1,9},{9,1},{17,25},{25,17},{2,10},{10... | collective-permute-start | bytes 7864328 | tf_op jit(solution)/shard_map/ppermute | solution.py:348
  38.7 16.2 %collective-permute-start.12 = (bf16[48,4096]{1,0:T(8,128)(2,1)S(1)}, bf16[48,4096]{1,0:T(8,128)(2,1)S(1)}, u32[]{:S(2)}, u32[]{:S(2)}) collective-permute-start(bf16[48,4096]{1,0:T(8,128)(2,1)S(1)} %collective-permute-done.8.refs_0_), channel_id=1, source_target_pairs={{0,1},{1,2},{2,3},{3,19},{19,18},{18,17},{17,16},{16,0},{8,9},{9,1... | collective-permute-start | bytes 1179656 | tf_op jit(solution)/shard_map/ppermute | solution.py:405
  40.0 15.9 %collective-permute-start.13 = (bf16[48,4096]{1,0:T(8,128)(2,1)S(1)}, bf16[48,4096]{1,0:T(8,128)(2,1)S(1)}, u32[]{:S(2)}, u32[]{:S(2)}) collective-permute-start(bf16[48,4096]{1,0:T(8,128)(2,1)S(1)} %collective-permute-done.9.refs_1_), channel_id=1, source_target_pairs={{0,16},{1,0},{2,1},{3,2},{19,3},{18,19},{17,18},{16,17},{8,24},{9,... | collective-permute-start | bytes 1179656 | tf_op jit(solution)/shard_map/ppermute | solution.py:405
  47.5 16.1 %collective-permute-start.10 = (bf16[48,4096]{1,0:T(8,128)(2,1)S(1)}, bf16[48,4096]{1,0:T(8,128)(2,1)S(1)}, u32[]{:S(2)}, u32[]{:S(2)}) collective-permute-start(bf16[48,4096]{1,0:T(8,128)(2,1)S(1)} %collective-permute-done.6.refs_0_), channel_id=1, source_target_pairs={{0,1},{1,2},{2,3},{3,19},{19,18},{18,17},{17,16},{16,0},{8,9},{9,1... | collective-permute-start | bytes 1179656 | tf_op jit(solution)/shard_map/ppermute | solution.py:405
  48.8 15.6 %collective-permute-start.11 = (bf16[48,4096]{1,0:T(8,128)(2,1)S(1)}, bf16[48,4096]{1,0:T(8,128)(2,1)S(1)}, u32[]{:S(2)}, u32[]{:S(2)}) collective-permute-start(bf16[48,4096]{1,0:T(8,128)(2,1)S(1)} %collective-permute-done.7.refs_1_), channel_id=1, source_target_pairs={{0,16},{1,0},{2,1},{3,2},{19,3},{18,19},{17,18},{16,17},{8,24},{9,... | collective-permute-start | bytes 1179656 | tf_op jit(solution)/shard_map/ppermute | solution.py:405
  55.9 15.8 %collective-permute-start.16 = (bf16[48,4096]{1,0:T(8,128)(2,1)S(1)}, bf16[48,4096]{1,0:T(8,128)(2,1)S(1)}, u32[]{:S(2)}, u32[]{:S(2)}) collective-permute-start(bf16[48,4096]{1,0:T(8,128)(2,1)S(1)} %collective-permute-done.12.refs_0_), channel_id=1, source_target_pairs={{0,1},{1,2},{2,3},{3,19},{19,18},{18,17},{17,16},{16,0},{8,9},{9,1... | collective-permute-start | bytes 1179656 | tf_op jit(solution)/shard_map/ppermute | solution.py:405
  57.2 15.6 %collective-permute-start.17 = (bf16[48,4096]{1,0:T(8,128)(2,1)S(1)}, bf16[48,4096]{1,0:T(8,128)(2,1)S(1)}, u32[]{:S(2)}, u32[]{:S(2)}) collective-permute-start(bf16[48,4096]{1,0:T(8,128)(2,1)S(1)} %collective-permute-done.13.refs_1_), channel_id=1, source_target_pairs={{0,16},{1,0},{2,1},{3,2},{19,3},{18,19},{17,18},{16,17},{8,24},{9,... | collective-permute-start | bytes 1179656 | tf_op jit(solution)/shard_map/ppermute | solution.py:405
  64.3 15.8 %collective-permute-start.14 = (bf16[48,4096]{1,0:T(8,128)(2,1)S(1)}, bf16[48,4096]{1,0:T(8,128)(2,1)S(1)}, u32[]{:S(2)}, u32[]{:S(2)}) collective-permute-start(bf16[48,4096]{1,0:T(8,128)(2,1)S(1)} %collective-permute-done.10.refs_0_), channel_id=1, source_target_pairs={{0,1},{1,2},{2,3},{3,19},{19,18},{18,17},{17,16},{16,0},{8,9},{9,1... | collective-permute-start | bytes 1179656 | tf_op jit(solution)/shard_map/ppermute | solution.py:405
  65.6 15.6 %collective-permute-start.15 = (bf16[48,4096]{1,0:T(8,128)(2,1)S(1)}, bf16[48,4096]{1,0:T(8,128)(2,1)S(1)}, u32[]{:S(2)}, u32[]{:S(2)}) collective-permute-start(bf16[48,4096]{1,0:T(8,128)(2,1)S(1)} %collective-permute-done.11.refs_1_), channel_id=1, source_target_pairs={{0,16},{1,0},{2,1},{3,2},{19,3},{18,19},{17,18},{16,17},{8,24},{9,... | collective-permute-start | bytes 1179656 | tf_op jit(solution)/shard_map/ppermute | solution.py:405
  82.7 12.2 %collective-permute-start.18 = (bf16[24,4096]{1,0:T(8,128)(2,1)S(1)}, bf16[24,4096]{1,0:T(8,128)(2,1)S(1)}, u32[]{:S(2)}, u32[]{:S(2)}) collective-permute-start(bf16[24,4096]{1,0:T(8,128)(2,1)S(1)} %get-tuple-element.179), channel_id=1, source_target_pairs={{0,1},{1,2},{2,3},{3,19},{19,18},{18,17},{17,16},{16,0},{8,9},{9,1... | collective-permute-start | bytes 589832 | tf_op jit(solution)/shard_map/ppermute | solution.py:405
  96.3 13.4 %collective-permute-start.24 = (bf16[48,4096]{1,0:T(8,128)(2,1)S(1)}, bf16[48,4096]{1,0:T(8,128)(2,1)S(1)}, u32[]{:S(2)}, u32[]{:S(2)}) collective-permute-start(bf16[48,4096]{1,0:T(8,128)(2,1)S(1)} %get-tuple-element.195), channel_id=1, source_target_pairs={{0,1},{1,2},{2,3},{3,19},{19,18},{18,17},{17,16},{16,0},{8,9},{9,1... | collective-permute-start | bytes 1179656 | tf_op jit(solution)/shard_map/ppermute | solution.py:405
  97.0 12.8 %collective-permute-start.25 = (bf16[48,4096]{1,0:T(8,128)(2,1)S(1)}, bf16[48,4096]{1,0:T(8,128)(2,1)S(1)}, u32[]{:S(2)}, u32[]{:S(2)}) collective-permute-start(bf16[48,4096]{1,0:T(8,128)(2,1)S(1)} %get-tuple-element.196), channel_id=1, source_target_pairs={{0,16},{1,0},{2,1},{3,2},{19,3},{18,19},{17,18},{16,17},{8,24},{9,... | collective-permute-start | bytes 1179656 | tf_op jit(solution)/shard_map/ppermute | solution.py:405
  109.9 13.3 %collective-permute-start.26 = (bf16[48,4096]{1,0:T(8,128)(2,1)S(1)}, bf16[48,4096]{1,0:T(8,128)(2,1)S(1)}, u32[]{:S(2)}, u32[]{:S(2)}) collective-permute-start(bf16[48,4096]{1,0:T(8,128)(2,1)S(1)} %get-tuple-element.197), channel_id=1, source_target_pairs={{0,1},{1,2},{2,3},{3,19},{19,18},{18,17},{17,16},{16,0},{8,9},{9,1... | collective-permute-start | bytes 1179656 | tf_op jit(solution)/shard_map/ppermute | solution.py:405
  110.3 13.7 %collective-permute-start.27 = (bf16[48,4096]{1,0:T(8,128)(2,1)S(1)}, bf16[48,4096]{1,0:T(8,128)(2,1)S(1)}, u32[]{:S(2)}, u32[]{:S(2)}) collective-permute-start(bf16[48,4096]{1,0:T(8,128)(2,1)S(1)} %get-tuple-element.198), channel_id=1, source_target_pairs={{0,16},{1,0},{2,1},{3,2},{19,3},{18,19},{17,18},{16,17},{8,24},{9,... | collective-permute-start | bytes 1179656 | tf_op jit(solution)/shard_map/ppermute | solution.py:405
  118.7 13.0 %collective-permute-start.32 = (bf16[48,4096]{1,0:T(8,128)(2,1)S(1)}, bf16[48,4096]{1,0:T(8,128)(2,1)S(1)}, u32[]{:S(2)}, u32[]{:S(2)}) collective-permute-start(bf16[48,4096]{1,0:T(8,128)(2,1)S(1)} %get-tuple-element.220), channel_id=1, source_target_pairs={{0,1},{1,2},{2,3},{3,19},{19,18},{18,17},{17,16},{16,0},{8,9},{9,1... | collective-permute-start | bytes 1179656 | tf_op jit(solution)/shard_map/ppermute | solution.py:405
  118.9 13.4 %collective-permute-start.33 = (bf16[48,4096]{1,0:T(8,128)(2,1)S(1)}, bf16[48,4096]{1,0:T(8,128)(2,1)S(1)}, u32[]{:S(2)}, u32[]{:S(2)}) collective-permute-start(bf16[48,4096]{1,0:T(8,128)(2,1)S(1)} %get-tuple-element.221), channel_id=1, source_target_pairs={{0,16},{1,0},{2,1},{3,2},{19,3},{18,19},{17,18},{16,17},{8,24},{9,... | collective-permute-start | bytes 1179656 | tf_op jit(solution)/shard_map/ppermute | solution.py:405
  124.1 16.0 %collective-permute-start.37 = (bf16[48,4096]{1,0:T(8,128)(2,1)S(1)}, bf16[48,4096]{1,0:T(8,128)(2,1)S(1)}, u32[]{:S(2)}, u32[]{:S(2)}) collective-permute-start(bf16[48,4096]{1,0:T(8,128)(2,1)S(1)} %get-tuple-element.225), channel_id=1, source_target_pairs={{0,1},{1,2},{2,3},{3,19},{19,18},{18,17},{17,16},{16,0},{8,9},{9,1... | collective-permute-start | bytes 1179656 | tf_op jit(solution)/shard_map/ppermute | solution.py:405
  124.6 16.1 %collective-permute-start.38 = (bf16[48,4096]{1,0:T(8,128)(2,1)S(1)}, bf16[48,4096]{1,0:T(8,128)(2,1)S(1)}, u32[]{:S(2)}, u32[]{:S(2)}) collective-permute-start(bf16[48,4096]{1,0:T(8,128)(2,1)S(1)} %get-tuple-element.226), channel_id=1, source_target_pairs={{0,16},{1,0},{2,1},{3,2},{19,3},{18,19},{17,18},{16,17},{8,24},{9,... | collective-permute-start | bytes 1179656 | tf_op jit(solution)/shard_map/ppermute | solution.py:405
  132.5 16.0 %collective-permute-start.34 = (bf16[48,4096]{1,0:T(8,128)(2,1)S(1)}, bf16[48,4096]{1,0:T(8,128)(2,1)S(1)}, u32[]{:S(2)}, u32[]{:S(2)}) collective-permute-start(bf16[48,4096]{1,0:T(8,128)(2,1)S(1)} %get-tuple-element.222), channel_id=1, source_target_pairs={{0,1},{1,2},{2,3},{3,19},{19,18},{18,17},{17,16},{16,0},{8,9},{9,1... | collective-permute-start | bytes 1179656 | tf_op jit(solution)/shard_map/ppermute | solution.py:405
  133.0 16.2 %collective-permute-start.35 = (bf16[48,4096]{1,0:T(8,128)(2,1)S(1)}, bf16[48,4096]{1,0:T(8,128)(2,1)S(1)}, u32[]{:S(2)}, u32[]{:S(2)}) collective-permute-start(bf16[48,4096]{1,0:T(8,128)(2,1)S(1)} %get-tuple-element.223), channel_id=1, source_target_pairs={{0,16},{1,0},{2,1},{3,2},{19,3},{18,19},{17,18},{16,17},{8,24},{9,... | collective-permute-start | bytes 1179656 | tf_op jit(solution)/shard_map/ppermute | solution.py:405
  140.9 16.4 %collective-permute-start.39 = (bf16[48,4096]{1,0:T(8,128)(2,1)S(1)}, bf16[48,4096]{1,0:T(8,128)(2,1)S(1)}, u32[]{:S(2)}, u32[]{:S(2)}) collective-permute-start(bf16[48,4096]{1,0:T(8,128)(2,1)S(1)} %finish_sums.3), channel_id=1, source_target_pairs={{0,4},{4,0},{1,5},{5,1},{2,6},{6,2},{3,7},{7,3},{8,12},{12,8},{9,1... | collective-permute-start | bytes 1179656 | tf_op jit(solution)/shard_map/ppermute | solution.py:386
  (29 other events, 224.2 us)

commit v2 on v1

--- a/solution.py
+++ b/solution.py
@@ -124,6 +124,17 @@
         copy.wait()
 
 
+def stage_kernel(core_ref, q_ref, res_ref, q_out_ref, res_out_ref, sems):
+    copies = [
+        pltpu.make_async_copy(q_ref, q_out_ref, sems.at[0]),
+        pltpu.make_async_copy(res_ref, res_out_ref, sems.at[1]),
+    ]
+    for copy in copies:
+        copy.start()
+    for copy in copies:
+        copy.wait()
+
+
 def pool_kernel(core_ref, in_ref, out_w_ref, pair_in_ref, pair_out_ref, unit_in_ref, unit_out_ref, sems):
     core = core_ref[0]
     units = pair_in_ref.shape[0]
@@ -145,18 +156,18 @@
         copy.wait()
 
 
-def staged(kernel, core, arrays, rows, copies, name):
-    anywhere = pl.BlockSpec(memory_space=pl.ANY)
+def staged(kernel, core, arrays, outs, copies, name):
     vmem = pl.BlockSpec(memory_space=pltpu.VMEM)
     return pl.pallas_call(
         kernel,
-        out_shape=[rows_like(rows), rows_like(rows)],
-        in_specs=[pl.BlockSpec(memory_space=pltpu.SMEM)] + [anywhere] * len(arrays),
-        out_specs=[vmem, vmem],
+        out_shape=outs,
+        in_specs=[pl.BlockSpec(memory_space=pltpu.SMEM)]
+        + [pl.BlockSpec(memory_space=pl.ANY)] * len(arrays),
+        out_specs=[vmem] * len(outs),
         scratch_shapes=[pltpu.SemaphoreType.DMA((copies,))],
         compiler_params=pltpu.CompilerParams(vmem_limit_bytes=EXPERT_VMEM),
         cost_estimate=pl.CostEstimate(
-            flops=0, bytes_accessed=4 * rows * D * 2, transcendentals=0
+            flops=0, bytes_accessed=sum(2 * x.size * 2 for x in outs), transcendentals=0
         ),
         name=name,
     )(core, *arrays)
@@ -216,86 +227,58 @@
     return local(kernel, outs, *stayed, crossed, name="join_slots")
 
 
-def split_rows(fore_rows, rear_rows, cut):
-    size = fore_rows.shape[0]
-
-    def kernel(fore_ref, rear_ref, *out_refs):
-        out_refs = list(out_refs)
-        if cut > 0:
-            rows = fore_ref[...].astype(jnp.float32)[:cut]
-            out_refs.pop(0)[...] = rows.astype(jnp.bfloat16)
-        if cut < size:
-            rows = rear_ref[...].astype(jnp.float32)[cut:]
-            out_refs.pop(0)[...] = rows.astype(jnp.bfloat16)
-
-    outs = [rows_like(rows) for rows in (cut, size - cut) if rows > 0]
-    return local(kernel, outs, fore_rows, rear_rows, name="split_rows")
-
-
-def add_sums(ahead_part, behind_part, ahead, behind, cut):
-    size = ahead_part.shape[0]
-
-    def filled(rows, before):
-        rows = rows.astype(jnp.float32)
-        edges = [jnp.zeros((before, D), jnp.float32)] if before else []
-        edges.append(rows)
-        after = size - before - rows.shape[0]
-        if after:
-            edges.append(jnp.zeros((after, D), jnp.float32))
-        return jnp.concatenate(edges, axis=0) if len(edges) > 1 else rows
-
-    totals = [x for x in (ahead, behind) if x is not None]
-
+def add_sums(parts, totals):
     def kernel(*refs):
-        refs = list(refs)
-        sums = [refs.pop(0)[...].astype(jnp.float32), refs.pop(0)[...].astype(jnp.float32)]
-        if ahead is not None:
-            sums[0] = sums[0] + filled(refs.pop(0)[...], 0)
-        if behind is not None:
-            sums[1] = sums[1] + filled(refs.pop(0)[...], size - behind.shape[0])
-        for out_ref, total in zip(refs, sums):
+        for part_ref, total_ref, out_ref in zip(refs[:2], refs[2:4], refs[4:]):
+            total = part_ref[...].astype(jnp.float32) + total_ref[...].astype(jnp.float32)
             out_ref[...] = total.astype(jnp.bfloat16)
 
-    outs = [rows_like(size), rows_like(size)]
-    return local(kernel, outs, ahead_part, behind_part, *totals, name="add_sums")
-
-
-def finish_sums(own, ahead, behind):
-    def kernel(own_ref, ahead_ref, behind_ref, out_ref):
-        total = own_ref[...].astype(jnp.float32) + ahead_ref[...].astype(jnp.float32)
-        out_ref[...] = (total + behind_ref[...].astype(jnp.float32)).astype(jnp.bfloat16)
-
-    return local(kernel, [rows_like(own.shape[0])], own, ahead, behind, name="finish_sums")[0]
-
-
-def combine_kernel(blocks, state_ref, scale_ref, *refs):
-    total = None
-    for j in range(blocks):
-        part = lax.dot_general(
-            refs[j][...],
-            refs[blocks + j][...],
-            (((1,), (0,)), ((), ())),
-            preferred_element_type=jnp.float32,
-        )
+    return local(kernel, [rows_like(x.shape[0]) for x in parts], *parts, *totals, name="add_sums")
+
+
+def finish_sums(*terms, pieces=1):
+    size = terms[0].shape[0] // pieces
+
+    def kernel(*refs):
+        total = refs[0][...].astype(jnp.float32)
+        for ref in refs[1 : len(terms)]:
+            total = total + ref[...].astype(jnp.float32)
+        for i, out_ref in enumerate(refs[len(terms) :]):
+            out_ref[...] = total[i * size : (i + 1) * size].astype(jnp.bfloat16)
+
+    return local(kernel, [rows_like(size)] * pieces, *terms, name="finish_sums")
+
+
+def combine_kernel(blocks, state_ref, scale_ref, undo_ref, *refs):
+    if refs[0].shape[0] % 8 == 0:
+        rows = [ref[...].astype(jnp.float32) for ref in refs[:blocks]]
+        rows = [jnp.concatenate(rows, axis=0).astype(jnp.bfloat16)]
+    else:
+        rows = [ref[...] for ref in refs[:blocks]]
+    begin, total = 0, None
+    for part in rows:
+        pick = undo_ref[:, begin : begin + part.shape[0]]
+        begin += part.shape[0]
+        part = jnp.dot(pick, part, preferred_element_type=jnp.float32)
         total = part if total is None else total + part
-    refs[2 * blocks][...] = (state_ref[...] + scale_ref[...] * total).astype(jnp.bfloat16)
+    refs[blocks][...] = (state_ref[...] + scale_ref[...] * total).astype(jnp.bfloat16)
 
 
 def combine(state, scale, undo, returned):
     tok_count = state.shape[0]
-    blocks = len(undo)
+    blocks = len(returned)
     vmem = pl.BlockSpec(memory_space=pltpu.VMEM)
     return pl.pallas_call(
         functools.partial(combine_kernel, blocks),
         out_shape=jax.ShapeDtypeStruct((tok_count, D), jnp.bfloat16),
-        in_specs=[vmem] * (2 + 2 * blocks),
+        in_specs=[vmem] * (3 + blocks),
         out_specs=vmem,
         compiler_params=pltpu.CompilerParams(vmem_limit_bytes=EXPERT_VMEM),
         cost_estimate=pl.CostEstimate(
             flops=2 * tok_count * tok_count * D, bytes_accessed=4_000_000, transcendentals=0
         ),
         name="combine",
-    )(state, scale, *undo, *returned)
+    )(state, scale, undo, *returned)
 
 
 def body(
@@ -323,10 +306,10 @@
     block = enc_kv[:, 0]
     if seqs == 2:
         shards = [
+            lax.ppermute(block, ("section", "seq"), route(lambda b: 1 - b)),
             lax.ppermute(block, ("section", "seq"), route(lambda b: b)),
-            lax.ppermute(block, ("section", "seq"), route(lambda b: 1 - b)),
         ]
-        origins = [q, 1 - q]
+        origins = [1 - q, q]
     else:
         shards = [
             lax.ppermute(block, ("section", "seq"), route(lambda b: b)),
@@ -343,7 +326,9 @@
 
     core_at = core.astype(jnp.int32)[None]
     share = w_in.shape[1]
-    pair_units = staged(pick_kernel, core_at, [w_in, w_out], share, 2, "pick_units")
+    pair_units = staged(
+        pick_kernel, core_at, [w_in, w_out], [rows_like(share)] * 2, 2, "pick_units"
+    )
     rel, pair_units = lax.optimization_barrier((rel, pair_units))
     pair_units = [lax.ppermute(rows, "section", core_pairs()) for rows in pair_units]
 
@@ -359,24 +344,31 @@
     turns = [(dq, dc) for dq in range(seqs) for dc in range(CORES)]
     slots = jnp.arange(capacity, dtype=jnp.int32)
     dispatch, undo = [], []
-    block_slots = jnp.arange(CORES * capacity, dtype=jnp.int32)
     for dq, dc in turns:
         named = ((q + dq) % seqs) * CORES + (core ^ dc)
         code = jnp.where(kept & (experts_of == named), slot_of, -1)
         dispatch.append((slots[:, None] == code[None, :]).astype(jnp.bfloat16))
-        code = jnp.where(code >= 0, code + dc * capacity, -1)
-        undo.append((code[:, None] == block_slots[None, :]).astype(jnp.bfloat16))
+        undo.append((code[:, None] == slots[None, :]).astype(jnp.bfloat16))
+    undo = jnp.concatenate(undo, axis=1)
     scale = (keep[0].astype(jnp.float32) * route_prob[0])[:, None]
 
     crossing = jnp.concatenate(
         [rows for (dq, dc), rows in zip(turns, dispatch) if dc == 1], axis=0
     )
     staying = [rows for (dq, dc), rows in zip(turns, dispatch) if dc == 0]
-    rel, crossing, staying, undo, scale = lax.optimization_barrier(
-        (rel, crossing, staying, undo, scale)
+    ready, rel, crossing, staying, undo, scale = lax.optimization_barrier(
+        (core_at, rel, crossing, staying, undo, scale)
+    )
+    query_rows, residual = staged(
+        stage_kernel,
+        ready,
+        [queries[0], dec_state[0]],
+        [rows_like(tok_count)] * 2,
+        2,
+        "stage_rows",
     )
     state, crossed, *stayed = attend(
-        rel, queries[0], dec_state[0], norm_gain[None, :], shards, [crossing] + staying
+        rel, query_rows, residual, norm_gain[None, :], shards, [crossing] + staying
     )
 
     def core_swap(rows):
@@ -390,7 +382,12 @@
     parts = [slot_blocks[0], moved[0] if seqs == 2 else jnp.concatenate(moved, axis=0)]
 
     unit_in, unit_out = staged(
-        pool_kernel, core_at, [w_in, w_out, *pair_units], CORES * share, 4, "pool_units"
+        pool_kernel,
+        core_at,
+        [w_in, w_out, *pair_units],
+        [rows_like(CORES * share)] * 2,
+        4,
+        "pool_units",
     )
     parts[1], unit_in, unit_out = lax.optimization_barrier((parts[1], unit_in, unit_out))
 
@@ -405,10 +402,6 @@
         return lax.ppermute(rows, ("section", "expert"), pairs)
 
     half = count // 2
-    sizes = [rows.shape[0] for rows in parts]
-    cut = [
-        rows // 2 if rows // 2 % 8 == 0 else rows * (1 - p) for p, rows in enumerate(sizes)
-    ]
     fore = [[rows] for rows in parts]
     rear = [[rows] for rows in parts]
     sums = {}
@@ -428,61 +421,55 @@
             rear[p].append(hop(rows[1], -1))
             if k < half - 1:
                 sums[p, k] = expert_sums([fore[p][k], rear[p][k]], unit_in, unit_out)
-    rows = (fore[0][-1], rear[0][-1])
-    lead = split_rows(*rows, cut[0])
-    rows, lead = lax.optimization_barrier((rows, lead))
-    sums[0, half - 1] = expert_sums(rows, unit_in, unit_out)
-    rows = (fore[1][-1], rear[1][-1])
-    follow = split_rows(*after([(0, half - 1), (1, half - 2)], rows), cut[1])
-    rows, follow = lax.optimization_barrier((rows, follow))
-    sums[1, half - 1] = expert_sums(rows, unit_in, unit_out)
+    fore[0].append(hop(fore[0][-1], 1))
+    rear[1].append(hop(rear[1][-1], -1))
     ahead_part, behind_part = [{}, {}], [{}, {}]
-    for p, rows in enumerate((lead, follow)):
-        got = []
-        if cut[p] > 0:
-            got.append(hop(rows[0], 1))
-        if cut[p] < sizes[p]:
-            got.append(hop(rows[-1], -1))
-        if p == 0:
-            got = after([(1, half - 1)], got)
-        sums[p, half] = expert_sums(got, unit_in, unit_out)
-    for p, k in list(sums):
-        got = list(sums[p, k])
-        if k < half:
-            behind_part[p][k], ahead_part[p][k] = got
-            continue
-        if cut[p] > 0:
-            ahead_part[p][half] = got.pop(0)
-        if cut[p] < sizes[p]:
-            behind_part[p][half] = got.pop(0)
-
-    ahead, behind = [None, None], [None, None]
-    for p in range(2):
-        if half in ahead_part[p]:
-            ahead[p] = hop(ahead_part[p][half], 1)
-        if half in behind_part[p]:
-            behind[p] = hop(behind_part[p][half], -1)
-    (ahead[0], behind[0]), parts = lax.optimization_barrier(((ahead[0], behind[0]), parts))
+    for (p, k), got in sums.items():
+        behind_part[p][k], ahead_part[p][k] = got
+    k = half - 1
+    behind_part[0][k], ahead_part[1][k] = expert_sums(
+        [fore[0][k], rear[1][k]], unit_in, unit_out
+    )
+    ahead_part[0][k], behind_part[1][k] = expert_sums(
+        [rear[0][k], fore[1][k]], unit_in, unit_out
+    )
+    lead = [behind_part[0][k], ahead_part[1][k]]
+    fore[0][half], lead = lax.optimization_barrier((fore[0][half], lead))
+    behind_part[0][k], ahead_part[1][k] = lead
+    ahead_part[0][half] = expert_sums([fore[0][half]], unit_in, unit_out)[0]
+    behind_part[1][half] = expert_sums([rear[1][half]], unit_in, unit_out)[0]
+
+    short = [hop(behind_part[0][half - 1], -1), hop(ahead_part[1][half - 1], 1)]
+    long = [hop(ahead_part[0][half], 1), hop(behind_part[1][half], -1)]
+    (short, parts) = lax.optimization_barrier((short, parts))
     own = expert_sums(parts, unit_in, unit_out)
     for k in range(half - 1, 0, -1):
-        for p in (1, 0):
-            totals = add_sums(
-                ahead_part[p][k], behind_part[p][k], ahead[p], behind[p], cut[p]
-            )
-            if k == 1 and p == 1:
+        if k < half - 1:
+            totals = add_sums([behind_part[0][k], ahead_part[1][k]], short)
+            if k == 1:
                 totals, own = lax.optimization_barrier((totals, own))
-            ahead[p], behind[p] = hop(totals[0], 1), hop(totals[1], -1)
-    done = [finish_sums(own[p], ahead[p], behind[p]) for p in range(2)]
-
-    width = CORES * capacity
-    if seqs == 2:
-        far = [done[1]]
+            short = [hop(totals[0], -1), hop(totals[1], 1)]
+        totals = add_sums([ahead_part[0][k], behind_part[1][k]], long)
+        long = [hop(totals[0], 1), hop(totals[1], -1)]
+    def cross(rows, dq, dc):
+        pairs = [
+            ((a ^ dc) * seqs + (b + dq) % seqs, a * seqs + b)
+            for a in range(sections)
+            for b in range(seqs)
+        ]
+        return lax.ppermute(rows, ("section", "seq"), pairs)
+
+    if seqs == 2 and capacity % 8 == 0:
+        blocks = finish_sums(own[1], short[1], long[1], pieces=CORES)
+        blocks = [*finish_sums(own[0], short[0], long[0], pieces=CORES), *blocks]
     else:
-        far = [done[1][i * width : (i + 1) * width] for i in range(seqs - 1)]
-    returned = []
-    for dq, rows in enumerate([done[0]] + far):
-        rows = seq_move(rows, -dq) if dq else rows
-        returned += [rows, core_swap(rows)]
+        near = finish_sums(own[0], short[0], long[0])[0]
+        far = finish_sums(own[1], short[1], long[1])[0]
+        blocks = [near[i * capacity : (i + 1) * capacity] for i in range(CORES)]
+        blocks += [far[i * capacity : (i + 1) * capacity] for i in range(len(turns) - CORES)]
+    returned = [
+        cross(rows, dq, dc) if dq or dc else rows for (dq, dc), rows in zip(turns, blocks)
+    ]
     return combine(state, scale, undo, returned)[None]
 
 

time: 165 us -> 157 us (0.952)
  waiting for transfers between devices: 69.7 us -> 65.3 us
  local copies, waits for them, and re-layouts: 11.2 us -> 8.71 us
    ppermute x0 -> x3, starting transfers between devices: none -> 12.7 us  [cross(): return lax.ppermute(rows, ('section', 'seq'), pairs)]
    ppermute x3 -> x1, starting transfers between devices: 11.6 us -> 1.39 us  [core_swap(): return lax.ppermute(rows, 'section', core_pairs())]
    ppermute x32 -> x28, waiting for transfers between devices: 59.8 us -> 52 us  [hop(): return lax.ppermute(rows, ('section', 'expert'), pairs)]
    ppermute x0 -> x3, waiting for transfers between devices: none -> 4.8 us  [cross(): return lax.ppermute(rows, ('section', 'seq'), pairs)]
    ppermute x2 -> x1, waiting for transfers between devices: 0.58 us -> 3.98 us  [seq_move(): lax.ppermute(rows, 'seq', [(b, (b + step) % seqs) for b in range(seqs)])]
    ppermute x1, waiting for transfers between devices: 6.35 us -> 3.12 us  [body(): lax.ppermute(block, ('section', 'seq'), route(lambda b: 1 - b))]
    ppermute x1, starting transfers between devices: 0.96 us -> 3.56 us  [body(): lax.ppermute(block, ('section', 'seq'), route(lambda b: 1 - b))]
    ppermute x1, starting transfers between devices: 2.6 us -> 0.01 us  [body(): lax.ppermute(block, ('section', 'seq'), route(lambda b: b))]
  transfers between devices with their start and end apart: 41 -> 37, of which waited for: 29 -> 20; matrix products, arithmetic and copies ran while one was open for 0% -> 1% of each run, Pallas kernels for 23% -> 24%
where the time goes in v2:
time: 157 us; the launch traced here: 156 us
  waiting for transfers between devices  65.3 us (42%)
  starting transfers between devices  41.4 us (26%)
  Pallas kernels  38.4 us (24%)
  local copies, waits for them, and re-layouts  8.71 us (6%)
    ppermute x28, waiting for transfers between devices, hop(): return lax.ppermute(rows, ('section', 'expert'), pairs)  52 us
    pallas_call x9, Pallas kernels, expert_sums(): pl.pallas_call(functools.partial(expert_kernel, len(parts)), out_shape=[j...  27.5 us
    ppermute x28, starting transfers between devices, hop(): return lax.ppermute(rows, ('section', 'expert'), pairs)  23.1 us
    ppermute x3, starting transfers between devices, cross(): return lax.ppermute(rows, ('section', 'seq'), pairs)  12.7 us
    unnamed x22, local copies, waits for them, and re-layouts  8.61 us
    pallas_call x3, Pallas kernels, staged(): pl.pallas_call(kernel, out_shape=outs, in_specs=[pl.BlockSpec(memory_spac...  5.13 us
    ppermute x3, waiting for transfers between devices, cross(): return lax.ppermute(rows, ('section', 'seq'), pairs)  4.8 us
    ppermute x1, waiting for transfers between devices, seq_move(): lax.ppermute(rows, 'seq', [(b, (b + step) % seqs) for b in range(seqs)])  3.98 us
  transfers between devices with their start and end apart: 37, of which 20 were waited for; matrix products, arithmetic and copies ran while one was open for 1% of the time, Pallas kernels for 24%

profile of v2, /device:TPU:1, one launch (start us, length us, event | category | flops | bytes accessed | tf_op | source)
XLA Modules:
  0.0 156.3 jit_solution(17160617478818988407)
XLA Ops:
  0.0 3.6 %collective-permute-start = (bf16[2,160,1024]{2,1,0:T(8,128)(2,1)}, bf16[2,160,1024]{2,1,0:T(8,128)(2,1)}, u32[]{:S(2)}, u32[]{:S(2)}) collective-permute-start(bf16[2,160,1024]{2,1,0:T(8,128)(2,1)} %bitcast.81), channel_id=1, source_target_pairs={{28,0},{24,4},{4,8},{0,12},{12,16},{8,20},{20,24},{16,28},{29,1},{... | collective-permute-start | bytes 1966088 | tf_op jit(solution)/shard_map/ppermute | solution.py:309
  15.4 3.1 %collective-permute-done.refs_0_ = bf16[2,160,1024]{2,1,0:T(8,128)(2,1)} collective-permute-done((bf16[2,160,1024]{2,1,0:T(8,128)(2,1)}, bf16[2,160,1024]{2,1,0:T(8,128)(2,1)}, u32[]{:S(2)}, u32[]{:S(2)}) %collective-permute-start) | collective-permute-done | bytes 655392 | tf_op jit(solution)/shard_map/ppermute | solution.py:309
  18.5 3.2 %attend.1 = (f32[96,4096]{1,0:T(8,128)S(1)}, bf16[48,4096]{1,0:T(8,128)(2,1)S(1)}, bf16[24,4096]{1,0:T(8,128)(2,1)S(1)}, bf16[24,4096]{1,0:T(8,128)(2,1)S(1)}) custom-call(s32[2]{0:T(128)S(1)} %pad_add_fusion.rel_ref, bf16[96,4096]{1,0:T(8,128)(2,1)S(1)} %get-tuple-element.98.q_ref, bf16[96,4096]{1,0:T(8,128)(2,1)S(1)} %get-tuple-element.99.res_ref, ...), custom_call_target="tpu_custom_call" | custom-call | flops 301989888 | bytes 6000000 | tf_op jit(solution)/shard_map/attend/pallas_call | solution.py:72
  31.0 4.0 %collective-permute-done.3.refs_1_ = bf16[48,4096]{1,0:T(8,128)(2,1)S(1)} collective-permute-done((bf16[48,4096]{1,0:T(8,128)(2,1)S(1)}, bf16[48,4096]{1,0:T(8,128)(2,1)S(1)}, u32[]{:S(2)}, u32[]{:S(2)}) %collective-permute-start.3) | collective-permute-done | bytes 393248 | tf_op jit(solution)/shard_map/ppermute | solution.py:378
  37.9 3.1 %expert.9 = (bf16[48,4096]{1,0:T(8,128)(2,1)S(1)}, bf16[48,4096]{1,0:T(8,128)(2,1)S(1)}) custom-call(bf16[48,4096]{1,0:T(8,128)(2,1)S(1)} %collective-permute-done.8.refs_0_, bf16[48,4096]{1,0:T(8,128)(2,1)S(1)} %collective-permute-done.9.refs_1_, bf16[640,4096]{1,0:T(8,128)(2,1)S(1)} %get-tuple-element.122.refs_2_.refs_1_, ...), custom_call_target="tpu_custom_call" | custom-call | flops 1 | bytes 1 | tf_op jit(solution)/shard_map/expert/pallas_call | solution.py:180
  41.0 3.4 %collective-permute-done.6.refs_0_ = bf16[48,4096]{1,0:T(8,128)(2,1)S(1)} collective-permute-done((bf16[48,4096]{1,0:T(8,128)(2,1)S(1)}, bf16[48,4096]{1,0:T(8,128)(2,1)S(1)}, u32[]{:S(2)}, u32[]{:S(2)}) %collective-permute-start.6) | collective-permute-done | bytes 393248 | tf_op jit(solution)/shard_map/ppermute | solution.py:402
  46.9 5.9 %collective-permute-done.12.refs_0_ = bf16[48,4096]{1,0:T(8,128)(2,1)S(1)} collective-permute-done((bf16[48,4096]{1,0:T(8,128)(2,1)S(1)}, bf16[48,4096]{1,0:T(8,128)(2,1)S(1)}, u32[]{:S(2)}, u32[]{:S(2)}) %collective-permute-start.12) | collective-permute-done | bytes 393248 | tf_op jit(solution)/shard_map/ppermute | solution.py:402
  55.1 3.1 %expert.10 = (bf16[48,4096]{1,0:T(8,128)(2,1)S(1)}, bf16[48,4096]{1,0:T(8,128)(2,1)S(1)}) custom-call(bf16[48,4096]{1,0:T(8,128)(2,1)S(1)} %collective-permute-done.12.refs_0_, bf16[48,4096]{1,0:T(8,128)(2,1)S(1)} %collective-permute-done.13.refs_1_, bf16[640,4096]{1,0:T(8,128)(2,1)S(1)} %get-tuple-element.122.refs_2_.refs_1_, ...), custom_call_target="tpu_custom_call" | custom-call | flops 1 | bytes 1 | tf_op jit(solution)/shard_map/expert/pallas_call | solution.py:180
  58.2 3.1 %expert.11 = (bf16[48,4096]{1,0:T(8,128)(2,1)S(1)}, bf16[48,4096]{1,0:T(8,128)(2,1)S(1)}) custom-call(bf16[48,4096]{1,0:T(8,128)(2,1)S(1)} %collective-permute-done.6.refs_0_, bf16[48,4096]{1,0:T(8,128)(2,1)S(1)} %collective-permute-done.7.refs_1_, bf16[640,4096]{1,0:T(8,128)(2,1)S(1)} %get-tuple-element.122.refs_2_.refs_1_, ...), custom_call_target="tpu_custom_call" | custom-call | flops 1 | bytes 1 | tf_op jit(solution)/shard_map/expert/pallas_call | solution.py:180
  62.4 7.2 %collective-permute-done.14.refs_0_ = bf16[48,4096]{1,0:T(8,128)(2,1)S(1)} collective-permute-done((bf16[48,4096]{1,0:T(8,128)(2,1)S(1)}, bf16[48,4096]{1,0:T(8,128)(2,1)S(1)}, u32[]{:S(2)}, u32[]{:S(2)}) %collective-permute-start.14) | collective-permute-done | bytes 393248 | tf_op jit(solution)/shard_map/ppermute | solution.py:402
  72.6 3.1 %expert.13 = (bf16[48,4096]{1,0:T(8,128)(2,1)S(1)}, bf16[48,4096]{1,0:T(8,128)(2,1)S(1)}) custom-call(bf16[48,4096]{1,0:T(8,128)(2,1)S(1)} %collective-permute-done.14.refs_0_, bf16[48,4096]{1,0:T(8,128)(2,1)S(1)} %collective-permute-done.16.refs_1_, bf16[640,4096]{1,0:T(8,128)(2,1)S(1)} %get-tuple-element.122.refs_2_.refs_1_, ...), custom_call_target="tpu_custom_call" | custom-call | flops 1 | bytes 1 | tf_op jit(solution)/shard_map/expert/pallas_call | solution.py:180
  78.1 2.9 %expert.16 = bf16[48,4096]{1,0:T(8,128)(2,1)S(1)} custom-call(bf16[48,4096]{1,0:T(8,128)(2,1)S(1)} %collective-permute-done.15.refs_0_, bf16[640,4096]{1,0:T(8,128)(2,1)S(1)} %get-tuple-element.122.refs_2_.refs_1_, bf16[640,4096]{1,0:T(8,128)(2,1)S(1)} %get-tuple-element.123.refs_3_.refs_2_), custom_call_target="tpu_custom_call" | custom-call | flops 1 | bytes 1 | tf_op jit(solution)/shard_map/expert/pallas_call | solution.py:180
  82.4 2.9 %expert.17 = bf16[48,4096]{1,0:T(8,128)(2,1)S(1)} custom-call(bf16[48,4096]{1,0:T(8,128)(2,1)S(1)} %collective-permute-done.25.refs_0_, bf16[640,4096]{1,0:T(8,128)(2,1)S(1)} %get-tuple-element.122.refs_2_.refs_1_, bf16[640,4096]{1,0:T(8,128)(2,1)S(1)} %get-tuple-element.123.refs_3_.refs_2_), custom_call_target="tpu_custom_call" | custom-call | flops 1 | bytes 1 | tf_op jit(solution)/shard_map/expert/pallas_call | solution.py:180
  88.4 3.1 %expert.15 = (bf16[48,4096]{1,0:T(8,128)(2,1)S(1)}, bf16[48,4096]{1,0:T(8,128)(2,1)S(1)}) custom-call(bf16[48,4096]{1,0:T(8,128)(2,1)S(1)} %collective-permute-done.22.refs_0_, bf16[48,4096]{1,0:T(8,128)(2,1)S(1)} %collective-permute-done.23.refs_1_, bf16[640,4096]{1,0:T(8,128)(2,1)S(1)} %get-tuple-element.122.refs_2_.refs_1_, ...), custom_call_target="tpu_custom_call" | custom-call | flops 1 | bytes 1 | tf_op jit(solution)/shard_map/expert/pallas_call | solution.py:180
  91.5 3.5 %collective-permute-done.24.refs_2_ = bf16[48,4096]{1,0:T(8,128)(2,1)S(1)} collective-permute-done((bf16[48,4096]{1,0:T(8,128)(2,1)S(1)}, bf16[48,4096]{1,0:T(8,128)(2,1)S(1)}, u32[]{:S(2)}, u32[]{:S(2)}) %collective-permute-start.24) | collective-permute-done | bytes 393248 | tf_op jit(solution)/shard_map/ppermute | solution.py:402
  96.7 3.1 %expert.12 = (bf16[48,4096]{1,0:T(8,128)(2,1)S(1)}, bf16[48,4096]{1,0:T(8,128)(2,1)S(1)}) custom-call(bf16[48,4096]{1,0:T(8,128)(2,1)S(1)} %collective-permute-done.10.refs_0_, bf16[48,4096]{1,0:T(8,128)(2,1)S(1)} %collective-permute-done.11.refs_1_, bf16[640,4096]{1,0:T(8,128)(2,1)S(1)} %get-tuple-element.122.refs_2_.refs_1_, ...), custom_call_target="tpu_custom_call" | custom-call | flops 1 | bytes 1 | tf_op jit(solution)/shard_map/expert/pallas_call | solution.py:180
  99.8 3.5 %collective-permute-done.17.refs_2_ = bf16[48,4096]{1,0:T(8,128)(2,1)S(1)} collective-permute-done((bf16[48,4096]{1,0:T(8,128)(2,1)S(1)}, bf16[48,4096]{1,0:T(8,128)(2,1)S(1)}, u32[]{:S(2)}, u32[]{:S(2)}) %collective-permute-start.17) | collective-permute-done | bytes 393248 | tf_op jit(solution)/shard_map/ppermute | solution.py:402
  105.1 6.7 %collective-permute-done.27.refs_2_ = bf16[48,4096]{1,0:T(8,128)(2,1)S(1)} collective-permute-done((bf16[48,4096]{1,0:T(8,128)(2,1)S(1)}, bf16[48,4096]{1,0:T(8,128)(2,1)S(1)}, u32[]{:S(2)}, u32[]{:S(2)}) %collective-permute-start.27) | collective-permute-done | bytes 393248 | tf_op jit(solution)/shard_map/ppermute | solution.py:402
  113.6 3.1 %expert.14 = (bf16[48,4096]{1,0:T(8,128)(2,1)S(1)}, bf16[48,4096]{1,0:T(8,128)(2,1)S(1)}) custom-call(bf16[48,4096]{1,0:T(8,128)(2,1)S(1)} %get-tuple-element.154.refs_0_, bf16[48,4096]{1,0:T(8,128)(2,1)S(1)} %collective-permute-done.3.refs_1_, bf16[640,4096]{1,0:T(8,128)(2,1)S(1)} %get-tuple-element.122.refs_2_.refs_1_, ...), custom_call_target="tpu_custom_call" | custom-call | flops 1 | bytes 1 | tf_op jit(solution)/shard_map/expert/pallas_call | solution.py:180
  116.7 3.4 %collective-permute-done.19.refs_2_ = bf16[48,4096]{1,0:T(8,128)(2,1)S(1)} collective-permute-done((bf16[48,4096]{1,0:T(8,128)(2,1)S(1)}, bf16[48,4096]{1,0:T(8,128)(2,1)S(1)}, u32[]{:S(2)}, u32[]{:S(2)}) %collective-permute-start.19) | collective-permute-done | bytes 393248 | tf_op jit(solution)/shard_map/ppermute | solution.py:402
  121.8 6.9 %collective-permute-done.29.refs_2_ = bf16[48,4096]{1,0:T(8,128)(2,1)S(1)} collective-permute-done((bf16[48,4096]{1,0:T(8,128)(2,1)S(1)}, bf16[48,4096]{1,0:T(8,128)(2,1)S(1)}, u32[]{:S(2)}, u32[]{:S(2)}) %collective-permute-start.29) | collective-permute-done | bytes 393248 | tf_op jit(solution)/shard_map/ppermute | solution.py:402
  131.6 5.5 %collective-permute-done.33.refs_1_ = bf16[48,4096]{1,0:T(8,128)(2,1)S(1)} collective-permute-done((bf16[48,4096]{1,0:T(8,128)(2,1)S(1)}, bf16[48,4096]{1,0:T(8,128)(2,1)S(1)}, u32[]{:S(2)}, u32[]{:S(2)}) %collective-permute-start.33) | collective-permute-done | bytes 393248 | tf_op jit(solution)/shard_map/ppermute | solution.py:402
  138.3 9.2 %collective-permute-start.36 = (bf16[24,4096]{1,0:T(8,128)(2,1)S(1)}, bf16[24,4096]{1,0:T(8,128)(2,1)S(1)}, u32[]{:S(2)}, u32[]{:S(2)}) collective-permute-start(bf16[24,4096]{1,0:T(8,128)(2,1)S(1)} %get-tuple-element.180), channel_id=1, source_target_pairs={{12,0},{8,4},{4,8},{0,12},{28,16},{24,20},{20,24},{16,28},{13,1},{... | collective-permute-start | bytes 589832 | tf_op jit(solution)/shard_map/ppermute | solution.py:460
  150.2 4.8 %collective-permute-done.36.refs_3_ = bf16[24,4096]{1,0:T(8,128)(2,1)S(1)} collective-permute-done((bf16[24,4096]{1,0:T(8,128)(2,1)S(1)}, bf16[24,4096]{1,0:T(8,128)(2,1)S(1)}, u32[]{:S(2)}, u32[]{:S(2)}) %collective-permute-start.36) | collective-permute-done | bytes 196640 | tf_op jit(solution)/shard_map/ppermute | solution.py:460
  (108 shorter events, 53.9 us)
Async XLA Ops:
  0.0 18.5 %collective-permute-start = (bf16[2,160,1024]{2,1,0:T(8,128)(2,1)}, bf16[2,160,1024]{2,1,0:T(8,128)(2,1)}, u32[]{:S(2)}, u32[]{:S(2)}) collective-permute-start(bf16[2,160,1024]{2,1,0:T(8,128)(2,1)} %bitcast.81), channel_id=1, source_target_pairs={{28,0},{24,4},{4,8},{0,12},{12,16},{8,20},{20,24},{16,28},{29,1},{... | collective-permute-start | bytes 1966088 | tf_op jit(solution)/shard_map/ppermute | solution.py:309
  3.6 15.0 %collective-permute-start.1 = (bf16[2,160,1024]{2,1,0:T(8,128)(2,1)}, bf16[2,160,1024]{2,1,0:T(8,128)(2,1)}, u32[]{:S(2)}, u32[]{:S(2)}) collective-permute-start(bf16[2,160,1024]{2,1,0:T(8,128)(2,1)} %bitcast.82), channel_id=1, source_target_pairs={{24,0},{28,4},{0,8},{4,12},{8,16},{12,20},{16,24},{20,28},{25,1},{... | collective-permute-start | bytes 1966088 | tf_op jit(solution)/shard_map/ppermute | solution.py:310
  12.0 14.2 %collective-permute-start.4 = (bf16[320,4096]{1,0:T(8,128)(2,1)}, bf16[320,4096]{1,0:T(8,128)(2,1)S(1)}, u32[]{:S(2)}, u32[]{:S(2)}) collective-permute-start(bf16[320,4096]{1,0:T(8,128)(2,1)} %get-tuple-element.110), channel_id=1, source_target_pairs={{0,8},{8,0},{16,24},{24,16},{1,9},{9,1},{17,25},{25,17},{2,10},{10... | collective-permute-start | bytes 7864328 | tf_op jit(solution)/shard_map/ppermute | solution.py:333
  12.6 13.6 %collective-permute-start.5 = (bf16[320,4096]{1,0:T(8,128)(2,1)}, bf16[320,4096]{1,0:T(8,128)(2,1)}, u32[]{:S(2)}, u32[]{:S(2)}) collective-permute-start(bf16[320,4096]{1,0:T(8,128)(2,1)} %get-tuple-element.111), channel_id=1, source_target_pairs={{0,8},{8,0},{16,24},{24,16},{1,9},{9,1},{17,25},{25,17},{2,10},{10... | collective-permute-start | bytes 7864328 | tf_op jit(solution)/shard_map/ppermute | solution.py:333
  36.4 16.4 %collective-permute-start.12 = (bf16[48,4096]{1,0:T(8,128)(2,1)S(1)}, bf16[48,4096]{1,0:T(8,128)(2,1)S(1)}, u32[]{:S(2)}, u32[]{:S(2)}) collective-permute-start(bf16[48,4096]{1,0:T(8,128)(2,1)S(1)} %collective-permute-done.8.refs_0_), channel_id=1, source_target_pairs={{0,1},{1,2},{2,3},{3,19},{19,18},{18,17},{17,16},{16,0},{8,9},{9,1... | collective-permute-start | bytes 1179656 | tf_op jit(solution)/shard_map/ppermute | solution.py:402
  37.7 16.1 %collective-permute-start.13 = (bf16[48,4096]{1,0:T(8,128)(2,1)S(1)}, bf16[48,4096]{1,0:T(8,128)(2,1)S(1)}, u32[]{:S(2)}, u32[]{:S(2)}) collective-permute-start(bf16[48,4096]{1,0:T(8,128)(2,1)S(1)} %collective-permute-done.9.refs_1_), channel_id=1, source_target_pairs={{0,16},{1,0},{2,1},{3,2},{19,3},{18,19},{17,18},{16,17},{8,24},{9,... | collective-permute-start | bytes 1179656 | tf_op jit(solution)/shard_map/ppermute | solution.py:402
  45.4 15.9 %collective-permute-start.10 = (bf16[48,4096]{1,0:T(8,128)(2,1)S(1)}, bf16[48,4096]{1,0:T(8,128)(2,1)S(1)}, u32[]{:S(2)}, u32[]{:S(2)}) collective-permute-start(bf16[48,4096]{1,0:T(8,128)(2,1)S(1)} %collective-permute-done.6.refs_0_), channel_id=1, source_target_pairs={{0,1},{1,2},{2,3},{3,19},{19,18},{18,17},{17,16},{16,0},{8,9},{9,1... | collective-permute-start | bytes 1179656 | tf_op jit(solution)/shard_map/ppermute | solution.py:402
  46.7 15.6 %collective-permute-start.11 = (bf16[48,4096]{1,0:T(8,128)(2,1)S(1)}, bf16[48,4096]{1,0:T(8,128)(2,1)S(1)}, u32[]{:S(2)}, u32[]{:S(2)}) collective-permute-start(bf16[48,4096]{1,0:T(8,128)(2,1)S(1)} %collective-permute-done.7.refs_1_), channel_id=1, source_target_pairs={{0,16},{1,0},{2,1},{3,2},{19,3},{18,19},{17,18},{16,17},{8,24},{9,... | collective-permute-start | bytes 1179656 | tf_op jit(solution)/shard_map/ppermute | solution.py:402
  53.8 15.8 %collective-permute-start.14 = (bf16[48,4096]{1,0:T(8,128)(2,1)S(1)}, bf16[48,4096]{1,0:T(8,128)(2,1)S(1)}, u32[]{:S(2)}, u32[]{:S(2)}) collective-permute-start(bf16[48,4096]{1,0:T(8,128)(2,1)S(1)} %collective-permute-done.12.refs_0_), channel_id=1, source_target_pairs={{0,1},{1,2},{2,3},{3,19},{19,18},{18,17},{17,16},{16,0},{8,9},{9,1... | collective-permute-start | bytes 1179656 | tf_op jit(solution)/shard_map/ppermute | solution.py:402
  71.1 16.0 %collective-permute-start.22 = (bf16[48,4096]{1,0:T(8,128)(2,1)S(1)}, bf16[48,4096]{1,0:T(8,128)(2,1)S(1)}, u32[]{:S(2)}, u32[]{:S(2)}) collective-permute-start(bf16[48,4096]{1,0:T(8,128)(2,1)S(1)} %collective-permute-done.13.refs_1_), channel_id=1, source_target_pairs={{0,16},{1,0},{2,1},{3,2},{19,3},{18,19},{17,18},{16,17},{8,24},{9,... | collective-permute-start | bytes 1179656 | tf_op jit(solution)/shard_map/ppermute | solution.py:402
  72.3 16.1 %collective-permute-start.23 = (bf16[48,4096]{1,0:T(8,128)(2,1)S(1)}, bf16[48,4096]{1,0:T(8,128)(2,1)S(1)}, u32[]{:S(2)}, u32[]{:S(2)}) collective-permute-start(bf16[48,4096]{1,0:T(8,128)(2,1)S(1)} %collective-permute-done.10.refs_0_), channel_id=1, source_target_pairs={{0,1},{1,2},{2,3},{3,19},{19,18},{18,17},{17,16},{16,0},{8,9},{9,1... | collective-permute-start | bytes 1179656 | tf_op jit(solution)/shard_map/ppermute | solution.py:402
  81.1 13.9 %collective-permute-start.24 = (bf16[48,4096]{1,0:T(8,128)(2,1)S(1)}, bf16[48,4096]{1,0:T(8,128)(2,1)S(1)}, u32[]{:S(2)}, u32[]{:S(2)}) collective-permute-start(bf16[48,4096]{1,0:T(8,128)(2,1)S(1)} %expert.16), channel_id=1, source_target_pairs={{0,1},{1,2},{2,3},{3,19},{19,18},{18,17},{17,16},{16,0},{8,9},{9,1... | collective-permute-start | bytes 1179656 | tf_op jit(solution)/shard_map/ppermute | solution.py:402
  85.6 17.7 %collective-permute-start.17 = (bf16[48,4096]{1,0:T(8,128)(2,1)S(1)}, bf16[48,4096]{1,0:T(8,128)(2,1)S(1)}, u32[]{:S(2)}, u32[]{:S(2)}) collective-permute-start(bf16[48,4096]{1,0:T(8,128)(2,1)S(1)} %get-tuple-element.146), channel_id=1, source_target_pairs={{0,16},{1,0},{2,1},{3,2},{19,3},{18,19},{17,18},{16,17},{8,24},{9,... | collective-permute-start | bytes 1179656 | tf_op jit(solution)/shard_map/ppermute | solution.py:402
  87.1 16.3 %collective-permute-start.18 = (bf16[48,4096]{1,0:T(8,128)(2,1)S(1)}, bf16[48,4096]{1,0:T(8,128)(2,1)S(1)}, u32[]{:S(2)}, u32[]{:S(2)}) collective-permute-start(bf16[48,4096]{1,0:T(8,128)(2,1)S(1)} %get-tuple-element.147), channel_id=1, source_target_pairs={{0,1},{1,2},{2,3},{3,19},{19,18},{18,17},{17,16},{16,0},{8,9},{9,1... | collective-permute-start | bytes 1179656 | tf_op jit(solution)/shard_map/ppermute | solution.py:402
  95.2 16.7 %collective-permute-start.27 = (bf16[48,4096]{1,0:T(8,128)(2,1)S(1)}, bf16[48,4096]{1,0:T(8,128)(2,1)S(1)}, u32[]{:S(2)}, u32[]{:S(2)}) collective-permute-start(bf16[48,4096]{1,0:T(8,128)(2,1)S(1)} %get-tuple-element.169), channel_id=1, source_target_pairs={{0,1},{1,2},{2,3},{3,19},{19,18},{18,17},{17,16},{16,0},{8,9},{9,1... | collective-permute-start | bytes 1179656 | tf_op jit(solution)/shard_map/ppermute | solution.py:402
  96.5 15.3 %collective-permute-start.28 = (bf16[48,4096]{1,0:T(8,128)(2,1)S(1)}, bf16[48,4096]{1,0:T(8,128)(2,1)S(1)}, u32[]{:S(2)}, u32[]{:S(2)}) collective-permute-start(bf16[48,4096]{1,0:T(8,128)(2,1)S(1)} %get-tuple-element.170), channel_id=1, source_target_pairs={{0,16},{1,0},{2,1},{3,2},{19,3},{18,19},{17,18},{16,17},{8,24},{9,... | collective-permute-start | bytes 1179656 | tf_op jit(solution)/shard_map/ppermute | solution.py:402
  103.6 16.5 %collective-permute-start.19 = (bf16[48,4096]{1,0:T(8,128)(2,1)S(1)}, bf16[48,4096]{1,0:T(8,128)(2,1)S(1)}, u32[]{:S(2)}, u32[]{:S(2)}) collective-permute-start(bf16[48,4096]{1,0:T(8,128)(2,1)S(1)} %get-tuple-element.150), channel_id=1, source_target_pairs={{0,16},{1,0},{2,1},{3,2},{19,3},{18,19},{17,18},{16,17},{8,24},{9,... | collective-permute-start | bytes 1179656 | tf_op jit(solution)/shard_map/ppermute | solution.py:402
  104.9 15.4 %collective-permute-start.20 = (bf16[48,4096]{1,0:T(8,128)(2,1)S(1)}, bf16[48,4096]{1,0:T(8,128)(2,1)S(1)}, u32[]{:S(2)}, u32[]{:S(2)}) collective-permute-start(bf16[48,4096]{1,0:T(8,128)(2,1)S(1)} %get-tuple-element.151), channel_id=1, source_target_pairs={{0,1},{1,2},{2,3},{3,19},{19,18},{18,17},{17,16},{16,0},{8,9},{9,1... | collective-permute-start | bytes 1179656 | tf_op jit(solution)/shard_map/ppermute | solution.py:402
  112.0 16.7 %collective-permute-start.29 = (bf16[48,4096]{1,0:T(8,128)(2,1)S(1)}, bf16[48,4096]{1,0:T(8,128)(2,1)S(1)}, u32[]{:S(2)}, u32[]{:S(2)}) collective-permute-start(bf16[48,4096]{1,0:T(8,128)(2,1)S(1)} %get-tuple-element.171), channel_id=1, source_target_pairs={{0,1},{1,2},{2,3},{3,19},{19,18},{18,17},{17,16},{16,0},{8,9},{9,1... | collective-permute-start | bytes 1179656 | tf_op jit(solution)/shard_map/ppermute | solution.py:402
  113.4 15.3 %collective-permute-start.30 = (bf16[48,4096]{1,0:T(8,128)(2,1)S(1)}, bf16[48,4096]{1,0:T(8,128)(2,1)S(1)}, u32[]{:S(2)}, u32[]{:S(2)}) collective-permute-start(bf16[48,4096]{1,0:T(8,128)(2,1)S(1)} %get-tuple-element.172), channel_id=1, source_target_pairs={{0,16},{1,0},{2,1},{3,2},{19,3},{18,19},{17,18},{16,17},{8,24},{9,... | collective-permute-start | bytes 1179656 | tf_op jit(solution)/shard_map/ppermute | solution.py:402
  120.5 16.7 %collective-permute-start.33 = (bf16[48,4096]{1,0:T(8,128)(2,1)S(1)}, bf16[48,4096]{1,0:T(8,128)(2,1)S(1)}, u32[]{:S(2)}, u32[]{:S(2)}) collective-permute-start(bf16[48,4096]{1,0:T(8,128)(2,1)S(1)} %get-tuple-element.177), channel_id=1, source_target_pairs={{0,1},{1,2},{2,3},{3,19},{19,18},{18,17},{17,16},{16,0},{8,9},{9,1... | collective-permute-start | bytes 1179656 | tf_op jit(solution)/shard_map/ppermute | solution.py:402
  130.1 17.4 %collective-permute-start.21 = (bf16[48,4096]{1,0:T(8,128)(2,1)S(1)}, bf16[48,4096]{1,0:T(8,128)(2,1)S(1)}, u32[]{:S(2)}, u32[]{:S(2)}) collective-permute-start(bf16[48,4096]{1,0:T(8,128)(2,1)S(1)} %get-tuple-element.159), channel_id=1, source_target_pairs={{0,16},{1,0},{2,1},{3,2},{19,3},{18,19},{17,18},{16,17},{8,24},{9,... | collective-permute-start | bytes 1179656 | tf_op jit(solution)/shard_map/ppermute | solution.py:402
  131.4 16.1 %collective-permute-start.31 = (bf16[48,4096]{1,0:T(8,128)(2,1)S(1)}, bf16[48,4096]{1,0:T(8,128)(2,1)S(1)}, u32[]{:S(2)}, u32[]{:S(2)}) collective-permute-start(bf16[48,4096]{1,0:T(8,128)(2,1)S(1)} %get-tuple-element.173), channel_id=1, source_target_pairs={{0,1},{1,2},{2,3},{3,19},{19,18},{18,17},{17,16},{16,0},{8,9},{9,1... | collective-permute-start | bytes 1179656 | tf_op jit(solution)/shard_map/ppermute | solution.py:402
  138.3 16.7 %collective-permute-start.36 = (bf16[24,4096]{1,0:T(8,128)(2,1)S(1)}, bf16[24,4096]{1,0:T(8,128)(2,1)S(1)}, u32[]{:S(2)}, u32[]{:S(2)}) collective-permute-start(bf16[24,4096]{1,0:T(8,128)(2,1)S(1)} %get-tuple-element.180), channel_id=1, source_target_pairs={{12,0},{8,4},{4,8},{0,12},{28,16},{24,20},{20,24},{16,28},{13,1},{... | collective-permute-start | bytes 589832 | tf_op jit(solution)/shard_map/ppermute | solution.py:460
  (24 other events, 208.9 us)

commit v3 on v2

--- a/solution.py
+++ b/solution.py
@@ -412,45 +412,51 @@
                 rows, sums[key] = lax.optimization_barrier((rows, sums[key]))
         return rows
 
+    def sums_of(*rows):
+        return expert_sums(list(rows), unit_in, unit_out)
+
     for k in range(1, half):
         for p in range(2):
-            rows = lax.optimization_barrier((fore[p][-1], rear[p][-1]))
+            rows = (fore[p][-1], rear[p][-1])
+            rows = lax.optimization_barrier(rows)
             if p == 1:
                 rows = after([(0, k - 1), (1, k - 2)], rows)
             fore[p].append(hop(rows[0], 1))
             rear[p].append(hop(rows[1], -1))
             if k < half - 1:
-                sums[p, k] = expert_sums([fore[p][k], rear[p][k]], unit_in, unit_out)
+                sums[p, k] = sums_of(fore[p][k], rear[p][k])
     fore[0].append(hop(fore[0][-1], 1))
     rear[1].append(hop(rear[1][-1], -1))
     ahead_part, behind_part = [{}, {}], [{}, {}]
     for (p, k), got in sums.items():
         behind_part[p][k], ahead_part[p][k] = got
     k = half - 1
-    behind_part[0][k], ahead_part[1][k] = expert_sums(
-        [fore[0][k], rear[1][k]], unit_in, unit_out
-    )
-    ahead_part[0][k], behind_part[1][k] = expert_sums(
-        [rear[0][k], fore[1][k]], unit_in, unit_out
-    )
+    behind_part[0][k], ahead_part[1][k] = sums_of(fore[0][k], rear[1][k])
+    ahead_part[0][k], behind_part[1][k] = sums_of(rear[0][k], fore[1][k])
     lead = [behind_part[0][k], ahead_part[1][k]]
     fore[0][half], lead = lax.optimization_barrier((fore[0][half], lead))
     behind_part[0][k], ahead_part[1][k] = lead
-    ahead_part[0][half] = expert_sums([fore[0][half]], unit_in, unit_out)[0]
-    behind_part[1][half] = expert_sums([rear[1][half]], unit_in, unit_out)[0]
+    ahead_part[0][half] = sums_of(fore[0][half])[0]
+    behind_part[1][half] = sums_of(rear[1][half])[0]
 
     short = [hop(behind_part[0][half - 1], -1), hop(ahead_part[1][half - 1], 1)]
     long = [hop(ahead_part[0][half], 1), hop(behind_part[1][half], -1)]
-    (short, parts) = lax.optimization_barrier((short, parts))
-    own = expert_sums(parts, unit_in, unit_out)
+    short, parts = lax.optimization_barrier((short, parts))
+    own = sums_of(*parts)
     for k in range(half - 1, 0, -1):
         if k < half - 1:
+            if k == 1:
+                short, own = lax.optimization_barrier((short, own))
             totals = add_sums([behind_part[0][k], ahead_part[1][k]], short)
-            if k == 1:
-                totals, own = lax.optimization_barrier((totals, own))
             short = [hop(totals[0], -1), hop(totals[1], 1)]
-        totals = add_sums([ahead_part[0][k], behind_part[1][k]], long)
-        long = [hop(totals[0], 1), hop(totals[1], -1)]
+        if k > 1:
+            totals = add_sums([ahead_part[0][k], behind_part[1][k]], long)
+            long = [hop(totals[0], 1), hop(totals[1], -1)]
+        else:
+            far = hop(finish_sums(behind_part[1][k], long[1])[0], -1)
+            near = hop(finish_sums(ahead_part[0][k], long[0])[0], 1)
+            long = [near, far]
+
     def cross(rows, dq, dc):
         pairs = [
             ((a ^ dc) * seqs + (b + dq) % seqs, a * seqs + b)

time: 157 us -> 157 us (level)
  no operation moved by 1% of the time
where the time goes in v3:
time: 157 us; the launch traced here: 156 us
  waiting for transfers between devices  66.2 us (42%)
  starting transfers between devices  40.5 us (26%)
  Pallas kernels  38.4 us (24%)
  local copies, waits for them, and re-layouts  8.71 us (6%)
    ppermute x28, waiting for transfers between devices, hop(): return lax.ppermute(rows, ('section', 'expert'), pairs)  52.9 us
    pallas_call x9, Pallas kernels, expert_sums(): pl.pallas_call(functools.partial(expert_kernel, len(parts)), out_shape=[j...  27.5 us
    ppermute x28, starting transfers between devices, hop(): return lax.ppermute(rows, ('section', 'expert'), pairs)  22.2 us
    ppermute x3, starting transfers between devices, cross(): return lax.ppermute(rows, ('section', 'seq'), pairs)  12.7 us
    unnamed x22, local copies, waits for them, and re-layouts  8.61 us
    pallas_call x3, Pallas kernels, staged(): pl.pallas_call(kernel, out_shape=outs, in_specs=[pl.BlockSpec(memory_spac...  5.13 us
    ppermute x3, waiting for transfers between devices, cross(): return lax.ppermute(rows, ('section', 'seq'), pairs)  4.8 us
    ppermute x1, waiting for transfers between devices, seq_move(): lax.ppermute(rows, 'seq', [(b, (b + step) % seqs) for b in range(seqs)])  3.98 us
  transfers between devices with their start and end apart: 37, of which 20 were waited for; matrix products, arithmetic and copies ran while one was open for 1% of the time, Pallas kernels for 24%

profile of v3, /device:TPU:1, one launch (start us, length us, event | category | flops | bytes accessed | tf_op | source)
XLA Modules:
  0.0 156.3 jit_solution(5981780645176060996)
XLA Ops:
  0.0 3.6 %collective-permute-start = (bf16[2,160,1024]{2,1,0:T(8,128)(2,1)}, bf16[2,160,1024]{2,1,0:T(8,128)(2,1)}, u32[]{:S(2)}, u32[]{:S(2)}) collective-permute-start(bf16[2,160,1024]{2,1,0:T(8,128)(2,1)} %bitcast.81), channel_id=1, source_target_pairs={{28,0},{24,4},{4,8},{0,12},{12,16},{8,20},{20,24},{16,28},{29,1},{... | collective-permute-start | bytes 1966088 | tf_op jit(solution)/shard_map/ppermute | solution.py:309
  15.4 3.1 %collective-permute-done.refs_0_ = bf16[2,160,1024]{2,1,0:T(8,128)(2,1)} collective-permute-done((bf16[2,160,1024]{2,1,0:T(8,128)(2,1)}, bf16[2,160,1024]{2,1,0:T(8,128)(2,1)}, u32[]{:S(2)}, u32[]{:S(2)}) %collective-permute-start) | collective-permute-done | bytes 655392 | tf_op jit(solution)/shard_map/ppermute | solution.py:309
  18.5 3.2 %attend.1 = (f32[96,4096]{1,0:T(8,128)S(1)}, bf16[48,4096]{1,0:T(8,128)(2,1)S(1)}, bf16[24,4096]{1,0:T(8,128)(2,1)S(1)}, bf16[24,4096]{1,0:T(8,128)(2,1)S(1)}) custom-call(s32[2]{0:T(128)S(1)} %pad_add_fusion.rel_ref, bf16[96,4096]{1,0:T(8,128)(2,1)S(1)} %get-tuple-element.96.q_ref, bf16[96,4096]{1,0:T(8,128)(2,1)S(1)} %get-tuple-element.97.res_ref, ...), custom_call_target="tpu_custom_call" | custom-call | flops 301989888 | bytes 6000000 | tf_op jit(solution)/shard_map/attend/pallas_call | solution.py:72
  31.0 4.0 %collective-permute-done.3.refs_1_ = bf16[48,4096]{1,0:T(8,128)(2,1)S(1)} collective-permute-done((bf16[48,4096]{1,0:T(8,128)(2,1)S(1)}, bf16[48,4096]{1,0:T(8,128)(2,1)S(1)}, u32[]{:S(2)}, u32[]{:S(2)}) %collective-permute-start.3) | collective-permute-done | bytes 393248 | tf_op jit(solution)/shard_map/ppermute | solution.py:378
  37.9 3.1 %expert.9 = (bf16[48,4096]{1,0:T(8,128)(2,1)S(1)}, bf16[48,4096]{1,0:T(8,128)(2,1)S(1)}) custom-call(bf16[48,4096]{1,0:T(8,128)(2,1)S(1)} %collective-permute-done.8.refs_0_, bf16[48,4096]{1,0:T(8,128)(2,1)S(1)} %collective-permute-done.9.refs_1_, bf16[640,4096]{1,0:T(8,128)(2,1)S(1)} %get-tuple-element.120.refs_2_.refs_1_, ...), custom_call_target="tpu_custom_call" | custom-call | flops 1 | bytes 1 | tf_op jit(solution)/shard_map/expert/pallas_call | solution.py:180
  41.0 3.4 %collective-permute-done.6.refs_0_ = bf16[48,4096]{1,0:T(8,128)(2,1)S(1)} collective-permute-done((bf16[48,4096]{1,0:T(8,128)(2,1)S(1)}, bf16[48,4096]{1,0:T(8,128)(2,1)S(1)}, u32[]{:S(2)}, u32[]{:S(2)}) %collective-permute-start.6) | collective-permute-done | bytes 393248 | tf_op jit(solution)/shard_map/ppermute | solution.py:402
  46.9 5.9 %collective-permute-done.12.refs_0_ = bf16[48,4096]{1,0:T(8,128)(2,1)S(1)} collective-permute-done((bf16[48,4096]{1,0:T(8,128)(2,1)S(1)}, bf16[48,4096]{1,0:T(8,128)(2,1)S(1)}, u32[]{:S(2)}, u32[]{:S(2)}) %collective-permute-start.12) | collective-permute-done | bytes 393248 | tf_op jit(solution)/shard_map/ppermute | solution.py:402
  55.1 3.1 %expert.10 = (bf16[48,4096]{1,0:T(8,128)(2,1)S(1)}, bf16[48,4096]{1,0:T(8,128)(2,1)S(1)}) custom-call(bf16[48,4096]{1,0:T(8,128)(2,1)S(1)} %collective-permute-done.12.refs_0_, bf16[48,4096]{1,0:T(8,128)(2,1)S(1)} %collective-permute-done.13.refs_1_, bf16[640,4096]{1,0:T(8,128)(2,1)S(1)} %get-tuple-element.120.refs_2_.refs_1_, ...), custom_call_target="tpu_custom_call" | custom-call | flops 1 | bytes 1 | tf_op jit(solution)/shard_map/expert/pallas_call | solution.py:180
  58.2 3.1 %expert.12 = (bf16[48,4096]{1,0:T(8,128)(2,1)S(1)}, bf16[48,4096]{1,0:T(8,128)(2,1)S(1)}) custom-call(bf16[48,4096]{1,0:T(8,128)(2,1)S(1)} %collective-permute-done.6.refs_0_, bf16[48,4096]{1,0:T(8,128)(2,1)S(1)} %collective-permute-done.7.refs_1_, bf16[640,4096]{1,0:T(8,128)(2,1)S(1)} %get-tuple-element.120.refs_2_.refs_1_, ...), custom_call_target="tpu_custom_call" | custom-call | flops 1 | bytes 1 | tf_op jit(solution)/shard_map/expert/pallas_call | solution.py:180
  62.4 7.2 %collective-permute-done.14.refs_0_ = bf16[48,4096]{1,0:T(8,128)(2,1)S(1)} collective-permute-done((bf16[48,4096]{1,0:T(8,128)(2,1)S(1)}, bf16[48,4096]{1,0:T(8,128)(2,1)S(1)}, u32[]{:S(2)}, u32[]{:S(2)}) %collective-permute-start.14) | collective-permute-done | bytes 393248 | tf_op jit(solution)/shard_map/ppermute | solution.py:402
  72.6 3.1 %expert.13 = (bf16[48,4096]{1,0:T(8,128)(2,1)S(1)}, bf16[48,4096]{1,0:T(8,128)(2,1)S(1)}) custom-call(bf16[48,4096]{1,0:T(8,128)(2,1)S(1)} %collective-permute-done.14.refs_0_, bf16[48,4096]{1,0:T(8,128)(2,1)S(1)} %collective-permute-done.16.refs_1_, bf16[640,4096]{1,0:T(8,128)(2,1)S(1)} %get-tuple-element.120.refs_2_.refs_1_, ...), custom_call_target="tpu_custom_call" | custom-call | flops 1 | bytes 1 | tf_op jit(solution)/shard_map/expert/pallas_call | solution.py:180
  78.1 2.9 %expert.16 = bf16[48,4096]{1,0:T(8,128)(2,1)S(1)} custom-call(bf16[48,4096]{1,0:T(8,128)(2,1)S(1)} %collective-permute-done.15.refs_0_, bf16[640,4096]{1,0:T(8,128)(2,1)S(1)} %get-tuple-element.120.refs_2_.refs_1_, bf16[640,4096]{1,0:T(8,128)(2,1)S(1)} %get-tuple-element.121.refs_3_.refs_2_), custom_call_target="tpu_custom_call" | custom-call | flops 1 | bytes 1 | tf_op jit(solution)/shard_map/expert/pallas_call | solution.py:180
  82.4 2.9 %expert.17 = bf16[48,4096]{1,0:T(8,128)(2,1)S(1)} custom-call(bf16[48,4096]{1,0:T(8,128)(2,1)S(1)} %collective-permute-done.25.refs_0_, bf16[640,4096]{1,0:T(8,128)(2,1)S(1)} %get-tuple-element.120.refs_2_.refs_1_, bf16[640,4096]{1,0:T(8,128)(2,1)S(1)} %get-tuple-element.121.refs_3_.refs_2_), custom_call_target="tpu_custom_call" | custom-call | flops 1 | bytes 1 | tf_op jit(solution)/shard_map/expert/pallas_call | solution.py:180
  88.4 3.1 %expert.15 = (bf16[48,4096]{1,0:T(8,128)(2,1)S(1)}, bf16[48,4096]{1,0:T(8,128)(2,1)S(1)}) custom-call(bf16[48,4096]{1,0:T(8,128)(2,1)S(1)} %collective-permute-done.22.refs_0_, bf16[48,4096]{1,0:T(8,128)(2,1)S(1)} %collective-permute-done.23.refs_1_, bf16[640,4096]{1,0:T(8,128)(2,1)S(1)} %get-tuple-element.120.refs_2_.refs_1_, ...), custom_call_target="tpu_custom_call" | custom-call | flops 1 | bytes 1 | tf_op jit(solution)/shard_map/expert/pallas_call | solution.py:180
  91.5 3.5 %collective-permute-done.24.refs_2_ = bf16[48,4096]{1,0:T(8,128)(2,1)S(1)} collective-permute-done((bf16[48,4096]{1,0:T(8,128)(2,1)S(1)}, bf16[48,4096]{1,0:T(8,128)(2,1)S(1)}, u32[]{:S(2)}, u32[]{:S(2)}) %collective-permute-start.24) | collective-permute-done | bytes 393248 | tf_op jit(solution)/shard_map/ppermute | solution.py:402
  96.7 3.1 %expert.11 = (bf16[48,4096]{1,0:T(8,128)(2,1)S(1)}, bf16[48,4096]{1,0:T(8,128)(2,1)S(1)}) custom-call(bf16[48,4096]{1,0:T(8,128)(2,1)S(1)} %collective-permute-done.10.refs_0_, bf16[48,4096]{1,0:T(8,128)(2,1)S(1)} %collective-permute-done.11.refs_1_, bf16[640,4096]{1,0:T(8,128)(2,1)S(1)} %get-tuple-element.120.refs_2_.refs_1_, ...), custom_call_target="tpu_custom_call" | custom-call | flops 1 | bytes 1 | tf_op jit(solution)/shard_map/expert/pallas_call | solution.py:180
  99.8 3.5 %collective-permute-done.17.refs_2_ = bf16[48,4096]{1,0:T(8,128)(2,1)S(1)} collective-permute-done((bf16[48,4096]{1,0:T(8,128)(2,1)S(1)}, bf16[48,4096]{1,0:T(8,128)(2,1)S(1)}, u32[]{:S(2)}, u32[]{:S(2)}) %collective-permute-start.17) | collective-permute-done | bytes 393248 | tf_op jit(solution)/shard_map/ppermute | solution.py:402
  105.1 6.7 %collective-permute-done.27.refs_2_ = bf16[48,4096]{1,0:T(8,128)(2,1)S(1)} collective-permute-done((bf16[48,4096]{1,0:T(8,128)(2,1)S(1)}, bf16[48,4096]{1,0:T(8,128)(2,1)S(1)}, u32[]{:S(2)}, u32[]{:S(2)}) %collective-permute-start.27) | collective-permute-done | bytes 393248 | tf_op jit(solution)/shard_map/ppermute | solution.py:402
  113.7 3.1 %expert.14 = (bf16[48,4096]{1,0:T(8,128)(2,1)S(1)}, bf16[48,4096]{1,0:T(8,128)(2,1)S(1)}) custom-call(bf16[48,4096]{1,0:T(8,128)(2,1)S(1)} %get-tuple-element.148.refs_0_, bf16[48,4096]{1,0:T(8,128)(2,1)S(1)} %collective-permute-done.3.refs_1_, bf16[640,4096]{1,0:T(8,128)(2,1)S(1)} %get-tuple-element.120.refs_2_.refs_1_, ...), custom_call_target="tpu_custom_call" | custom-call | flops 1 | bytes 1 | tf_op jit(solution)/shard_map/expert/pallas_call | solution.py:180
  116.8 3.3 %collective-permute-done.19.refs_2_ = bf16[48,4096]{1,0:T(8,128)(2,1)S(1)} collective-permute-done((bf16[48,4096]{1,0:T(8,128)(2,1)S(1)}, bf16[48,4096]{1,0:T(8,128)(2,1)S(1)}, u32[]{:S(2)}, u32[]{:S(2)}) %collective-permute-start.19) | collective-permute-done | bytes 393248 | tf_op jit(solution)/shard_map/ppermute | solution.py:402
  121.8 6.7 %collective-permute-done.33.refs_1_ = bf16[48,4096]{1,0:T(8,128)(2,1)S(1)} collective-permute-done((bf16[48,4096]{1,0:T(8,128)(2,1)S(1)}, bf16[48,4096]{1,0:T(8,128)(2,1)S(1)}, u32[]{:S(2)}, u32[]{:S(2)}) %collective-permute-start.33) | collective-permute-done | bytes 393248 | tf_op jit(solution)/shard_map/ppermute | solution.py:402
  130.5 6.7 %collective-permute-done.32.refs_1_ = bf16[48,4096]{1,0:T(8,128)(2,1)S(1)} collective-permute-done((bf16[48,4096]{1,0:T(8,128)(2,1)S(1)}, bf16[48,4096]{1,0:T(8,128)(2,1)S(1)}, u32[]{:S(2)}, u32[]{:S(2)}) %collective-permute-start.32) | collective-permute-done | bytes 393248 | tf_op jit(solution)/shard_map/ppermute | solution.py:402
  138.3 9.2 %collective-permute-start.36 = (bf16[24,4096]{1,0:T(8,128)(2,1)S(1)}, bf16[24,4096]{1,0:T(8,128)(2,1)S(1)}, u32[]{:S(2)}, u32[]{:S(2)}) collective-permute-start(bf16[24,4096]{1,0:T(8,128)(2,1)S(1)} %get-tuple-element.176), channel_id=1, source_target_pairs={{12,0},{8,4},{4,8},{0,12},{28,16},{24,20},{20,24},{16,28},{13,1},{... | collective-permute-start | bytes 589832 | tf_op jit(solution)/shard_map/ppermute | solution.py:466
  150.2 4.8 %collective-permute-done.36.refs_3_ = bf16[24,4096]{1,0:T(8,128)(2,1)S(1)} collective-permute-done((bf16[24,4096]{1,0:T(8,128)(2,1)S(1)}, bf16[24,4096]{1,0:T(8,128)(2,1)S(1)}, u32[]{:S(2)}, u32[]{:S(2)}) %collective-permute-start.36) | collective-permute-done | bytes 196640 | tf_op jit(solution)/shard_map/ppermute | solution.py:466
  (109 shorter events, 53.0 us)
Async XLA Ops:
  0.0 18.5 %collective-permute-start = (bf16[2,160,1024]{2,1,0:T(8,128)(2,1)}, bf16[2,160,1024]{2,1,0:T(8,128)(2,1)}, u32[]{:S(2)}, u32[]{:S(2)}) collective-permute-start(bf16[2,160,1024]{2,1,0:T(8,128)(2,1)} %bitcast.81), channel_id=1, source_target_pairs={{28,0},{24,4},{4,8},{0,12},{12,16},{8,20},{20,24},{16,28},{29,1},{... | collective-permute-start | bytes 1966088 | tf_op jit(solution)/shard_map/ppermute | solution.py:309
  3.6 15.0 %collective-permute-start.1 = (bf16[2,160,1024]{2,1,0:T(8,128)(2,1)}, bf16[2,160,1024]{2,1,0:T(8,128)(2,1)}, u32[]{:S(2)}, u32[]{:S(2)}) collective-permute-start(bf16[2,160,1024]{2,1,0:T(8,128)(2,1)} %bitcast.82), channel_id=1, source_target_pairs={{24,0},{28,4},{0,8},{4,12},{8,16},{12,20},{16,24},{20,28},{25,1},{... | collective-permute-start | bytes 1966088 | tf_op jit(solution)/shard_map/ppermute | solution.py:310
  12.0 14.2 %collective-permute-start.4 = (bf16[320,4096]{1,0:T(8,128)(2,1)}, bf16[320,4096]{1,0:T(8,128)(2,1)S(1)}, u32[]{:S(2)}, u32[]{:S(2)}) collective-permute-start(bf16[320,4096]{1,0:T(8,128)(2,1)} %get-tuple-element.108), channel_id=1, source_target_pairs={{0,8},{8,0},{16,24},{24,16},{1,9},{9,1},{17,25},{25,17},{2,10},{10... | collective-permute-start | bytes 7864328 | tf_op jit(solution)/shard_map/ppermute | solution.py:333
  12.6 13.6 %collective-permute-start.5 = (bf16[320,4096]{1,0:T(8,128)(2,1)}, bf16[320,4096]{1,0:T(8,128)(2,1)}, u32[]{:S(2)}, u32[]{:S(2)}) collective-permute-start(bf16[320,4096]{1,0:T(8,128)(2,1)} %get-tuple-element.109), channel_id=1, source_target_pairs={{0,8},{8,0},{16,24},{24,16},{1,9},{9,1},{17,25},{25,17},{2,10},{10... | collective-permute-start | bytes 7864328 | tf_op jit(solution)/shard_map/ppermute | solution.py:333
  36.4 16.4 %collective-permute-start.12 = (bf16[48,4096]{1,0:T(8,128)(2,1)S(1)}, bf16[48,4096]{1,0:T(8,128)(2,1)S(1)}, u32[]{:S(2)}, u32[]{:S(2)}) collective-permute-start(bf16[48,4096]{1,0:T(8,128)(2,1)S(1)} %collective-permute-done.8.refs_0_), channel_id=1, source_target_pairs={{0,1},{1,2},{2,3},{3,19},{19,18},{18,17},{17,16},{16,0},{8,9},{9,1... | collective-permute-start | bytes 1179656 | tf_op jit(solution)/shard_map/ppermute | solution.py:402
  37.7 16.1 %collective-permute-start.13 = (bf16[48,4096]{1,0:T(8,128)(2,1)S(1)}, bf16[48,4096]{1,0:T(8,128)(2,1)S(1)}, u32[]{:S(2)}, u32[]{:S(2)}) collective-permute-start(bf16[48,4096]{1,0:T(8,128)(2,1)S(1)} %collective-permute-done.9.refs_1_), channel_id=1, source_target_pairs={{0,16},{1,0},{2,1},{3,2},{19,3},{18,19},{17,18},{16,17},{8,24},{9,... | collective-permute-start | bytes 1179656 | tf_op jit(solution)/shard_map/ppermute | solution.py:402
  45.4 15.9 %collective-permute-start.10 = (bf16[48,4096]{1,0:T(8,128)(2,1)S(1)}, bf16[48,4096]{1,0:T(8,128)(2,1)S(1)}, u32[]{:S(2)}, u32[]{:S(2)}) collective-permute-start(bf16[48,4096]{1,0:T(8,128)(2,1)S(1)} %collective-permute-done.6.refs_0_), channel_id=1, source_target_pairs={{0,1},{1,2},{2,3},{3,19},{19,18},{18,17},{17,16},{16,0},{8,9},{9,1... | collective-permute-start | bytes 1179656 | tf_op jit(solution)/shard_map/ppermute | solution.py:402
  46.7 15.6 %collective-permute-start.11 = (bf16[48,4096]{1,0:T(8,128)(2,1)S(1)}, bf16[48,4096]{1,0:T(8,128)(2,1)S(1)}, u32[]{:S(2)}, u32[]{:S(2)}) collective-permute-start(bf16[48,4096]{1,0:T(8,128)(2,1)S(1)} %collective-permute-done.7.refs_1_), channel_id=1, source_target_pairs={{0,16},{1,0},{2,1},{3,2},{19,3},{18,19},{17,18},{16,17},{8,24},{9,... | collective-permute-start | bytes 1179656 | tf_op jit(solution)/shard_map/ppermute | solution.py:402
  53.8 15.8 %collective-permute-start.14 = (bf16[48,4096]{1,0:T(8,128)(2,1)S(1)}, bf16[48,4096]{1,0:T(8,128)(2,1)S(1)}, u32[]{:S(2)}, u32[]{:S(2)}) collective-permute-start(bf16[48,4096]{1,0:T(8,128)(2,1)S(1)} %collective-permute-done.12.refs_0_), channel_id=1, source_target_pairs={{0,1},{1,2},{2,3},{3,19},{19,18},{18,17},{17,16},{16,0},{8,9},{9,1... | collective-permute-start | bytes 1179656 | tf_op jit(solution)/shard_map/ppermute | solution.py:402
  71.1 16.0 %collective-permute-start.22 = (bf16[48,4096]{1,0:T(8,128)(2,1)S(1)}, bf16[48,4096]{1,0:T(8,128)(2,1)S(1)}, u32[]{:S(2)}, u32[]{:S(2)}) collective-permute-start(bf16[48,4096]{1,0:T(8,128)(2,1)S(1)} %collective-permute-done.13.refs_1_), channel_id=1, source_target_pairs={{0,16},{1,0},{2,1},{3,2},{19,3},{18,19},{17,18},{16,17},{8,24},{9,... | collective-permute-start | bytes 1179656 | tf_op jit(solution)/shard_map/ppermute | solution.py:402
  72.3 16.1 %collective-permute-start.23 = (bf16[48,4096]{1,0:T(8,128)(2,1)S(1)}, bf16[48,4096]{1,0:T(8,128)(2,1)S(1)}, u32[]{:S(2)}, u32[]{:S(2)}) collective-permute-start(bf16[48,4096]{1,0:T(8,128)(2,1)S(1)} %collective-permute-done.10.refs_0_), channel_id=1, source_target_pairs={{0,1},{1,2},{2,3},{3,19},{19,18},{18,17},{17,16},{16,0},{8,9},{9,1... | collective-permute-start | bytes 1179656 | tf_op jit(solution)/shard_map/ppermute | solution.py:402
  81.1 13.9 %collective-permute-start.24 = (bf16[48,4096]{1,0:T(8,128)(2,1)S(1)}, bf16[48,4096]{1,0:T(8,128)(2,1)S(1)}, u32[]{:S(2)}, u32[]{:S(2)}) collective-permute-start(bf16[48,4096]{1,0:T(8,128)(2,1)S(1)} %expert.16), channel_id=1, source_target_pairs={{0,1},{1,2},{2,3},{3,19},{19,18},{18,17},{17,16},{16,0},{8,9},{9,1... | collective-permute-start | bytes 1179656 | tf_op jit(solution)/shard_map/ppermute | solution.py:402
  85.6 17.7 %collective-permute-start.17 = (bf16[48,4096]{1,0:T(8,128)(2,1)S(1)}, bf16[48,4096]{1,0:T(8,128)(2,1)S(1)}, u32[]{:S(2)}, u32[]{:S(2)}) collective-permute-start(bf16[48,4096]{1,0:T(8,128)(2,1)S(1)} %get-tuple-element.142), channel_id=1, source_target_pairs={{0,16},{1,0},{2,1},{3,2},{19,3},{18,19},{17,18},{16,17},{8,24},{9,... | collective-permute-start | bytes 1179656 | tf_op jit(solution)/shard_map/ppermute | solution.py:402
  87.1 16.3 %collective-permute-start.18 = (bf16[48,4096]{1,0:T(8,128)(2,1)S(1)}, bf16[48,4096]{1,0:T(8,128)(2,1)S(1)}, u32[]{:S(2)}, u32[]{:S(2)}) collective-permute-start(bf16[48,4096]{1,0:T(8,128)(2,1)S(1)} %get-tuple-element.143), channel_id=1, source_target_pairs={{0,1},{1,2},{2,3},{3,19},{19,18},{18,17},{17,16},{16,0},{8,9},{9,1... | collective-permute-start | bytes 1179656 | tf_op jit(solution)/shard_map/ppermute | solution.py:402
  95.2 16.7 %collective-permute-start.27 = (bf16[48,4096]{1,0:T(8,128)(2,1)S(1)}, bf16[48,4096]{1,0:T(8,128)(2,1)S(1)}, u32[]{:S(2)}, u32[]{:S(2)}) collective-permute-start(bf16[48,4096]{1,0:T(8,128)(2,1)S(1)} %get-tuple-element.166), channel_id=1, source_target_pairs={{0,1},{1,2},{2,3},{3,19},{19,18},{18,17},{17,16},{16,0},{8,9},{9,1... | collective-permute-start | bytes 1179656 | tf_op jit(solution)/shard_map/ppermute | solution.py:402
  96.5 15.3 %collective-permute-start.28 = (bf16[48,4096]{1,0:T(8,128)(2,1)S(1)}, bf16[48,4096]{1,0:T(8,128)(2,1)S(1)}, u32[]{:S(2)}, u32[]{:S(2)}) collective-permute-start(bf16[48,4096]{1,0:T(8,128)(2,1)S(1)} %get-tuple-element.167), channel_id=1, source_target_pairs={{0,16},{1,0},{2,1},{3,2},{19,3},{18,19},{17,18},{16,17},{8,24},{9,... | collective-permute-start | bytes 1179656 | tf_op jit(solution)/shard_map/ppermute | solution.py:402
  103.6 16.5 %collective-permute-start.19 = (bf16[48,4096]{1,0:T(8,128)(2,1)S(1)}, bf16[48,4096]{1,0:T(8,128)(2,1)S(1)}, u32[]{:S(2)}, u32[]{:S(2)}) collective-permute-start(bf16[48,4096]{1,0:T(8,128)(2,1)S(1)} %get-tuple-element.146), channel_id=1, source_target_pairs={{0,16},{1,0},{2,1},{3,2},{19,3},{18,19},{17,18},{16,17},{8,24},{9,... | collective-permute-start | bytes 1179656 | tf_op jit(solution)/shard_map/ppermute | solution.py:402
  104.9 15.4 %collective-permute-start.20 = (bf16[48,4096]{1,0:T(8,128)(2,1)S(1)}, bf16[48,4096]{1,0:T(8,128)(2,1)S(1)}, u32[]{:S(2)}, u32[]{:S(2)}) collective-permute-start(bf16[48,4096]{1,0:T(8,128)(2,1)S(1)} %get-tuple-element.147), channel_id=1, source_target_pairs={{0,1},{1,2},{2,3},{3,19},{19,18},{18,17},{17,16},{16,0},{8,9},{9,1... | collective-permute-start | bytes 1179656 | tf_op jit(solution)/shard_map/ppermute | solution.py:402
  112.0 16.5 %collective-permute-start.33 = (bf16[48,4096]{1,0:T(8,128)(2,1)S(1)}, bf16[48,4096]{1,0:T(8,128)(2,1)S(1)}, u32[]{:S(2)}, u32[]{:S(2)}) collective-permute-start(bf16[48,4096]{1,0:T(8,128)(2,1)S(1)} %get-tuple-element.174), channel_id=1, source_target_pairs={{0,16},{1,0},{2,1},{3,2},{19,3},{18,19},{17,18},{16,17},{8,24},{9,... | collective-permute-start | bytes 1179656 | tf_op jit(solution)/shard_map/ppermute | solution.py:402
  113.3 16.8 %collective-permute-start.29 = (bf16[48,4096]{1,0:T(8,128)(2,1)S(1)}, bf16[48,4096]{1,0:T(8,128)(2,1)S(1)}, u32[]{:S(2)}, u32[]{:S(2)}) collective-permute-start(bf16[48,4096]{1,0:T(8,128)(2,1)S(1)} %get-tuple-element.168), channel_id=1, source_target_pairs={{0,1},{1,2},{2,3},{3,19},{19,18},{18,17},{17,16},{16,0},{8,9},{9,1... | collective-permute-start | bytes 1179656 | tf_op jit(solution)/shard_map/ppermute | solution.py:402
  120.5 16.7 %collective-permute-start.32 = (bf16[48,4096]{1,0:T(8,128)(2,1)S(1)}, bf16[48,4096]{1,0:T(8,128)(2,1)S(1)}, u32[]{:S(2)}, u32[]{:S(2)}) collective-permute-start(bf16[48,4096]{1,0:T(8,128)(2,1)S(1)} %get-tuple-element.172), channel_id=1, source_target_pairs={{0,1},{1,2},{2,3},{3,19},{19,18},{18,17},{17,16},{16,0},{8,9},{9,1... | collective-permute-start | bytes 1179656 | tf_op jit(solution)/shard_map/ppermute | solution.py:402
  128.8 18.7 %collective-permute-start.21 = (bf16[48,4096]{1,0:T(8,128)(2,1)S(1)}, bf16[48,4096]{1,0:T(8,128)(2,1)S(1)}, u32[]{:S(2)}, u32[]{:S(2)}) collective-permute-start(bf16[48,4096]{1,0:T(8,128)(2,1)S(1)} %get-tuple-element.157), channel_id=1, source_target_pairs={{0,16},{1,0},{2,1},{3,2},{19,3},{18,19},{17,18},{16,17},{8,24},{9,... | collective-permute-start | bytes 1179656 | tf_op jit(solution)/shard_map/ppermute | solution.py:402
  130.2 17.4 %collective-permute-start.30 = (bf16[48,4096]{1,0:T(8,128)(2,1)S(1)}, bf16[48,4096]{1,0:T(8,128)(2,1)S(1)}, u32[]{:S(2)}, u32[]{:S(2)}) collective-permute-start(bf16[48,4096]{1,0:T(8,128)(2,1)S(1)} %finish_sums.4), channel_id=1, source_target_pairs={{0,1},{1,2},{2,3},{3,19},{19,18},{18,17},{17,16},{16,0},{8,9},{9,1... | collective-permute-start | bytes 1179656 | tf_op jit(solution)/shard_map/ppermute | solution.py:402
  138.3 16.7 %collective-permute-start.36 = (bf16[24,4096]{1,0:T(8,128)(2,1)S(1)}, bf16[24,4096]{1,0:T(8,128)(2,1)S(1)}, u32[]{:S(2)}, u32[]{:S(2)}) collective-permute-start(bf16[24,4096]{1,0:T(8,128)(2,1)S(1)} %get-tuple-element.176), channel_id=1, source_target_pairs={{12,0},{8,4},{4,8},{0,12},{28,16},{24,20},{20,24},{16,28},{13,1},{... | collective-permute-start | bytes 589832 | tf_op jit(solution)/shard_map/ppermute | solution.py:466
  (24 other events, 205.4 us)

commit v4 on v3

--- a/solution.py
+++ b/solution.py
@@ -16,6 +16,7 @@
 CORES = 2
 VMEM_LIMIT = 16 * 1024 * 1024
 EXPERT_VMEM = 8 * 1024 * 1024
+WIDE_VMEM = 56 * 1024 * 1024
 SPAN = 1024
 
 
@@ -156,16 +157,16 @@
         copy.wait()
 
 
-def staged(kernel, core, arrays, outs, copies, name):
-    vmem = pl.BlockSpec(memory_space=pltpu.VMEM)
+def staged(kernel, core, arrays, outs, copies, name, limit=EXPERT_VMEM, space=pltpu.VMEM):
+    target = pl.BlockSpec(memory_space=space)
     return pl.pallas_call(
         kernel,
         out_shape=outs,
         in_specs=[pl.BlockSpec(memory_space=pltpu.SMEM)]
         + [pl.BlockSpec(memory_space=pl.ANY)] * len(arrays),
-        out_specs=[vmem] * len(outs),
+        out_specs=[target] * len(outs),
         scratch_shapes=[pltpu.SemaphoreType.DMA((copies,))],
-        compiler_params=pltpu.CompilerParams(vmem_limit_bytes=EXPERT_VMEM),
+        compiler_params=pltpu.CompilerParams(vmem_limit_bytes=limit),
         cost_estimate=pl.CostEstimate(
             flops=0, bytes_accessed=sum(2 * x.size * 2 for x in outs), transcendentals=0
         ),
@@ -327,7 +328,13 @@
     core_at = core.astype(jnp.int32)[None]
     share = w_in.shape[1]
     pair_units = staged(
-        pick_kernel, core_at, [w_in, w_out], [rows_like(share)] * 2, 2, "pick_units"
+        pick_kernel,
+        core_at,
+        [w_in, w_out],
+        [rows_like(share)] * 2,
+        2,
+        "pick_units",
+        limit=WIDE_VMEM,
     )
     rel, pair_units = lax.optimization_barrier((rel, pair_units))
     pair_units = [lax.ppermute(rows, "section", core_pairs()) for rows in pair_units]

time: 157 us -> 157 us (level)
  local copies, waits for them, and re-layouts: 8.71 us -> 3.74 us
  waiting for transfers between devices: 66.2 us -> 68.9 us
  Pallas kernels: 38.4 us -> 40.6 us
    unnamed x22 -> x18, local copies, waits for them, and re-layouts: 8.61 us -> 3.64 us
    ppermute x1, waiting for transfers between devices: 3.11 us -> 5.85 us  [body(): lax.ppermute(block, ('section', 'seq'), route(lambda b: 1 - b))]
    pallas_call x3, Pallas kernels: 5.13 us -> 7.37 us  [staged(): pl.pallas_call(kernel, out_shape=outs, in_specs=[pl.BlockSpec(memory_spac...]
  transfers between devices with their start and end apart: 37 -> 37, of which waited for: 20 -> 20; matrix products, arithmetic and copies ran while one was open for 1% -> 1% of each run, Pallas kernels for 24% -> 25%
where the time goes in v4:
time: 157 us; the launch traced here: 156 us
  waiting for transfers between devices  68.9 us (44%)
  Pallas kernels  40.6 us (26%)
  starting transfers between devices  40.5 us (26%)
  local copies, waits for them, and re-layouts  3.74 us (2%)
    ppermute x28, waiting for transfers between devices, hop(): return lax.ppermute(rows, ('section', 'expert'), pairs)  52.9 us
    pallas_call x9, Pallas kernels, expert_sums(): pl.pallas_call(functools.partial(expert_kernel, len(parts)), out_shape=[j...  27.5 us
    ppermute x28, starting transfers between devices, hop(): return lax.ppermute(rows, ('section', 'expert'), pairs)  22.2 us
    ppermute x3, starting transfers between devices, cross(): return lax.ppermute(rows, ('section', 'seq'), pairs)  12.7 us
    pallas_call x3, Pallas kernels, staged(): pl.pallas_call(kernel, out_shape=outs, in_specs=[pl.BlockSpec(memory_spac...  7.37 us
    ppermute x1, waiting for transfers between devices, body(): lax.ppermute(block, ('section', 'seq'), route(lambda b: 1 - b))  5.85 us
    ppermute x3, waiting for transfers between devices, cross(): return lax.ppermute(rows, ('section', 'seq'), pairs)  4.8 us
    ppermute x1, waiting for transfers between devices, seq_move(): lax.ppermute(rows, 'seq', [(b, (b + step) % seqs) for b in range(seqs)])  3.98 us
  transfers between devices with their start and end apart: 37, of which 20 were waited for; matrix products, arithmetic and copies ran while one was open for 1% of the time, Pallas kernels for 25%

profile of v4, /device:TPU:1, one launch (start us, length us, event | category | flops | bytes accessed | tf_op | source)
XLA Modules:
  0.0 156.3 jit_solution(7931114699669963021)
XLA Ops:
  0.0 3.6 %collective-permute-start = (bf16[2,160,1024]{2,1,0:T(8,128)(2,1)}, bf16[2,160,1024]{2,1,0:T(8,128)(2,1)}, u32[]{:S(2)}, u32[]{:S(2)}) collective-permute-start(bf16[2,160,1024]{2,1,0:T(8,128)(2,1)} %bitcast.81), channel_id=1, source_target_pairs={{28,0},{24,4},{4,8},{0,12},{12,16},{8,20},{20,24},{16,28},{29,1},{... | collective-permute-start | bytes 1966088 | tf_op jit(solution)/shard_map/ppermute | solution.py:310
  4.3 5.0 %pick_units.1 = (bf16[320,4096]{1,0:T(8,128)(2,1)}, bf16[320,4096]{1,0:T(8,128)(2,1)}) custom-call(s32[1]{0:T(128)} %bitcast.core_ref, bf16[2,320,4096]{2,1,0:T(8,128)(2,1)} %in_ref.3, bf16[2,320,4096]{2,1,0:T(8,128)(2,1)} %out_w_ref.3), custom_call_target="tpu_custom_call" | custom-call | bytes 10485760 | tf_op jit(solution)/shard_map/pick_units/pallas_call | solution.py:162
  12.7 5.8 %collective-permute-done.refs_0_ = bf16[2,160,1024]{2,1,0:T(8,128)(2,1)} collective-permute-done((bf16[2,160,1024]{2,1,0:T(8,128)(2,1)}, bf16[2,160,1024]{2,1,0:T(8,128)(2,1)}, u32[]{:S(2)}, u32[]{:S(2)}) %collective-permute-start) | collective-permute-done | bytes 655392 | tf_op jit(solution)/shard_map/ppermute | solution.py:310
  18.5 3.2 %attend.1 = (f32[96,4096]{1,0:T(8,128)S(1)}, bf16[48,4096]{1,0:T(8,128)(2,1)S(1)}, bf16[24,4096]{1,0:T(8,128)(2,1)S(1)}, bf16[24,4096]{1,0:T(8,128)(2,1)S(1)}) custom-call(s32[2]{0:T(128)S(1)} %pad_add_fusion.rel_ref, bf16[96,4096]{1,0:T(8,128)(2,1)S(1)} %get-tuple-element.96.q_ref, bf16[96,4096]{1,0:T(8,128)(2,1)S(1)} %get-tuple-element.97.res_ref, ...), custom_call_target="tpu_custom_call" | custom-call | flops 301989888 | bytes 6000000 | tf_op jit(solution)/shard_map/attend/pallas_call | solution.py:73
  31.0 4.0 %collective-permute-done.3.refs_1_ = bf16[48,4096]{1,0:T(8,128)(2,1)S(1)} collective-permute-done((bf16[48,4096]{1,0:T(8,128)(2,1)S(1)}, bf16[48,4096]{1,0:T(8,128)(2,1)S(1)}, u32[]{:S(2)}, u32[]{:S(2)}) %collective-permute-start.3) | collective-permute-done | bytes 393248 | tf_op jit(solution)/shard_map/ppermute | solution.py:385
  37.9 3.1 %expert.9 = (bf16[48,4096]{1,0:T(8,128)(2,1)S(1)}, bf16[48,4096]{1,0:T(8,128)(2,1)S(1)}) custom-call(bf16[48,4096]{1,0:T(8,128)(2,1)S(1)} %collective-permute-done.8.refs_0_, bf16[48,4096]{1,0:T(8,128)(2,1)S(1)} %collective-permute-done.9.refs_1_, bf16[640,4096]{1,0:T(8,128)(2,1)S(1)} %get-tuple-element.120.refs_2_.refs_1_, ...), custom_call_target="tpu_custom_call" | custom-call | flops 1 | bytes 1 | tf_op jit(solution)/shard_map/expert/pallas_call | solution.py:181
  41.0 3.4 %collective-permute-done.6.refs_0_ = bf16[48,4096]{1,0:T(8,128)(2,1)S(1)} collective-permute-done((bf16[48,4096]{1,0:T(8,128)(2,1)S(1)}, bf16[48,4096]{1,0:T(8,128)(2,1)S(1)}, u32[]{:S(2)}, u32[]{:S(2)}) %collective-permute-start.6) | collective-permute-done | bytes 393248 | tf_op jit(solution)/shard_map/ppermute | solution.py:409
  46.9 5.9 %collective-permute-done.12.refs_0_ = bf16[48,4096]{1,0:T(8,128)(2,1)S(1)} collective-permute-done((bf16[48,4096]{1,0:T(8,128)(2,1)S(1)}, bf16[48,4096]{1,0:T(8,128)(2,1)S(1)}, u32[]{:S(2)}, u32[]{:S(2)}) %collective-permute-start.12) | collective-permute-done | bytes 393248 | tf_op jit(solution)/shard_map/ppermute | solution.py:409
  55.1 3.1 %expert.10 = (bf16[48,4096]{1,0:T(8,128)(2,1)S(1)}, bf16[48,4096]{1,0:T(8,128)(2,1)S(1)}) custom-call(bf16[48,4096]{1,0:T(8,128)(2,1)S(1)} %collective-permute-done.12.refs_0_, bf16[48,4096]{1,0:T(8,128)(2,1)S(1)} %collective-permute-done.13.refs_1_, bf16[640,4096]{1,0:T(8,128)(2,1)S(1)} %get-tuple-element.120.refs_2_.refs_1_, ...), custom_call_target="tpu_custom_call" | custom-call | flops 1 | bytes 1 | tf_op jit(solution)/shard_map/expert/pallas_call | solution.py:181
  58.2 3.1 %expert.12 = (bf16[48,4096]{1,0:T(8,128)(2,1)S(1)}, bf16[48,4096]{1,0:T(8,128)(2,1)S(1)}) custom-call(bf16[48,4096]{1,0:T(8,128)(2,1)S(1)} %collective-permute-done.6.refs_0_, bf16[48,4096]{1,0:T(8,128)(2,1)S(1)} %collective-permute-done.7.refs_1_, bf16[640,4096]{1,0:T(8,128)(2,1)S(1)} %get-tuple-element.120.refs_2_.refs_1_, ...), custom_call_target="tpu_custom_call" | custom-call | flops 1 | bytes 1 | tf_op jit(solution)/shard_map/expert/pallas_call | solution.py:181
  62.4 7.2 %collective-permute-done.14.refs_0_ = bf16[48,4096]{1,0:T(8,128)(2,1)S(1)} collective-permute-done((bf16[48,4096]{1,0:T(8,128)(2,1)S(1)}, bf16[48,4096]{1,0:T(8,128)(2,1)S(1)}, u32[]{:S(2)}, u32[]{:S(2)}) %collective-permute-start.14) | collective-permute-done | bytes 393248 | tf_op jit(solution)/shard_map/ppermute | solution.py:409
  72.6 3.1 %expert.13 = (bf16[48,4096]{1,0:T(8,128)(2,1)S(1)}, bf16[48,4096]{1,0:T(8,128)(2,1)S(1)}) custom-call(bf16[48,4096]{1,0:T(8,128)(2,1)S(1)} %collective-permute-done.14.refs_0_, bf16[48,4096]{1,0:T(8,128)(2,1)S(1)} %collective-permute-done.16.refs_1_, bf16[640,4096]{1,0:T(8,128)(2,1)S(1)} %get-tuple-element.120.refs_2_.refs_1_, ...), custom_call_target="tpu_custom_call" | custom-call | flops 1 | bytes 1 | tf_op jit(solution)/shard_map/expert/pallas_call | solution.py:181
  82.4 2.9 %expert.17 = bf16[48,4096]{1,0:T(8,128)(2,1)S(1)} custom-call(bf16[48,4096]{1,0:T(8,128)(2,1)S(1)} %collective-permute-done.25.refs_0_, bf16[640,4096]{1,0:T(8,128)(2,1)S(1)} %get-tuple-element.120.refs_2_.refs_1_, bf16[640,4096]{1,0:T(8,128)(2,1)S(1)} %get-tuple-element.121.refs_3_.refs_2_), custom_call_target="tpu_custom_call" | custom-call | flops 1 | bytes 1 | tf_op jit(solution)/shard_map/expert/pallas_call | solution.py:181
  88.4 3.1 %expert.15 = (bf16[48,4096]{1,0:T(8,128)(2,1)S(1)}, bf16[48,4096]{1,0:T(8,128)(2,1)S(1)}) custom-call(bf16[48,4096]{1,0:T(8,128)(2,1)S(1)} %collective-permute-done.22.refs_0_, bf16[48,4096]{1,0:T(8,128)(2,1)S(1)} %collective-permute-done.23.refs_1_, bf16[640,4096]{1,0:T(8,128)(2,1)S(1)} %get-tuple-element.120.refs_2_.refs_1_, ...), custom_call_target="tpu_custom_call" | custom-call | flops 1 | bytes 1 | tf_op jit(solution)/shard_map/expert/pallas_call | solution.py:181
  91.5 3.5 %collective-permute-done.24.refs_2_ = bf16[48,4096]{1,0:T(8,128)(2,1)S(1)} collective-permute-done((bf16[48,4096]{1,0:T(8,128)(2,1)S(1)}, bf16[48,4096]{1,0:T(8,128)(2,1)S(1)}, u32[]{:S(2)}, u32[]{:S(2)}) %collective-permute-start.24) | collective-permute-done | bytes 393248 | tf_op jit(solution)/shard_map/ppermute | solution.py:409
  96.7 3.1 %expert.11 = (bf16[48,4096]{1,0:T(8,128)(2,1)S(1)}, bf16[48,4096]{1,0:T(8,128)(2,1)S(1)}) custom-call(bf16[48,4096]{1,0:T(8,128)(2,1)S(1)} %collective-permute-done.10.refs_0_, bf16[48,4096]{1,0:T(8,128)(2,1)S(1)} %collective-permute-done.11.refs_1_, bf16[640,4096]{1,0:T(8,128)(2,1)S(1)} %get-tuple-element.120.refs_2_.refs_1_, ...), custom_call_target="tpu_custom_call" | custom-call | flops 1 | bytes 1 | tf_op jit(solution)/shard_map/expert/pallas_call | solution.py:181
  99.8 3.5 %collective-permute-done.17.refs_2_ = bf16[48,4096]{1,0:T(8,128)(2,1)S(1)} collective-permute-done((bf16[48,4096]{1,0:T(8,128)(2,1)S(1)}, bf16[48,4096]{1,0:T(8,128)(2,1)S(1)}, u32[]{:S(2)}, u32[]{:S(2)}) %collective-permute-start.17) | collective-permute-done | bytes 393248 | tf_op jit(solution)/shard_map/ppermute | solution.py:409
  105.1 6.7 %collective-permute-done.27.refs_2_ = bf16[48,4096]{1,0:T(8,128)(2,1)S(1)} collective-permute-done((bf16[48,4096]{1,0:T(8,128)(2,1)S(1)}, bf16[48,4096]{1,0:T(8,128)(2,1)S(1)}, u32[]{:S(2)}, u32[]{:S(2)}) %collective-permute-start.27) | collective-permute-done | bytes 393248 | tf_op jit(solution)/shard_map/ppermute | solution.py:409
  113.7 3.1 %expert.14 = (bf16[48,4096]{1,0:T(8,128)(2,1)S(1)}, bf16[48,4096]{1,0:T(8,128)(2,1)S(1)}) custom-call(bf16[48,4096]{1,0:T(8,128)(2,1)S(1)} %get-tuple-element.148.refs_0_, bf16[48,4096]{1,0:T(8,128)(2,1)S(1)} %collective-permute-done.3.refs_1_, bf16[640,4096]{1,0:T(8,128)(2,1)S(1)} %get-tuple-element.120.refs_2_.refs_1_, ...), custom_call_target="tpu_custom_call" | custom-call | flops 1 | bytes 1 | tf_op jit(solution)/shard_map/expert/pallas_call | solution.py:181
  116.8 3.3 %collective-permute-done.19.refs_2_ = bf16[48,4096]{1,0:T(8,128)(2,1)S(1)} collective-permute-done((bf16[48,4096]{1,0:T(8,128)(2,1)S(1)}, bf16[48,4096]{1,0:T(8,128)(2,1)S(1)}, u32[]{:S(2)}, u32[]{:S(2)}) %collective-permute-start.19) | collective-permute-done | bytes 393248 | tf_op jit(solution)/shard_map/ppermute | solution.py:409
  121.8 6.7 %collective-permute-done.33.refs_1_ = bf16[48,4096]{1,0:T(8,128)(2,1)S(1)} collective-permute-done((bf16[48,4096]{1,0:T(8,128)(2,1)S(1)}, bf16[48,4096]{1,0:T(8,128)(2,1)S(1)}, u32[]{:S(2)}, u32[]{:S(2)}) %collective-permute-start.33) | collective-permute-done | bytes 393248 | tf_op jit(solution)/shard_map/ppermute | solution.py:409
  130.5 6.7 %collective-permute-done.32.refs_1_ = bf16[48,4096]{1,0:T(8,128)(2,1)S(1)} collective-permute-done((bf16[48,4096]{1,0:T(8,128)(2,1)S(1)}, bf16[48,4096]{1,0:T(8,128)(2,1)S(1)}, u32[]{:S(2)}, u32[]{:S(2)}) %collective-permute-start.32) | collective-permute-done | bytes 393248 | tf_op jit(solution)/shard_map/ppermute | solution.py:409
  138.3 9.2 %collective-permute-start.36 = (bf16[24,4096]{1,0:T(8,128)(2,1)S(1)}, bf16[24,4096]{1,0:T(8,128)(2,1)S(1)}, u32[]{:S(2)}, u32[]{:S(2)}) collective-permute-start(bf16[24,4096]{1,0:T(8,128)(2,1)S(1)} %get-tuple-element.176), channel_id=1, source_target_pairs={{12,0},{8,4},{4,8},{0,12},{28,16},{24,20},{20,24},{16,28},{13,1},{... | collective-permute-start | bytes 589832 | tf_op jit(solution)/shard_map/ppermute | solution.py:473
  150.2 4.8 %collective-permute-done.36.refs_3_ = bf16[24,4096]{1,0:T(8,128)(2,1)S(1)} collective-permute-done((bf16[24,4096]{1,0:T(8,128)(2,1)S(1)}, bf16[24,4096]{1,0:T(8,128)(2,1)S(1)}, u32[]{:S(2)}, u32[]{:S(2)}) %collective-permute-start.36) | collective-permute-done | bytes 196640 | tf_op jit(solution)/shard_map/ppermute | solution.py:473
  (105 shorter events, 48.2 us)
Async XLA Ops:
  0.0 18.5 %collective-permute-start = (bf16[2,160,1024]{2,1,0:T(8,128)(2,1)}, bf16[2,160,1024]{2,1,0:T(8,128)(2,1)}, u32[]{:S(2)}, u32[]{:S(2)}) collective-permute-start(bf16[2,160,1024]{2,1,0:T(8,128)(2,1)} %bitcast.81), channel_id=1, source_target_pairs={{28,0},{24,4},{4,8},{0,12},{12,16},{8,20},{20,24},{16,28},{29,1},{... | collective-permute-start | bytes 1966088 | tf_op jit(solution)/shard_map/ppermute | solution.py:310
  3.6 15.0 %collective-permute-start.1 = (bf16[2,160,1024]{2,1,0:T(8,128)(2,1)}, bf16[2,160,1024]{2,1,0:T(8,128)(2,1)}, u32[]{:S(2)}, u32[]{:S(2)}) collective-permute-start(bf16[2,160,1024]{2,1,0:T(8,128)(2,1)} %bitcast.82), channel_id=1, source_target_pairs={{24,0},{28,4},{0,8},{4,12},{8,16},{12,20},{16,24},{20,28},{25,1},{... | collective-permute-start | bytes 1966088 | tf_op jit(solution)/shard_map/ppermute | solution.py:311
  9.3 16.9 %collective-permute-start.4 = (bf16[320,4096]{1,0:T(8,128)(2,1)}, bf16[320,4096]{1,0:T(8,128)(2,1)S(1)}, u32[]{:S(2)}, u32[]{:S(2)}) collective-permute-start(bf16[320,4096]{1,0:T(8,128)(2,1)} %get-tuple-element.108), channel_id=1, source_target_pairs={{0,8},{8,0},{16,24},{24,16},{1,9},{9,1},{17,25},{25,17},{2,10},{10... | collective-permute-start | bytes 7864328 | tf_op jit(solution)/shard_map/ppermute | solution.py:340
  9.8 16.3 %collective-permute-start.5 = (bf16[320,4096]{1,0:T(8,128)(2,1)}, bf16[320,4096]{1,0:T(8,128)(2,1)}, u32[]{:S(2)}, u32[]{:S(2)}) collective-permute-start(bf16[320,4096]{1,0:T(8,128)(2,1)} %get-tuple-element.109), channel_id=1, source_target_pairs={{0,8},{8,0},{16,24},{24,16},{1,9},{9,1},{17,25},{25,17},{2,10},{10... | collective-permute-start | bytes 7864328 | tf_op jit(solution)/shard_map/ppermute | solution.py:340
  36.4 16.4 %collective-permute-start.12 = (bf16[48,4096]{1,0:T(8,128)(2,1)S(1)}, bf16[48,4096]{1,0:T(8,128)(2,1)S(1)}, u32[]{:S(2)}, u32[]{:S(2)}) collective-permute-start(bf16[48,4096]{1,0:T(8,128)(2,1)S(1)} %collective-permute-done.8.refs_0_), channel_id=1, source_target_pairs={{0,1},{1,2},{2,3},{3,19},{19,18},{18,17},{17,16},{16,0},{8,9},{9,1... | collective-permute-start | bytes 1179656 | tf_op jit(solution)/shard_map/ppermute | solution.py:409
  37.7 16.1 %collective-permute-start.13 = (bf16[48,4096]{1,0:T(8,128)(2,1)S(1)}, bf16[48,4096]{1,0:T(8,128)(2,1)S(1)}, u32[]{:S(2)}, u32[]{:S(2)}) collective-permute-start(bf16[48,4096]{1,0:T(8,128)(2,1)S(1)} %collective-permute-done.9.refs_1_), channel_id=1, source_target_pairs={{0,16},{1,0},{2,1},{3,2},{19,3},{18,19},{17,18},{16,17},{8,24},{9,... | collective-permute-start | bytes 1179656 | tf_op jit(solution)/shard_map/ppermute | solution.py:409
  45.4 15.9 %collective-permute-start.10 = (bf16[48,4096]{1,0:T(8,128)(2,1)S(1)}, bf16[48,4096]{1,0:T(8,128)(2,1)S(1)}, u32[]{:S(2)}, u32[]{:S(2)}) collective-permute-start(bf16[48,4096]{1,0:T(8,128)(2,1)S(1)} %collective-permute-done.6.refs_0_), channel_id=1, source_target_pairs={{0,1},{1,2},{2,3},{3,19},{19,18},{18,17},{17,16},{16,0},{8,9},{9,1... | collective-permute-start | bytes 1179656 | tf_op jit(solution)/shard_map/ppermute | solution.py:409
  46.7 15.6 %collective-permute-start.11 = (bf16[48,4096]{1,0:T(8,128)(2,1)S(1)}, bf16[48,4096]{1,0:T(8,128)(2,1)S(1)}, u32[]{:S(2)}, u32[]{:S(2)}) collective-permute-start(bf16[48,4096]{1,0:T(8,128)(2,1)S(1)} %collective-permute-done.7.refs_1_), channel_id=1, source_target_pairs={{0,16},{1,0},{2,1},{3,2},{19,3},{18,19},{17,18},{16,17},{8,24},{9,... | collective-permute-start | bytes 1179656 | tf_op jit(solution)/shard_map/ppermute | solution.py:409
  53.8 15.8 %collective-permute-start.14 = (bf16[48,4096]{1,0:T(8,128)(2,1)S(1)}, bf16[48,4096]{1,0:T(8,128)(2,1)S(1)}, u32[]{:S(2)}, u32[]{:S(2)}) collective-permute-start(bf16[48,4096]{1,0:T(8,128)(2,1)S(1)} %collective-permute-done.12.refs_0_), channel_id=1, source_target_pairs={{0,1},{1,2},{2,3},{3,19},{19,18},{18,17},{17,16},{16,0},{8,9},{9,1... | collective-permute-start | bytes 1179656 | tf_op jit(solution)/shard_map/ppermute | solution.py:409
  71.1 16.0 %collective-permute-start.22 = (bf16[48,4096]{1,0:T(8,128)(2,1)S(1)}, bf16[48,4096]{1,0:T(8,128)(2,1)S(1)}, u32[]{:S(2)}, u32[]{:S(2)}) collective-permute-start(bf16[48,4096]{1,0:T(8,128)(2,1)S(1)} %collective-permute-done.13.refs_1_), channel_id=1, source_target_pairs={{0,16},{1,0},{2,1},{3,2},{19,3},{18,19},{17,18},{16,17},{8,24},{9,... | collective-permute-start | bytes 1179656 | tf_op jit(solution)/shard_map/ppermute | solution.py:409
  72.3 16.1 %collective-permute-start.23 = (bf16[48,4096]{1,0:T(8,128)(2,1)S(1)}, bf16[48,4096]{1,0:T(8,128)(2,1)S(1)}, u32[]{:S(2)}, u32[]{:S(2)}) collective-permute-start(bf16[48,4096]{1,0:T(8,128)(2,1)S(1)} %collective-permute-done.10.refs_0_), channel_id=1, source_target_pairs={{0,1},{1,2},{2,3},{3,19},{19,18},{18,17},{17,16},{16,0},{8,9},{9,1... | collective-permute-start | bytes 1179656 | tf_op jit(solution)/shard_map/ppermute | solution.py:409
  81.1 13.9 %collective-permute-start.24 = (bf16[48,4096]{1,0:T(8,128)(2,1)S(1)}, bf16[48,4096]{1,0:T(8,128)(2,1)S(1)}, u32[]{:S(2)}, u32[]{:S(2)}) collective-permute-start(bf16[48,4096]{1,0:T(8,128)(2,1)S(1)} %expert.16), channel_id=1, source_target_pairs={{0,1},{1,2},{2,3},{3,19},{19,18},{18,17},{17,16},{16,0},{8,9},{9,1... | collective-permute-start | bytes 1179656 | tf_op jit(solution)/shard_map/ppermute | solution.py:409
  85.6 17.7 %collective-permute-start.17 = (bf16[48,4096]{1,0:T(8,128)(2,1)S(1)}, bf16[48,4096]{1,0:T(8,128)(2,1)S(1)}, u32[]{:S(2)}, u32[]{:S(2)}) collective-permute-start(bf16[48,4096]{1,0:T(8,128)(2,1)S(1)} %get-tuple-element.142), channel_id=1, source_target_pairs={{0,16},{1,0},{2,1},{3,2},{19,3},{18,19},{17,18},{16,17},{8,24},{9,... | collective-permute-start | bytes 1179656 | tf_op jit(solution)/shard_map/ppermute | solution.py:409
  87.1 16.3 %collective-permute-start.18 = (bf16[48,4096]{1,0:T(8,128)(2,1)S(1)}, bf16[48,4096]{1,0:T(8,128)(2,1)S(1)}, u32[]{:S(2)}, u32[]{:S(2)}) collective-permute-start(bf16[48,4096]{1,0:T(8,128)(2,1)S(1)} %get-tuple-element.143), channel_id=1, source_target_pairs={{0,1},{1,2},{2,3},{3,19},{19,18},{18,17},{17,16},{16,0},{8,9},{9,1... | collective-permute-start | bytes 1179656 | tf_op jit(solution)/shard_map/ppermute | solution.py:409
  95.2 16.7 %collective-permute-start.27 = (bf16[48,4096]{1,0:T(8,128)(2,1)S(1)}, bf16[48,4096]{1,0:T(8,128)(2,1)S(1)}, u32[]{:S(2)}, u32[]{:S(2)}) collective-permute-start(bf16[48,4096]{1,0:T(8,128)(2,1)S(1)} %get-tuple-element.166), channel_id=1, source_target_pairs={{0,1},{1,2},{2,3},{3,19},{19,18},{18,17},{17,16},{16,0},{8,9},{9,1... | collective-permute-start | bytes 1179656 | tf_op jit(solution)/shard_map/ppermute | solution.py:409
  96.5 15.3 %collective-permute-start.28 = (bf16[48,4096]{1,0:T(8,128)(2,1)S(1)}, bf16[48,4096]{1,0:T(8,128)(2,1)S(1)}, u32[]{:S(2)}, u32[]{:S(2)}) collective-permute-start(bf16[48,4096]{1,0:T(8,128)(2,1)S(1)} %get-tuple-element.167), channel_id=1, source_target_pairs={{0,16},{1,0},{2,1},{3,2},{19,3},{18,19},{17,18},{16,17},{8,24},{9,... | collective-permute-start | bytes 1179656 | tf_op jit(solution)/shard_map/ppermute | solution.py:409
  103.6 16.5 %collective-permute-start.19 = (bf16[48,4096]{1,0:T(8,128)(2,1)S(1)}, bf16[48,4096]{1,0:T(8,128)(2,1)S(1)}, u32[]{:S(2)}, u32[]{:S(2)}) collective-permute-start(bf16[48,4096]{1,0:T(8,128)(2,1)S(1)} %get-tuple-element.146), channel_id=1, source_target_pairs={{0,16},{1,0},{2,1},{3,2},{19,3},{18,19},{17,18},{16,17},{8,24},{9,... | collective-permute-start | bytes 1179656 | tf_op jit(solution)/shard_map/ppermute | solution.py:409
  104.9 15.4 %collective-permute-start.20 = (bf16[48,4096]{1,0:T(8,128)(2,1)S(1)}, bf16[48,4096]{1,0:T(8,128)(2,1)S(1)}, u32[]{:S(2)}, u32[]{:S(2)}) collective-permute-start(bf16[48,4096]{1,0:T(8,128)(2,1)S(1)} %get-tuple-element.147), channel_id=1, source_target_pairs={{0,1},{1,2},{2,3},{3,19},{19,18},{18,17},{17,16},{16,0},{8,9},{9,1... | collective-permute-start | bytes 1179656 | tf_op jit(solution)/shard_map/ppermute | solution.py:409
  112.0 16.5 %collective-permute-start.33 = (bf16[48,4096]{1,0:T(8,128)(2,1)S(1)}, bf16[48,4096]{1,0:T(8,128)(2,1)S(1)}, u32[]{:S(2)}, u32[]{:S(2)}) collective-permute-start(bf16[48,4096]{1,0:T(8,128)(2,1)S(1)} %get-tuple-element.174), channel_id=1, source_target_pairs={{0,16},{1,0},{2,1},{3,2},{19,3},{18,19},{17,18},{16,17},{8,24},{9,... | collective-permute-start | bytes 1179656 | tf_op jit(solution)/shard_map/ppermute | solution.py:409
  113.3 16.8 %collective-permute-start.29 = (bf16[48,4096]{1,0:T(8,128)(2,1)S(1)}, bf16[48,4096]{1,0:T(8,128)(2,1)S(1)}, u32[]{:S(2)}, u32[]{:S(2)}) collective-permute-start(bf16[48,4096]{1,0:T(8,128)(2,1)S(1)} %get-tuple-element.168), channel_id=1, source_target_pairs={{0,1},{1,2},{2,3},{3,19},{19,18},{18,17},{17,16},{16,0},{8,9},{9,1... | collective-permute-start | bytes 1179656 | tf_op jit(solution)/shard_map/ppermute | solution.py:409
  120.5 16.7 %collective-permute-start.32 = (bf16[48,4096]{1,0:T(8,128)(2,1)S(1)}, bf16[48,4096]{1,0:T(8,128)(2,1)S(1)}, u32[]{:S(2)}, u32[]{:S(2)}) collective-permute-start(bf16[48,4096]{1,0:T(8,128)(2,1)S(1)} %get-tuple-element.172), channel_id=1, source_target_pairs={{0,1},{1,2},{2,3},{3,19},{19,18},{18,17},{17,16},{16,0},{8,9},{9,1... | collective-permute-start | bytes 1179656 | tf_op jit(solution)/shard_map/ppermute | solution.py:409
  128.8 18.7 %collective-permute-start.21 = (bf16[48,4096]{1,0:T(8,128)(2,1)S(1)}, bf16[48,4096]{1,0:T(8,128)(2,1)S(1)}, u32[]{:S(2)}, u32[]{:S(2)}) collective-permute-start(bf16[48,4096]{1,0:T(8,128)(2,1)S(1)} %get-tuple-element.157), channel_id=1, source_target_pairs={{0,16},{1,0},{2,1},{3,2},{19,3},{18,19},{17,18},{16,17},{8,24},{9,... | collective-permute-start | bytes 1179656 | tf_op jit(solution)/shard_map/ppermute | solution.py:409
  130.2 17.4 %collective-permute-start.30 = (bf16[48,4096]{1,0:T(8,128)(2,1)S(1)}, bf16[48,4096]{1,0:T(8,128)(2,1)S(1)}, u32[]{:S(2)}, u32[]{:S(2)}) collective-permute-start(bf16[48,4096]{1,0:T(8,128)(2,1)S(1)} %finish_sums.4), channel_id=1, source_target_pairs={{0,1},{1,2},{2,3},{3,19},{19,18},{18,17},{17,16},{16,0},{8,9},{9,1... | collective-permute-start | bytes 1179656 | tf_op jit(solution)/shard_map/ppermute | solution.py:409
  138.3 16.7 %collective-permute-start.36 = (bf16[24,4096]{1,0:T(8,128)(2,1)S(1)}, bf16[24,4096]{1,0:T(8,128)(2,1)S(1)}, u32[]{:S(2)}, u32[]{:S(2)}) collective-permute-start(bf16[24,4096]{1,0:T(8,128)(2,1)S(1)} %get-tuple-element.176), channel_id=1, source_target_pairs={{12,0},{8,4},{4,8},{0,12},{28,16},{24,20},{20,24},{16,28},{13,1},{... | collective-permute-start | bytes 589832 | tf_op jit(solution)/shard_map/ppermute | solution.py:473
  (22 other events, 214.9 us)
